TPU v7x, 32 devices: a whole 2x2x4 slice. The times are simulated.
32 devices in a mesh: rep: 2 (over y), tp: 4 (over z), pd: 2 (over x), st: 2 (over core).
Axes of the slice: x: 2, y: 2, z: 4, core: 2. Of those that a mesh axis runs over, the one named last changes fastest.
Arguments:
- tokens: bfloat16 [4096, 8192], P(('rep', 'pd', 'st'), 'tp'), parts along dimension 0, may hold values from -6 to 6
- key_value_matrix: bfloat16 [8192, 2048], P('tp'), may hold values from -0.09375 to 0.09375
- adapter_down_weight: bfloat16 [128, 8192, 128], P(('rep', 'pd', 'st'), 'tp'), parts along dimension 0, may hold values from -0.0625 to 0.0625
- adapter_up_weight: bfloat16 [128, 64, 2048], P(('rep', 'pd', 'st'), None, 'tp'), parts along dimension 0, may hold values from -0.75 to 0.75
- adapter_store_slot: int32 [128], P('rep'), parts along dimension 0, may hold values from 0 to 63, as said below
- request_adapter: int32 [8, 8], P(('rep', 'pd', 'st')), parts along dimension 0, may hold values from 0 to 63, as said below
- prefill_span_pages: int32 [8, 8], P(('rep', 'pd', 'st')), parts along dimension 0, may hold values from 1 to 16, 32 in all within a row
- decode_pool_slot: int32 [8, 32], P('rep'), parts along dimension 0, may hold values from 0 to 127, as said below
Outputs:
- decode_pool: bfloat16 [256, 16, 2048], P(('rep', 'pd', 'st'), None, 'tp'), parts along dimension 0
There are 2 independent parts, one for each index of `rep`. A program takes and returns all parts, laid end to end along the dimension named above; an argument that names none is the same for every part. Nothing has to cross between parts.
Inputs may be any that keep to these rules, and one draw needn't show every extreme that they name: `adapter_store_slot`: a permutation of the store slots; slot s lies on the store device with index s // 16 of the joined axes pd and st. `request_adapter`: no group asks more than 3 of its requests from one store device, and every group asks exactly 3 from some store device. `prefill_span_pages`: each row sums to 32, its largest entry is 16. `decode_pool_slot`: a permutation of the pool slots; the pages of group g go to pools of groups that differ from g only in their pd index.
All inputs are finite; a program needn't handle non-finite values.
Results may differ from a plain program's by a relative error of at most 0.006.
Values may be sent and summed in bfloat16 or wider, within the bound.
A program may use at most 128 MiB of HBM per device.

v0:
```python
import jax
import jax.numpy as jnp
from jax import lax
from jax.sharding import PartitionSpec as P

PAGE_TOKENS = 16


adapter_scale = 0.5


def adapter_update(
    adapter_portion,
    request_up_weight,
    request_of_page,
    adapter_rank_value,
    token_rows,
    column_range,
):
    half_tensor_parallel = lax.axis_size("tp") // 2
    adapter_whole = lax.psum(adapter_portion.astype(jnp.bfloat16), "tp").astype(jnp.float32)
    halfway_start = jnp.where(lax.axis_index("tp") >= half_tensor_parallel, adapter_rank_value, 0)
    adapter_halfway = lax.dynamic_slice_in_dim(adapter_whole, halfway_start, adapter_rank_value, 2)
    page_up_weight = jnp.take(request_up_weight, request_of_page, axis=0).astype(jnp.float32)
    return jnp.einsum(
        "ueo,uox->uex", adapter_halfway, page_up_weight, precision=lax.Precision.HIGHEST
    ).reshape(token_rows, column_range)


def on_device(
    tokens,
    key_value_matrix,
    adapter_down_weight,
    adapter_up_weight,
    adapter_store_slot,
    request_adapter,
    prefill_span_pages,
    decode_pool_slot,
):
    request_groups = lax.axis_size(("pd", "st"))
    adapter_rank_value = adapter_up_weight.shape[1]
    column_range = adapter_up_weight.shape[2]
    local_width = tokens.shape[1]
    requests = request_adapter.shape[1]
    slot_capacity = requests // request_groups + 1
    holding_count = adapter_down_weight.shape[0]
    token_rows = tokens.shape[0]
    page_count = token_rows // PAGE_TOKENS
    wanted = request_adapter[0]
    store_slot = jnp.take(adapter_store_slot, wanted)
    holder = store_slot // holding_count
    local_index = store_slot % holding_count
    order_ids = jnp.arange(requests)
    earlier = (holder[None, :] == holder[:, None]) & (order_ids[None, :] < order_ids[:, None])
    rank_in = jnp.sum(earlier.astype(jnp.int32), axis=1)
    slot_hits = (holder[:, None, None] == jnp.arange(request_groups)[None, :, None]) & (
        rank_in[:, None, None] == jnp.arange(slot_capacity)[None, None, :]
    )
    asked_pages = jnp.sum(jnp.where(slot_hits, local_index[:, None, None], 0), axis=0)
    incoming = lax.all_to_all(asked_pages, ("pd", "st"), split_axis=0, concat_axis=0, tiled=True)
    flattened_index = incoming.reshape(-1)
    down_page_list = jnp.take(adapter_down_weight, flattened_index, axis=0).reshape(
        request_groups, slot_capacity, local_width, 2 * adapter_rank_value
    )
    up_page_list = jnp.take(adapter_up_weight, flattened_index, axis=0).reshape(
        request_groups, slot_capacity, adapter_rank_value, column_range
    )
    arrived_down, arrived_up = (
        lax.all_to_all(down_page_list, ("pd", "st"), split_axis=0, concat_axis=0, tiled=True),
        lax.all_to_all(up_page_list, ("pd", "st"), split_axis=0, concat_axis=0, tiled=True),
    )
    source_store = holder * slot_capacity + rank_in
    request_down = jnp.take(
        arrived_down.reshape(request_groups * slot_capacity, local_width, 2 * adapter_rank_value),
        source_store,
        axis=0,
    )
    request_up_weight = jnp.take(
        arrived_up.reshape(request_groups * slot_capacity, adapter_rank_value, column_range),
        source_store,
        axis=0,
    )
    page_ends = jnp.cumsum(prefill_span_pages[0])
    request_of_page = jnp.sum(
        (page_ends[None, :] <= jnp.arange(page_count)[:, None]).astype(jnp.int32), axis=1
    )
    page_down = jnp.take(request_down, request_of_page, axis=0)
    token_pages = tokens.reshape(page_count, PAGE_TOKENS, local_width)
    adapter_portion = jnp.einsum(
        "ptd,pdr->ptr", token_pages, page_down, preferred_element_type=jnp.float32
    )
    base_part = jnp.dot(tokens, key_value_matrix, preferred_element_type=jnp.float32)
    summed_key_value = lax.psum_scatter(base_part, "tp", scatter_dimension=1, tiled=True)
    completed_output = summed_key_value + adapter_scale * adapter_update(
        adapter_portion,
        request_up_weight,
        request_of_page,
        adapter_rank_value,
        token_rows,
        column_range,
    )
    key_value_rows = completed_output.astype(jnp.bfloat16).reshape(
        page_count, PAGE_TOKENS * column_range
    )
    arrived = lax.all_gather(key_value_rows, "pd", axis=0, tiled=True)
    pd_count = lax.axis_size("pd")
    st_count = lax.axis_size("st")
    st_index = lax.axis_index("st")
    pd_index = lax.axis_index("pd")
    slot_table = decode_pool_slot.reshape(pd_count, st_count, page_count)
    dest_column = lax.dynamic_index_in_dim(slot_table, st_index, 1, keepdims=False).reshape(-1)
    own_slots = (pd_index * st_count + st_index) * page_count + jnp.arange(page_count)
    selector = (dest_column[None, :] == own_slots[:, None]).astype(jnp.bfloat16)
    decode_pool = jnp.dot(selector, arrived, preferred_element_type=jnp.float32).astype(
        jnp.bfloat16
    )
    return decode_pool.reshape(page_count, PAGE_TOKENS, column_range)


def solution(mesh):
    placed = (
        P(("rep", "pd", "st"), "tp"),
        P("tp", None),
        P(("rep", "pd", "st"), "tp", None),
        P(("rep", "pd", "st"), None, "tp"),
        P("rep"),
        P(("rep", "pd", "st"), None),
        P(("rep", "pd", "st"), None),
        P("rep", None),
    )
    return jax.shard_map(
        on_device,
        mesh=mesh,
        in_specs=placed,
        out_specs=P(("rep", "pd", "st"), None, "tp"),
        check_vma=False,
    )
```

profile of v0, /device:TPU:0, one launch (start us, length us, event | category | flops | bytes accessed | tf_op | source)
XLA Modules:
  0.0 284.8 jit_solution(17407005473618985999)
XLA Ops:
  7.4 1.3 gather_fusion
  10.5 7.8 %all_to_all.19 = s32[4,1,3]{2,1,0:T(1,128)S(1)} all-to-all(s32[4,1,3]{2,1,0:T(1,128)S(1)} %copy.11), channel_id=1, replica_groups=mesh['rep'=2,'tp'=4,'pd'=2,'st'=2] {'pd','st'}, dimensions={0} | all-to-all | bytes 96 | tf_op jit(solution)/shard_map/all_to_all | solution.py:60
  19.5 7.6 %gather_fusion.1 = bf16[12,2048,128]{2,1,0:T(8,128)(2,1)} fusion(bf16[16,2048,128]{2,1,0:T(8,128)(2,1)} %param.10, s32[1024]{0:T(1024)S(1)} %pad_clamp_fusion.2), kind=kCustom, calls=%fused_computation.1 | custom fusion | bytes 12582960 | tf_op jit(solution)/shard_map/jit(_take)/gather | solution.py:62
  27.1 6.1 %broadcast_select_fusion = bf16[4,3,2048,128]{3,2,1,0:T(8,128)(2,1)} fusion(bf16[4,3,2048,128]{3,2,1,0:T(8,128)(2,1)} %bitcast.56, pred[4,3]{1,0:T(4,128)(4,1)S(1)} %compare_and_fusion), kind=kLoop, calls=%fused_computation.12 | loop fusion | flops 3145728 | bytes 12582924 | tf_op jit(solution)/shard_map/jit(_take)/select_n | solution.py:62
  33.2 5.4 %all-to-all-start.1 = ((bf16[4,3,2048,128]{3,2,1,0:T(8,128)(2,1)}), bf16[4,3,2048,128]{3,2,1,0:T(8,128)(2,1)}, u32[]{:S(2)}, u32[]{:S(2)}) async-start(bf16[4,3,2048,128]{3,2,1,0:T(8,128)(2,1)} %broadcast_select_fusion), calls=%async_computation.2 | async-start | bytes 12582912 | tf_op jit(solution)/shard_map/all_to_all | solution.py:69
  39.0 70.3 %all-to-all-done.1 = bf16[4,3,2048,128]{3,2,1,0:T(8,128)(2,1)} async-done(((bf16[4,3,2048,128]{3,2,1,0:T(8,128)(2,1)}), bf16[4,3,2048,128]{3,2,1,0:T(8,128)(2,1)}, u32[]{:S(2)}, u32[]{:S(2)}) %all-to-all-start.1) | async-done | bytes 6291488 | tf_op jit(solution)/shard_map/all_to_all | solution.py:69
  109.3 5.8 %gather_fusion.2 = bf16[8,2048,128]{2,1,0:T(8,128)(2,1)} fusion(bf16[12,2048,128]{2,1,0:T(8,128)(2,1)} %bitcast.12, s32[1024]{0:T(1024)S(1)} %pad_clamp_fusion.1), kind=kCustom, calls=%fused_computation.2 | custom fusion | bytes 8388640 | tf_op jit(solution)/shard_map/jit(_take)/gather | solution.py:73
  115.1 4.6 %broadcast_select_fusion.1 = bf16[8,2048,128]{2,1,0:T(8,128)(2,1)} fusion(bf16[8,2048,128]{2,1,0:T(8,128)(2,1)} %gather_fusion.2, pred[8]{0:T(512)(128)(4,1)S(1)} %compare_and_fusion.1), kind=kLoop, calls=%fused_computation.13 | loop fusion | flops 2097152 | bytes 8388616 | tf_op jit(solution)/shard_map/jit(_take)/select_n | solution.py:73
  119.6 9.3 %gather_fusion.3 = bf16[32,2048,128]{2,1,0:T(8,128)(2,1)} fusion(bf16[8,2048,128]{2,1,0:T(8,128)(2,1)} %broadcast_select_fusion.1, s32[1024]{0:T(1024)S(1)} %pad_clamp_fusion), kind=kCustom, calls=%fused_computation.3 | custom fusion | bytes 33554560 | tf_op jit(solution)/shard_map/jit(_take)/gather | solution.py:87
  128.9 8.1 %fusion.13 = bf16[32,16,128]{2,1,0:T(8,128)(2,1)} fusion(bf16[32,16,2048]{2,1,0:T(8,128)(2,1)S(1)} %bitcast.55, bf16[32,2048,128]{2,1,0:T(8,128)(2,1)} %gather_fusion.3, pred[32]{0:T(512)(128)(4,1)S(1)} %compare_and_fusion.2), kind=kOutput, calls=%fused_computation.19 | convolution fusion | flops 276889600 | bytes 19005472 | tf_op jit(solution)/shard_map/ptd,pdr->ptr/dot_general | solution.py:89
  137.1 9.4 %fusion.31 = f32[512,2048]{1,0:T(8,128)} fusion(bf16[512,2048]{1,0:T(8,128)(2,1)S(1)} %copy-done, bf16[2048,2048]{1,0:T(8,128)(2,1)} %param.9), kind=kOutput, calls=%fused_computation.80 | convolution fusion | flops 4294967296 | bytes 14680064 | tf_op jit(solution)/shard_map/dot_general | solution.py:92
  146.5 1.8 gather_fusion.4
  148.3 1.0 broadcast_select_fusion.2
  149.3 3.5 %all-to-all-start.2 = ((bf16[4,3,64,512]{3,2,1,0:T(8,128)(2,1)}), bf16[4,3,64,512]{3,2,1,0:T(8,128)(2,1)S(1)}, u32[]{:S(2)}, u32[]{:S(2)}) async-start(bf16[4,3,64,512]{3,2,1,0:T(8,128)(2,1)} %broadcast_select_fusion.2), calls=%async_computation.3 | async-start | bytes 1572864 | tf_op jit(solution)/shard_map/all_to_all | solution.py:70
  152.9 11.6 %all-to-all-done.2 = bf16[4,3,64,512]{3,2,1,0:T(8,128)(2,1)S(1)} async-done(((bf16[4,3,64,512]{3,2,1,0:T(8,128)(2,1)}), bf16[4,3,64,512]{3,2,1,0:T(8,128)(2,1)S(1)}, u32[]{:S(2)}, u32[]{:S(2)}) %all-to-all-start.2) | async-done | bytes 786464 | tf_op jit(solution)/shard_map/all_to_all | solution.py:70
  165.2 2.0 gather_fusion.6
  167.2 5.0 %all-reduce.2.cloned.1.call-done = bf16[32,16,128]{2,1,0:T(8,128)(2,1)} async-done(((bf16[32,16,128]{2,1,0:T(8,128)(2,1)}), bf16[32,16,128]{2,1,0:T(8,128)(2,1)}) %all-reduce.2.cloned.1.call-update) | async-done | bytes 131088 | tf_op jit(solution)/shard_map/psum | solution.py:21
  172.1 3.1 %fusion.7 = f32[32,16,512]{2,1,0:T(8,128)} fusion(bf16[32,64,512]{2,1,0:T(8,128)(2,1)} %gather_fusion.6, pred[32]{0:T(512)(128)(4,1)S(1)} %compare_and_fusion.2, bf16[32,16,128]{2,1,0:T(8,128)(2,1)} %all-reduce.2.cloned.1.call-done, s32[]{:T(128)S(6)} %select_n.213), kind=kOutput, calls=%fused_computation.17 | convolution fusion | flops 34865152 | bytes 3276836 | tf_op jit(solution)/shard_map/ueo,uox->uex/dot_general | solution.py:25
  175.2 75.8 %reduce-scatter.2.cloned.1.call-done = f32[512,512]{1,0:T(8,128)} async-done(((f32[512,2048]{1,0:T(8,128)}), f32[512,512]{1,0:T(8,128)}) %reduce-scatter.2.cloned.1.call-update) | async-done | bytes 1048592 | tf_op jit(solution)/shard_map/reduce_scatter | solution.py:93
  251.0 1.7 fusion.16
  252.7 1.0 reshape.368
  253.9 21.8 %all-gather.2.cloned.1.call-done = bf16[64,8192]{1,0:T(8,128)(2,1)} async-done(((bf16[32,8192]{1,0:T(8,128)(2,1)}), bf16[64,8192]{1,0:T(8,128)(2,1)}) %all-gather.2.cloned.1.call-update) | async-done | bytes 1048592 | tf_op jit(solution)/shard_map/all_gather | solution.py:105
  275.7 1.6 convolution_convert_fusion
  277.3 1.0 copy.14
  (43 shorter events, 5.2 us)
Async XLA Ops:
  6.5 122.4 %copy-start = (bf16[512,2048]{1,0:T(8,128)(2,1)S(1)}, bf16[512,2048]{1,0:T(8,128)(2,1)}, u32[]{:S(2)}) copy-start(bf16[512,2048]{1,0:T(8,128)(2,1)} %param.8) | copy-start | bytes 6291460
  33.2 5.4 %copy-start.3 = (s32[1,8]{1,0:T(1,128)S(1)}, s32[1,8]{1,0:T(1,128)}, u32[]{:S(2)}) copy-start(s32[1,8]{1,0:T(1,128)} %param.14) | copy-start | bytes 100
  33.2 5.6 %copy-start.1 = (s32[1,8]{1,0:T(1,128)S(1)}, s32[1,8]{1,0:T(1,128)}, u32[]{:S(2)}) copy-start(s32[1,8]{1,0:T(1,128)} %param.13) | copy-start | bytes 100
  33.2 76.1 %all-to-all-start.1 = ((bf16[4,3,2048,128]{3,2,1,0:T(8,128)(2,1)}), bf16[4,3,2048,128]{3,2,1,0:T(8,128)(2,1)}, u32[]{:S(2)}, u32[]{:S(2)}) async-start(bf16[4,3,2048,128]{3,2,1,0:T(8,128)(2,1)} %broadcast_select_fusion), calls=%async_computation.2 | async-start | bytes 12582912 | tf_op jit(solution)/shard_map/all_to_all | solution.py:69
  38.6 133.6 %all-reduce.2.cloned.1.call-start = ((), (), s32[]{:S(2)}) async-start(), calls=%async_computation.5 | async-start | bytes 262144 | tf_op jit(solution)/shard_map/psum | solution.py:21
  137.0 114.0 %reduce-scatter.2.cloned.1.call-start = ((), (), s32[]{:S(2)}) async-start(), calls=%async_computation.4 | async-start | bytes 5242880 | tf_op jit(solution)/shard_map/reduce_scatter | solution.py:93
  149.3 15.1 %all-to-all-start.2 = ((bf16[4,3,64,512]{3,2,1,0:T(8,128)(2,1)}), bf16[4,3,64,512]{3,2,1,0:T(8,128)(2,1)S(1)}, u32[]{:S(2)}, u32[]{:S(2)}) async-start(bf16[4,3,64,512]{3,2,1,0:T(8,128)(2,1)} %broadcast_select_fusion.2), calls=%async_computation.3 | async-start | bytes 1572864 | tf_op jit(solution)/shard_map/all_to_all | solution.py:70
  152.8 122.9 %all-gather.2.cloned.1.call-start = ((), (), s32[]{:S(2)}) async-start(), calls=%async_computation.6 | async-start | bytes 1572864 | tf_op jit(solution)/shard_map/all_gather | solution.py:105
  167.2 86.6 %copy-start.2 = (s32[4,32]{1,0:T(4,128)S(1)}, s32[4,32]{1,0:T(4,128)}, u32[]{:S(2)}) copy-start(s32[4,32]{1,0:T(4,128)} %param.15) | copy-start | bytes 1540
Sparse Core Ops, SparseCore 0:
  137.2 34.9 all-reduce.1
  174.5 76.4 reduce-scatter.1
  253.9 21.8 all-gather.1
where the time goes:
time: 285 us
  waiting for transfers between devices  184 us (65%)
  local copies, waits for them, and re-layouts  31.2 us (11%)
  matrix products  22.2 us (8%)
  other arithmetic  17 us (6%)
  between operations  13.2 us (5%)
  starting transfers between devices  8.99 us (3%)
  blocking collectives  7.75 us (3%)
    reduce_scatter x1, waiting for transfers between devices, on_device(): lax.psum_scatter(base_part, 'tp', scatter_dimension=1, tiled=True)  75.8 us
    all_to_all x1, waiting for transfers between devices, on_device(): lax.all_to_all(down_page_list, ('pd', 'st'), split_axis=0, concat_axis=0,...  70.3 us
    all_gather x1, waiting for transfers between devices, on_device(): arrived = lax.all_gather(key_value_rows, 'pd', axis=0, tiled=True)  21.8 us
    all_to_all x1, waiting for transfers between devices, on_device(): lax.all_to_all(up_page_list, ('pd', 'st'), split_axis=0, concat_axis=0, t...  11.6 us
    dot_general x1, matrix products, on_device(): jnp.dot(tokens, key_value_matrix, preferred_element_type=jnp.float32)  9.36 us
    gather x1, local copies, waits for them, and re-layouts, on_device(): page_down = jnp.take(request_down, request_of_page, axis=0)  9.27 us
    dot_general x1, matrix products, on_device(): jnp.einsum('ptd,pdr->ptr', token_pages, page_down, preferred_element_type...  8.1 us
    all_to_all x1, blocking collectives, on_device(): lax.all_to_all(asked_pages, ('pd', 'st'), split_axis=0, concat_axis=0, ti...  7.75 us
  transfers between devices with their start and end apart: 5, of which 5 were waited for; matrix products, arithmetic and copies ran while one was open for 6% of the time, Pallas kernels for 0%

commit v1 on v0

v1 whole, which is shorter than its diff:
```python
import functools

import jax
import jax.numpy as jnp
from jax import lax
from jax.experimental import pallas as pl
from jax.experimental.pallas import tpu as pltpu
from jax.sharding import PartitionSpec as P

PAGE_TOKENS = 16
CHUNK_PAGES = 8


adapter_scale = 0.5


def down_kernel(sources, requests, slots, starts, counts, down, *refs):
    rows, outs = refs[:sources], refs[sources:]
    page_count = rows[0].shape[0] // PAGE_TOKENS
    chunk_rows = CHUNK_PAGES * PAGE_TOKENS
    for source in range(sources):
        outs[source][...] = jnp.zeros_like(outs[source])

        @pl.loop(0, requests)
        def _(request):
            slot = slots[source, request]
            start = starts[source, request]
            count = counts[source, request]

            @pl.when(slot >= 0)
            def _():
                @pl.loop(0, (count + CHUNK_PAGES - 1) // CHUNK_PAGES)
                def _(chunk):
                    first = jnp.minimum(start + chunk * CHUNK_PAGES, page_count - CHUNK_PAGES)
                    place = pl.ds(pl.multiple_of(first * PAGE_TOKENS, PAGE_TOKENS), chunk_rows)
                    product = jnp.dot(
                        rows[source][place, :], down[slot], preferred_element_type=jnp.float32
                    )
                    row = first * PAGE_TOKENS + lax.broadcasted_iota(jnp.int32, product.shape, 0)
                    inside = (row >= start * PAGE_TOKENS) & (row < (start + count) * PAGE_TOKENS)
                    held = outs[source][place, :].astype(jnp.float32)
                    outs[source][place, :] = jnp.where(inside, product, held).astype(jnp.bfloat16)


def down_products(row_list, slots, starts, counts, down):
    sources, requests = slots.shape
    token_rows, width = row_list[0].shape
    rank = down.shape[2]
    in_vmem = pl.BlockSpec(memory_space=pltpu.VMEM)
    in_smem = pl.BlockSpec(memory_space=pltpu.SMEM)
    return pl.pallas_call(
        functools.partial(down_kernel, sources, requests),
        out_shape=[jax.ShapeDtypeStruct((token_rows, rank), jnp.bfloat16)] * sources,
        in_specs=[in_smem] * 3 + [in_vmem] * (1 + sources),
        out_specs=[in_vmem] * sources,
        compiler_params=pltpu.CompilerParams(vmem_limit_bytes=40 * 1024 * 1024),
        cost_estimate=pl.CostEstimate(
            flops=2 * sources * token_rows * width * rank,
            bytes_accessed=2 * (down.size + sources * token_rows * (width + rank)),
            transcendentals=0,
        ),
        name="down_products",
    )(slots, starts, counts, down, *row_list)


def shifted(value, axis, step):
    size = lax.axis_size(axis)
    return lax.ppermute(value, axis, [(i, (i + step) % size) for i in range(size)])


def on_device(
    tokens,
    key_value_matrix,
    adapter_down_weight,
    adapter_up_weight,
    adapter_store_slot,
    request_adapter,
    prefill_span_pages,
    decode_pool_slot,
):
    pd_count = lax.axis_size("pd")
    st_count = lax.axis_size("st")
    pd_index = lax.axis_index("pd")
    st_index = lax.axis_index("st")
    groups = pd_count * st_count
    me = pd_index * st_count + st_index
    adapter_rank_value = adapter_up_weight.shape[1]
    column_range = adapter_up_weight.shape[2]
    requests = request_adapter.shape[1]
    slot_capacity = requests // groups + 1
    holding_count = adapter_down_weight.shape[0]
    token_rows = tokens.shape[0]
    page_count = token_rows // PAGE_TOKENS

    travelled = {(0, 0): tokens}
    for step in range(1, pd_count):
        travelled[step, 0] = shifted(tokens, "pd", step)
    for step in range(pd_count):
        for turn in range(1, st_count):
            travelled[step, turn] = shifted(travelled[step, 0], "st", turn)

    asked = jnp.concatenate([request_adapter, prefill_span_pages], axis=1)
    asked = lax.all_gather(asked, ("pd", "st"), axis=0, tiled=True)
    store_slot = jnp.take(adapter_store_slot, asked[:, :requests])
    counts = asked[:, requests:]
    ends = jnp.cumsum(counts, axis=1)
    starts = ends - counts
    holder = store_slot // holding_count
    local_index = store_slot % holding_count
    own_slot = jnp.where(holder == me, local_index, -1)

    base_part = jnp.dot(tokens, key_value_matrix, preferred_element_type=jnp.float32)
    base_sum = lax.psum_scatter(
        base_part.astype(jnp.bfloat16), "tp", scatter_dimension=1, tiled=True
    )

    order_ids = jnp.arange(requests)
    earlier = (holder[:, None, :] == holder[:, :, None]) & (
        order_ids[None, None, :] < order_ids[None, :, None]
    )
    rank_in = jnp.sum(earlier.astype(jnp.int32), axis=2)
    hits = (holder == me)[:, :, None] & (
        rank_in[:, :, None] == jnp.arange(slot_capacity)[None, None, :]
    )
    asked_pages = jnp.sum(jnp.where(hits, local_index[:, :, None], 0), axis=1).reshape(-1)
    up_page_list = jnp.take(adapter_up_weight, asked_pages, axis=0, mode="clip").reshape(
        groups, slot_capacity, adapter_rank_value, column_range
    )
    arrived_up = lax.all_to_all(
        up_page_list, ("pd", "st"), split_axis=0, concat_axis=0, tiled=True
    )
    own_holder = lax.dynamic_index_in_dim(holder, me, 0, keepdims=False)
    own_rank = lax.dynamic_index_in_dim(rank_in, me, 0, keepdims=False)
    own_ends = lax.dynamic_index_in_dim(ends, me, 0, keepdims=False)
    request_of_page = jnp.sum(
        (own_ends[None, :] <= jnp.arange(page_count)[:, None]).astype(jnp.int32), axis=1
    )
    source_of_page = jnp.take(own_holder * slot_capacity + own_rank, request_of_page, mode="clip")
    page_up_weight = jnp.take(
        arrived_up.reshape(groups * slot_capacity, adapter_rank_value, column_range),
        source_of_page,
        axis=0,
        mode="clip",
    )

    inner = None
    for step in range(pd_count):
        source_group = jnp.stack(
            [
                (pd_index - step) % pd_count * st_count + (st_index - turn) % st_count
                for turn in range(st_count)
            ]
        )
        products = down_products(
            [travelled[step, turn] for turn in range(st_count)],
            jnp.take(own_slot, source_group, axis=0, mode="clip"),
            jnp.take(starts, source_group, axis=0, mode="clip"),
            jnp.take(counts, source_group, axis=0, mode="clip"),
            adapter_down_weight,
        )
        chip_sum = products[0]
        for turn in range(1, st_count):
            chip_sum = chip_sum + shifted(products[turn], "st", -turn)
        returned = chip_sum if step == 0 else shifted(chip_sum, "pd", -step)
        inner = returned if inner is None else inner + returned

    adapter_whole = lax.psum(inner, "tp").reshape(page_count, PAGE_TOKENS, -1)
    half_tensor_parallel = lax.axis_size("tp") // 2
    halfway_start = jnp.where(lax.axis_index("tp") >= half_tensor_parallel, adapter_rank_value, 0)
    adapter_halfway = lax.dynamic_slice_in_dim(adapter_whole, halfway_start, adapter_rank_value, 2)
    update = jnp.einsum(
        "ueo,uox->uex", adapter_halfway, page_up_weight, preferred_element_type=jnp.float32
    )
    completed = base_sum.astype(jnp.float32).reshape(update.shape) + adapter_scale * update
    pages = completed.astype(jnp.bfloat16).reshape(page_count, PAGE_TOKENS * column_range)

    slot_table = decode_pool_slot.reshape(pd_count, st_count, page_count)
    slot_table = lax.dynamic_index_in_dim(slot_table, st_index, 1, keepdims=False)
    own_slots = me * page_count + jnp.arange(page_count)
    decode_pool = None
    for step in range(pd_count):
        arrived = pages if step == 0 else shifted(pages, "pd", step)
        dest = lax.dynamic_index_in_dim(
            slot_table, (pd_index - step) % pd_count, 0, keepdims=False
        )
        selector = (dest[None, :] == own_slots[:, None]).astype(jnp.bfloat16)
        picked = jnp.dot(selector, arrived, preferred_element_type=jnp.float32)
        decode_pool = picked if decode_pool is None else decode_pool + picked
    return decode_pool.astype(jnp.bfloat16).reshape(page_count, PAGE_TOKENS, column_range)


def solution(mesh):
    placed = (
        P(("rep", "pd", "st"), "tp"),
        P("tp", None),
        P(("rep", "pd", "st"), "tp", None),
        P(("rep", "pd", "st"), None, "tp"),
        P("rep"),
        P(("rep", "pd", "st"), None),
        P(("rep", "pd", "st"), None),
        P("rep", None),
    )
    return jax.shard_map(
        on_device,
        mesh=mesh,
        in_specs=placed,
        out_specs=P(("rep", "pd", "st"), None, "tp"),
        check_vma=False,
    )
```

time: 285 us -> 151 us (0.53)
  waiting for transfers between devices: 184 us -> 82.9 us
  local copies, waits for them, and re-layouts: 31.2 us -> 13.1 us
  other arithmetic: 17 us -> 1.72 us
  matrix products: 22.2 us -> 12.1 us
  Pallas kernels: 0 us -> 7.13 us
  starting transfers between devices: 8.99 us -> 12.5 us
    reduce_scatter x1, waiting for transfers between devices: 75.8 us -> 0.02 us  [on_device(): lax.psum_scatter(base_part.astype(jnp.bfloat16), 'tp', scatter_dimension=...]
    all_to_all x1 -> x0, waiting for transfers between devices: 70.3 us -> none  [on_device(): lax.all_to_all(down_page_list, ('pd', 'st'), split_axis=0, concat_axis=0,...]
    ppermute x0 -> x7, waiting for transfers between devices: none -> 50.1 us  [shifted(): lax.ppermute(value, axis, [(i, (i + step) % size) for i in range(size)])]
    psum x1, waiting for transfers between devices: 4.96 us -> 32.8 us  [on_device(): adapter_whole = lax.psum(inner, 'tp').reshape(page_count, PAGE_TOKENS, -1)]
    all_gather x1 -> x0, waiting for transfers between devices: 21.8 us -> none  [on_device(): arrived = lax.all_gather(key_value_rows, 'pd', axis=0, tiled=True)]
    gather x7 -> x11, local copies, waits for them, and re-layouts: 28.4 us -> 8.15 us  [the longest x1 1.81 us: on_device(): jnp.take(arrived_up.reshape(groups * slot_capacity, adapter_rank_value, c...]
    select_n x10 -> x1, other arithmetic: 13.3 us -> 0.08 us  [on_device(): own_slot = jnp.where(holder == me, local_index, -1)]
    all_to_all x1, waiting for transfers between devices: 11.6 us -> 0.01 us  [on_device(): lax.all_to_all(up_page_list, ('pd', 'st'), split_axis=0, concat_axis=0, t...]
  transfers between devices with their start and end apart: 5 -> 10, of which waited for: 5 -> 4; matrix products, arithmetic and copies ran while one was open for 6% -> 14% of each run, Pallas kernels for 0% -> 5%
where the time goes in v1:
time: 151 us; the launch traced here: 150 us
  waiting for transfers between devices  82.9 us (55%)
  between operations  13.6 us (9%)
  local copies, waits for them, and re-layouts  13.1 us (9%)
  starting transfers between devices  12.5 us (8%)
  matrix products  12.1 us (8%)
  blocking collectives  7.35 us (5%)
  Pallas kernels  7.13 us (5%)
  other arithmetic  1.72 us (1%)
    ppermute x7, waiting for transfers between devices, shifted(): lax.ppermute(value, axis, [(i, (i + step) % size) for i in range(size)])  50.1 us
    psum x1, waiting for transfers between devices, on_device(): adapter_whole = lax.psum(inner, 'tp').reshape(page_count, PAGE_TOKENS, -1)  32.8 us
    dot_general x1, matrix products, on_device(): jnp.dot(tokens, key_value_matrix, preferred_element_type=jnp.float32)  9.84 us
    ppermute x7, starting transfers between devices, shifted(): lax.ppermute(value, axis, [(i, (i + step) % size) for i in range(size)])  8.22 us
    all_gather x1, blocking collectives, on_device(): asked = lax.all_gather(asked, ('pd', 'st'), axis=0, tiled=True)  7.35 us
    pallas_call x2, Pallas kernels, down_products(): pl.pallas_call(functools.partial(down_kernel, sources, requests), out_sha...  7.13 us
    unnamed x18, local copies, waits for them, and re-layouts  4.66 us
    all_to_all x1, starting transfers between devices, on_device(): lax.all_to_all(up_page_list, ('pd', 'st'), split_axis=0, concat_axis=0, t...  4.2 us
  transfers between devices with their start and end apart: 10, of which 4 were waited for; matrix products, arithmetic and copies ran while one was open for 14% of the time, Pallas kernels for 5%

profile of v1, /device:TPU:0, one launch (start us, length us, event | category | flops | bytes accessed | tf_op | source)
XLA Modules:
  0.0 150.4 jit_solution(5194449662266170359)
XLA Ops:
  6.5 2.9 %collective-permute-start.2 = (bf16[512,2048]{1,0:T(8,128)(2,1)}, bf16[512,2048]{1,0:T(8,128)(2,1)}, u32[]{:S(2)}, u32[]{:S(2)}) collective-permute-start(bf16[512,2048]{1,0:T(8,128)(2,1)} %refs_0_.1), channel_id=1, source_target_pairs={{0,2},{2,0},{1,3},{3,1},{4,6},{6,4},{5,7},{7,5},{8,10},{10,8},{9,1... | collective-permute-start | bytes 6291464 | tf_op jit(solution)/shard_map/ppermute | solution.py:68
  9.5 9.8 %convolution_convert_fusion = bf16[512,2048]{1,0:T(8,128)(2,1)} fusion(bf16[512,2048]{1,0:T(8,128)(2,1)} %refs_0_.1, bf16[2048,2048]{1,0:T(8,128)(2,1)} %param.9), kind=kOutput, calls=%fused_computation.12 | convolution fusion | flops 4296015872 | bytes 12582912 | tf_op jit(solution)/shard_map/dot_general | solution.py:112
  19.4 36.1 %collective-permute-done.2.refs_0_ = bf16[512,2048]{1,0:T(8,128)(2,1)} collective-permute-done((bf16[512,2048]{1,0:T(8,128)(2,1)}, bf16[512,2048]{1,0:T(8,128)(2,1)}, u32[]{:S(2)}, u32[]{:S(2)}) %collective-permute-start.2) | collective-permute-done | bytes 2097184 | tf_op jit(solution)/shard_map/ppermute | solution.py:68
  56.0 7.3 %all-gather = s32[4,1,16]{2,1,0:T(1,128)S(1)} all-gather(s32[1,1,16]{2,1,0:T(1,128)S(1)} %add_bitcast_fusion), channel_id=1, replica_groups=mesh['rep'=2,'tp'=4,'pd'=2,'st'=2] {'pd','st'}, dimensions={0}, use_global_device_ids=true | all-gather | bytes 320 | tf_op jit(solution)/shard_map/all_gather | solution.py:103
  63.5 0.7 gather_fusion
  65.1 1.5 %gather_fusion.7 = bf16[12,64,512]{2,1,0:T(8,128)(2,1)} fusion(bf16[16,64,512]{2,1,0:T(8,128)(2,1)S(1)} %copy-done, s32[1024]{0:T(1024)S(1)} %pad_clamp_fusion.2), kind=kCustom, calls=%fused_computation.7 | custom fusion | bytes 1572912 | tf_op jit(solution)/shard_map/jit(_take)/gather | solution.py:126
  66.7 4.2 %all-to-all-start = ((bf16[4,3,64,512]{3,2,1,0:T(8,128)(2,1)}), bf16[4,3,64,512]{3,2,1,0:T(8,128)(2,1)}, u32[]{:S(2)}, u32[]{:S(2)}) async-start(bf16[4,3,64,512]{3,2,1,0:T(8,128)(2,1)} %bitcast.30), calls=%async_computation.1 | async-start | bytes 1572864 | tf_op jit(solution)/shard_map/all_to_all | solution.py:129
  71.1 0.6 gather_fusion.6
  71.6 0.6 gather_fusion.4
  72.7 0.6 gather_fusion.1
  74.4 3.4 %copy-done.1 = bf16[16,2048,128]{2,1,0:T(8,128)(2,1)S(1)} copy-done((bf16[16,2048,128]{2,1,0:T(8,128)(2,1)S(1)}, bf16[16,2048,128]{2,1,0:T(8,128)(2,1)}, u32[]{:S(2)}) %copy-start.1) | copy-done | bytes 8388632
  77.8 3.5 %down_products.3 = (bf16[512,128]{1,0:T(8,128)(2,1)S(1)}, bf16[512,128]{1,0:T(8,128)(2,1)S(1)}) custom-call(s32[2,8]{1,0:T(2,128)S(1)} %gather_fusion.4, s32[2,8]{1,0:T(2,128)S(1)} %gather_fusion.5, s32[2,8]{1,0:T(2,128)S(1)} %gather_fusion.6, bf16[16,2048,128]{2,1,0:T(8,128)(2,1)S(1)} %copy-done.1, bf16[512,2048]{1,0:T(8,128)(2,1)} %collective-permute-done.2.refs_0_, ...), custom_call_target="tpu_custom_call" | custom-call | flops 536870912 | bytes 12845056 | tf_op jit(solution)/shard_map/down_products/pallas_call | solution.py:51
  81.3 1.6 %collective-permute-start.4 = (bf16[512,128]{1,0:T(8,128)(2,1)S(1)}, bf16[512,128]{1,0:T(8,128)(2,1)S(1)}, u32[]{:S(2)}, u32[]{:S(2)}) collective-permute-start(bf16[512,128]{1,0:T(8,128)(2,1)S(1)} %get-tuple-element.12), channel_id=1, source_target_pairs={{0,1},{1,0},{2,3},{3,2},{4,5},{5,4},{6,7},{7,6},{8,9},{9,8},{10,11... | collective-permute-start | bytes 393224 | tf_op jit(solution)/shard_map/ppermute | solution.py:68
  82.9 3.6 %down_products.2 = (bf16[512,128]{1,0:T(8,128)(2,1)S(1)}, bf16[512,128]{1,0:T(8,128)(2,1)S(1)}) custom-call(s32[2,8]{1,0:T(2,128)S(1)} %gather_fusion.1, s32[2,8]{1,0:T(2,128)S(1)} %gather_fusion.2, s32[2,8]{1,0:T(2,128)S(1)} %gather_fusion.3, bf16[16,2048,128]{2,1,0:T(8,128)(2,1)S(1)} %copy-done.2, bf16[512,2048]{1,0:T(8,128)(2,1)S(1)} %copy-done.3, ...), custom_call_target="tpu_custom_call" | custom-call | flops 536870912 | bytes 12845056 | tf_op jit(solution)/shard_map/down_products/pallas_call | solution.py:51
  86.7 1.6 %collective-permute-start.5 = (bf16[512,128]{1,0:T(8,128)(2,1)S(1)}, bf16[512,128]{1,0:T(8,128)(2,1)S(1)}, u32[]{:S(2)}, u32[]{:S(2)}) collective-permute-start(bf16[512,128]{1,0:T(8,128)(2,1)S(1)} %add.134), channel_id=1, source_target_pairs={{0,2},{2,0},{1,3},{3,1},{4,6},{6,4},{5,7},{7,5},{8,10},{10,8},{9,1... | collective-permute-start | bytes 393224 | tf_op jit(solution)/shard_map/ppermute | solution.py:68
  88.4 4.3 %collective-permute-done.5 = bf16[512,128]{1,0:T(8,128)(2,1)S(1)} collective-permute-done((bf16[512,128]{1,0:T(8,128)(2,1)S(1)}, bf16[512,128]{1,0:T(8,128)(2,1)S(1)}, u32[]{:S(2)}, u32[]{:S(2)}) %collective-permute-start.5) | collective-permute-done | bytes 131104 | tf_op jit(solution)/shard_map/ppermute | solution.py:68
  92.7 0.7 add_add_fusion
  93.4 0.7 gather_fusion.8
  94.1 1.8 %gather_fusion.9 = bf16[32,64,512]{2,1,0:T(8,128)(2,1)S(1)} fusion(bf16[12,64,512]{2,1,0:T(8,128)(2,1)} %bitcast.11, s32[1024]{0:T(1024)S(1)} %pad_clamp_fusion), kind=kCustom, calls=%fused_computation.9 | custom fusion | bytes 4194432 | tf_op jit(solution)/shard_map/jit(_take)/gather | solution.py:139
  96.0 32.8 %all-reduce.2.cloned.1.call-done = bf16[32,16,128]{2,1,0:T(8,128)(2,1)} async-done(((bf16[32,16,128]{2,1,0:T(8,128)(2,1)}), bf16[32,16,128]{2,1,0:T(8,128)(2,1)}) %all-reduce.2.cloned.1.call-update) | async-done | bytes 131088 | tf_op jit(solution)/shard_map/psum | solution.py:167
  128.7 1.6 %fusion.2 = bf16[32,16,512]{2,1,0:T(8,128)(2,1)S(1)} fusion(bf16[32,64,512]{2,1,0:T(8,128)(2,1)S(1)} %gather_fusion.9, bf16[32,16,512]{2,1,0:T(8,128)(2,1)} %bitcast.36, bf16[32,16,128]{2,1,0:T(8,128)(2,1)} %all-reduce.2.cloned.1.call-done, s32[]{:T(128)S(6)} %select_n.112), kind=kOutput, calls=%fused_computation.15 | convolution fusion | flops 34603008 | bytes 3276804 | tf_op jit(solution)/shard_map/ueo,uox->uex/dot_general | solution.py:171
  130.6 1.5 %collective-permute-start.6 = (bf16[32,8192]{1,0:T(8,128)(2,1)S(1)}, bf16[32,8192]{1,0:T(8,128)(2,1)S(1)}, u32[]{:S(2)}, u32[]{:S(2)}) collective-permute-start(bf16[32,8192]{1,0:T(8,128)(2,1)S(1)} %bitcast.31), channel_id=1, source_target_pairs={{0,2},{2,0},{1,3},{3,1},{4,6},{6,4},{5,7},{7,5},{8,10},{10,8},{9,1... | collective-permute-start | bytes 1572872 | tf_op jit(solution)/shard_map/ppermute | solution.py:68
  132.5 9.8 %collective-permute-done.6 = bf16[32,8192]{1,0:T(8,128)(2,1)S(1)} collective-permute-done((bf16[32,8192]{1,0:T(8,128)(2,1)S(1)}, bf16[32,8192]{1,0:T(8,128)(2,1)S(1)}, u32[]{:S(2)}, u32[]{:S(2)}) %collective-permute-start.6) | collective-permute-done | bytes 524320 | tf_op jit(solution)/shard_map/ppermute | solution.py:68
  142.6 1.0 copy.11
  (58 shorter events, 4.8 us)
Async XLA Ops:
  6.5 58.6 %copy-start = (bf16[16,64,512]{2,1,0:T(8,128)(2,1)S(1)}, bf16[16,64,512]{2,1,0:T(8,128)(2,1)}, u32[]{:S(2)}) copy-start(bf16[16,64,512]{2,1,0:T(8,128)(2,1)} %param.11) | copy-start | bytes 3145732
  6.5 89.4 %reduce-scatter.2.cloned.1.call-start = ((), (), s32[]{:S(2)}) async-start(), calls=%async_computation.2 | async-start | bytes 2621440 | tf_op jit(solution)/shard_map/reduce_scatter | solution.py:113
  6.5 48.9 %collective-permute-start.2 = (bf16[512,2048]{1,0:T(8,128)(2,1)}, bf16[512,2048]{1,0:T(8,128)(2,1)}, u32[]{:S(2)}, u32[]{:S(2)}) collective-permute-start(bf16[512,2048]{1,0:T(8,128)(2,1)} %refs_0_.1), channel_id=1, source_target_pairs={{0,2},{2,0},{1,3},{3,1},{4,6},{6,4},{5,7},{7,5},{8,10},{10,8},{9,1... | collective-permute-start | bytes 6291464 | tf_op jit(solution)/shard_map/ppermute | solution.py:68
  19.3 36.1 %copy-start.3 = (bf16[512,2048]{1,0:T(8,128)(2,1)S(1)}, bf16[512,2048]{1,0:T(8,128)(2,1)}, u32[]{:S(2)}) copy-start(bf16[512,2048]{1,0:T(8,128)(2,1)} %refs_0_.1) | copy-start | bytes 6291460
  19.3 36.6 %copy-start.6 = (s32[1,8]{1,0:T(1,128)S(1)}, s32[1,8]{1,0:T(1,128)}, u32[]{:S(2)}) copy-start(s32[1,8]{1,0:T(1,128)} %param.14) | copy-start | bytes 100
  19.3 36.6 %copy-start.7 = (s32[1,8]{1,0:T(1,128)S(1)}, s32[1,8]{1,0:T(1,128)}, u32[]{:S(2)}) copy-start(s32[1,8]{1,0:T(1,128)} %param.13) | copy-start | bytes 100
  19.3 44.2 %copy-start.4 = (s32[64]{0:T(128)S(1)}, s32[64]{0:T(128)}, u32[]{:S(2)}) copy-start(s32[64]{0:T(128)} %param.12) | copy-start | bytes 772
  55.4 19.0 %collective-permute-start.3 = (bf16[512,2048]{1,0:T(8,128)(2,1)}, bf16[512,2048]{1,0:T(8,128)(2,1)}, u32[]{:S(2)}, u32[]{:S(2)}) collective-permute-start(bf16[512,2048]{1,0:T(8,128)(2,1)} %collective-permute-done.2.refs_0_), channel_id=1, source_target_pairs={{0,1},{1,0},{2,3},{3,2},{4,5},{5,4},{6,7},{7,6},{8,9},{9,8},{10,11... | collective-permute-start | bytes 6291464 | tf_op jit(solution)/shard_map/ppermute | solution.py:68
  55.4 27.5 %collective-permute-start = (bf16[512,2048]{1,0:T(8,128)(2,1)S(1)}, bf16[512,2048]{1,0:T(8,128)(2,1)}, u32[]{:S(2)}, u32[]{:S(2)}) collective-permute-start(bf16[512,2048]{1,0:T(8,128)(2,1)S(1)} %copy-done.3), channel_id=1, source_target_pairs={{0,1},{1,0},{2,3},{3,2},{4,5},{5,4},{6,7},{7,6},{8,9},{9,8},{10,11... | collective-permute-start | bytes 6291464 | tf_op jit(solution)/shard_map/ppermute | solution.py:68
  66.7 27.4 %all-to-all-start = ((bf16[4,3,64,512]{3,2,1,0:T(8,128)(2,1)}), bf16[4,3,64,512]{3,2,1,0:T(8,128)(2,1)}, u32[]{:S(2)}, u32[]{:S(2)}) async-start(bf16[4,3,64,512]{3,2,1,0:T(8,128)(2,1)} %bitcast.30), calls=%async_computation.1 | async-start | bytes 1572864 | tf_op jit(solution)/shard_map/all_to_all | solution.py:129
  70.9 57.8 %all-reduce.2.cloned.1.call-start = ((), (), s32[]{:S(2)}) async-start(), calls=%async_computation.3 | async-start | bytes 262144 | tf_op jit(solution)/shard_map/psum | solution.py:167
  74.4 3.4 %copy-start.1 = (bf16[16,2048,128]{2,1,0:T(8,128)(2,1)S(1)}, bf16[16,2048,128]{2,1,0:T(8,128)(2,1)}, u32[]{:S(2)}) copy-start(bf16[16,2048,128]{2,1,0:T(8,128)(2,1)} %down.3) | copy-start | bytes 25165828
  77.8 5.1 %copy-start.2 = (bf16[16,2048,128]{2,1,0:T(8,128)(2,1)S(1)}, bf16[16,2048,128]{2,1,0:T(8,128)(2,1)}, u32[]{:S(2)}) copy-start(bf16[16,2048,128]{2,1,0:T(8,128)(2,1)} %down.3) | copy-start | bytes 25165828
  81.3 5.3 %collective-permute-start.4 = (bf16[512,128]{1,0:T(8,128)(2,1)S(1)}, bf16[512,128]{1,0:T(8,128)(2,1)S(1)}, u32[]{:S(2)}, u32[]{:S(2)}) collective-permute-start(bf16[512,128]{1,0:T(8,128)(2,1)S(1)} %get-tuple-element.12), channel_id=1, source_target_pairs={{0,1},{1,0},{2,3},{3,2},{4,5},{5,4},{6,7},{7,6},{8,9},{9,8},{10,11... | collective-permute-start | bytes 393224 | tf_op jit(solution)/shard_map/ppermute | solution.py:68
  86.6 1.8 %collective-permute-start.1 = (bf16[512,128]{1,0:T(8,128)(2,1)S(1)}, bf16[512,128]{1,0:T(8,128)(2,1)S(1)}, u32[]{:S(2)}, u32[]{:S(2)}) collective-permute-start(bf16[512,128]{1,0:T(8,128)(2,1)S(1)} %get-tuple-element.10), channel_id=1, source_target_pairs={{0,1},{1,0},{2,3},{3,2},{4,5},{5,4},{6,7},{7,6},{8,9},{9,8},{10,11... | collective-permute-start | bytes 393224 | tf_op jit(solution)/shard_map/ppermute | solution.py:68
  86.7 6.0 %collective-permute-start.5 = (bf16[512,128]{1,0:T(8,128)(2,1)S(1)}, bf16[512,128]{1,0:T(8,128)(2,1)S(1)}, u32[]{:S(2)}, u32[]{:S(2)}) collective-permute-start(bf16[512,128]{1,0:T(8,128)(2,1)S(1)} %add.134), channel_id=1, source_target_pairs={{0,2},{2,0},{1,3},{3,1},{4,6},{6,4},{5,7},{7,5},{8,10},{10,8},{9,1... | collective-permute-start | bytes 393224 | tf_op jit(solution)/shard_map/ppermute | solution.py:68
  128.7 3.4 %copy-start.5 = (s32[4,32]{1,0:T(4,128)S(1)}, s32[4,32]{1,0:T(4,128)}, u32[]{:S(2)}) copy-start(s32[4,32]{1,0:T(4,128)} %param.15) | copy-start | bytes 1540
  130.6 11.7 %collective-permute-start.6 = (bf16[32,8192]{1,0:T(8,128)(2,1)S(1)}, bf16[32,8192]{1,0:T(8,128)(2,1)S(1)}, u32[]{:S(2)}, u32[]{:S(2)}) collective-permute-start(bf16[32,8192]{1,0:T(8,128)(2,1)S(1)} %bitcast.31), channel_id=1, source_target_pairs={{0,2},{2,0},{1,3},{3,1},{4,6},{6,4},{5,7},{7,5},{8,10},{10,8},{9,1... | collective-permute-start | bytes 1572872 | tf_op jit(solution)/shard_map/ppermute | solution.py:68
Sparse Core Ops, SparseCore 0:
  19.5 44.1 reduce-scatter.1
  93.5 35.1 all-reduce.1

commit v2 on v1

--- a/solution.py
+++ b/solution.py
@@ -95,9 +95,19 @@
     travelled = {(0, 0): tokens}
     for step in range(1, pd_count):
         travelled[step, 0] = shifted(tokens, "pd", step)
-    for step in range(pd_count):
-        for turn in range(1, st_count):
-            travelled[step, turn] = shifted(travelled[step, 0], "st", turn)
+    for turn in range(1, st_count):
+        travelled[0, turn] = shifted(tokens, "st", turn)
+
+    tokens, near_other = lax.optimization_barrier(
+        (tokens, [travelled[0, turn] for turn in range(1, st_count)])
+    )
+    for turn in range(1, st_count):
+        travelled[0, turn] = near_other[turn - 1]
+    base_part = jnp.dot(tokens, key_value_matrix, preferred_element_type=jnp.float32)
+    base_part, request_adapter, prefill_span_pages = lax.optimization_barrier(
+        (base_part.astype(jnp.bfloat16), request_adapter, prefill_span_pages)
+    )
+    base_sum = lax.psum_scatter(base_part, "tp", scatter_dimension=1, tiled=True)
 
     asked = jnp.concatenate([request_adapter, prefill_span_pages], axis=1)
     asked = lax.all_gather(asked, ("pd", "st"), axis=0, tiled=True)
@@ -109,11 +119,6 @@
     local_index = store_slot % holding_count
     own_slot = jnp.where(holder == me, local_index, -1)
 
-    base_part = jnp.dot(tokens, key_value_matrix, preferred_element_type=jnp.float32)
-    base_sum = lax.psum_scatter(
-        base_part.astype(jnp.bfloat16), "tp", scatter_dimension=1, tiled=True
-    )
-
     order_ids = jnp.arange(requests)
     earlier = (holder[:, None, :] == holder[:, :, None]) & (
         order_ids[None, None, :] < order_ids[None, :, None]
@@ -143,31 +148,60 @@
         mode="clip",
     )
 
-    inner = None
-    for step in range(pd_count):
+    def request_tables(step):
         source_group = jnp.stack(
             [
                 (pd_index - step) % pd_count * st_count + (st_index - turn) % st_count
                 for turn in range(st_count)
             ]
         )
-        products = down_products(
-            [travelled[step, turn] for turn in range(st_count)],
-            jnp.take(own_slot, source_group, axis=0, mode="clip"),
-            jnp.take(starts, source_group, axis=0, mode="clip"),
-            jnp.take(counts, source_group, axis=0, mode="clip"),
-            adapter_down_weight,
-        )
+        tables = [
+            jnp.take(table, source_group, axis=0, mode="clip")
+            for table in (own_slot, starts, counts)
+        ]
+        return tables
+
+    def summed_products(tables, row_list):
+        products = down_products(row_list, *tables, adapter_down_weight)
         chip_sum = products[0]
         for turn in range(1, st_count):
             chip_sum = chip_sum + shifted(products[turn], "st", -turn)
-        returned = chip_sum if step == 0 else shifted(chip_sum, "pd", -step)
-        inner = returned if inner is None else inner + returned
-
-    adapter_whole = lax.psum(inner, "tp").reshape(page_count, PAGE_TOKENS, -1)
-    half_tensor_parallel = lax.axis_size("tp") // 2
-    halfway_start = jnp.where(lax.axis_index("tp") >= half_tensor_parallel, adapter_rank_value, 0)
-    adapter_halfway = lax.dynamic_slice_in_dim(adapter_whole, halfway_start, adapter_rank_value, 2)
+        return chip_sum
+
+    near_rows = [travelled[0, turn] for turn in range(st_count)]
+    inner = summed_products(request_tables(0), near_rows).astype(jnp.float32)
+    far_tables = [request_tables(step) for step in range(1, pd_count)]
+    far_rows = [travelled[step, 0] for step in range(1, pd_count)]
+    inner, page_up_weight, base_sum, far_tables, far_rows = lax.optimization_barrier(
+        (inner, page_up_weight, base_sum, far_tables, far_rows)
+    )
+    for step in range(1, pd_count):
+        rows = far_rows[step - 1]
+        row_list = [rows] + [shifted(rows, "st", turn) for turn in range(1, st_count)]
+        returned = shifted(summed_products(far_tables[step - 1], row_list), "pd", -step)
+        inner = inner + returned
+
+    tp_count = lax.axis_size("tp")
+    half_tensor_parallel = tp_count // 2
+    upper = lax.axis_index("tp") >= half_tensor_parallel
+    half_rows = token_rows // 2
+
+    def packed(columns):
+        return jnp.concatenate([columns[:half_rows], columns[half_rows:]], axis=1)
+
+    first, second = packed(inner[:, :adapter_rank_value]), packed(inner[:, adapter_rank_value:])
+    mine = jnp.where(upper, second, first)
+    theirs = jnp.where(upper, first, second).astype(jnp.bfloat16)
+    mine = mine + shifted(theirs, "tp", half_tensor_parallel)
+    distance = half_tensor_parallel // 2
+    while distance >= 1:
+        pairs = [(i, i ^ distance) for i in range(tp_count)]
+        mine = mine + lax.ppermute(mine.astype(jnp.bfloat16), "tp", pairs)
+        distance //= 2
+    mine = mine.astype(jnp.bfloat16)
+    adapter_halfway = jnp.concatenate(
+        [mine[:, :adapter_rank_value], mine[:, adapter_rank_value:]], axis=0
+    ).reshape(page_count, PAGE_TOKENS, adapter_rank_value)
     update = jnp.einsum(
         "ueo,uox->uex", adapter_halfway, page_up_weight, preferred_element_type=jnp.float32
     )

time: 151 us -> 148 us (0.980)
  waiting for transfers between devices: 82.9 us -> 28.5 us
  blocking collectives: 7.35 us -> 46.7 us
  local copies, waits for them, and re-layouts: 13.1 us -> 22.6 us
  starting transfers between devices: 12.5 us -> 16.4 us
  Pallas kernels: 7.13 us -> 5.32 us
    all_gather x1, blocking collectives: 7.35 us -> 46.7 us  [on_device(): asked = lax.all_gather(asked, ('pd', 'st'), axis=0, tiled=True)]
    psum x1 -> x0, waiting for transfers between devices: 32.8 us -> none  [on_device(): adapter_whole = lax.psum(inner, 'tp').reshape(page_count, PAGE_TOKENS, -1)]
    ppermute x7 -> x8, waiting for transfers between devices: 50.1 us -> 25.5 us  [shifted(): lax.ppermute(value, axis, [(i, (i + step) % size) for i in range(size)])]
    unnamed x18 -> x26, local copies, waits for them, and re-layouts: 4.66 us -> 12.5 us
    ppermute x0 -> x1, waiting for transfers between devices: none -> 2.75 us  [on_device(): mine = mine + lax.ppermute(mine.astype(jnp.bfloat16), 'tp', pairs)]
    ppermute x7 -> x8, starting transfers between devices: 8.22 us -> 10.7 us  [shifted(): lax.ppermute(value, axis, [(i, (i + step) % size) for i in range(size)])]
    pallas_call x2, Pallas kernels: 7.13 us -> 5.32 us  [down_products(): pl.pallas_call(functools.partial(down_kernel, sources, requests), out_sha...]
    ppermute x0 -> x1, starting transfers between devices: none -> 1.58 us  [on_device(): mine = mine + lax.ppermute(mine.astype(jnp.bfloat16), 'tp', pairs)]
  transfers between devices with their start and end apart: 10 -> 11, of which waited for: 4 -> 8; matrix products, arithmetic and copies ran while one was open for 14% -> 8% of each run, Pallas kernels for 5% -> 1%
where the time goes in v2:
time: 148 us; the launch traced here: 147 us
  blocking collectives  46.7 us (32%)
  waiting for transfers between devices  28.5 us (19%)
  local copies, waits for them, and re-layouts  22.6 us (15%)
  starting transfers between devices  16.4 us (11%)
  between operations  13.6 us (9%)
  matrix products  10.9 us (7%)
  Pallas kernels  5.32 us (4%)
  other arithmetic  3.19 us (2%)
    all_gather x1, blocking collectives, on_device(): asked = lax.all_gather(asked, ('pd', 'st'), axis=0, tiled=True)  46.7 us
    ppermute x8, waiting for transfers between devices, shifted(): lax.ppermute(value, axis, [(i, (i + step) % size) for i in range(size)])  25.5 us
    unnamed x26, local copies, waits for them, and re-layouts  12.5 us
    ppermute x8, starting transfers between devices, shifted(): lax.ppermute(value, axis, [(i, (i + step) % size) for i in range(size)])  10.7 us
    dot_general x1, matrix products, on_device(): jnp.dot(tokens, key_value_matrix, preferred_element_type=jnp.float32)  9.85 us
    pallas_call x2, Pallas kernels, down_products(): pl.pallas_call(functools.partial(down_kernel, sources, requests), out_sha...  5.32 us
    all_to_all x1, starting transfers between devices, on_device(): lax.all_to_all(up_page_list, ('pd', 'st'), split_axis=0, concat_axis=0, t...  4.19 us
    gather x6, local copies, waits for them, and re-layouts, request_tables(): jnp.take(table, source_group, axis=0, mode='clip')  3.35 us
  transfers between devices with their start and end apart: 11, of which 8 were waited for; matrix products, arithmetic and copies ran while one was open for 8% of the time, Pallas kernels for 1%

profile of v2, /device:TPU:0, one launch (start us, length us, event | category | flops | bytes accessed | tf_op | source)
XLA Modules:
  0.0 147.2 jit_solution(14107706698283334718)
XLA Ops:
  7.0 4.0 %collective-permute-done.refs_1_ = bf16[512,2048]{1,0:T(8,128)(2,1)S(1)} collective-permute-done((bf16[512,2048]{1,0:T(8,128)(2,1)}, bf16[512,2048]{1,0:T(8,128)(2,1)S(1)}, u32[]{:S(2)}, u32[]{:S(2)}) %collective-permute-start) | collective-permute-done | bytes 2097184 | tf_op jit(solution)/shard_map/ppermute | solution.py:68
  11.0 1.4 copy-done.4
  12.3 9.9 %convolution_convert_fusion = bf16[512,2048]{1,0:T(8,128)(2,1)} fusion(bf16[512,2048]{1,0:T(8,128)(2,1)} %refs_0_.1, bf16[2048,2048]{1,0:T(8,128)(2,1)} %param.9), kind=kOutput, calls=%fused_computation.12 | convolution fusion | flops 4296015872 | bytes 12582912 | tf_op jit(solution)/shard_map/dot_general | solution.py:106
  22.2 1.6 %copy-done.3 = bf16[512,2048]{1,0:T(8,128)(2,1)S(1)} copy-done((bf16[512,2048]{1,0:T(8,128)(2,1)S(1)}, bf16[512,2048]{1,0:T(8,128)(2,1)}, u32[]{:S(2)}) %copy-start.3) | copy-done | bytes 2097176
  23.8 2.9 %collective-permute-start.2 = (bf16[512,2048]{1,0:T(8,128)(2,1)S(1)}, bf16[512,2048]{1,0:T(8,128)(2,1)}, u32[]{:S(2)}, u32[]{:S(2)}) collective-permute-start(bf16[512,2048]{1,0:T(8,128)(2,1)S(1)} %copy-done.3), channel_id=1, source_target_pairs={{0,2},{2,0},{1,3},{3,1},{4,6},{6,4},{5,7},{7,5},{8,10},{10,8},{9,1... | collective-permute-start | bytes 6291464 | tf_op jit(solution)/shard_map/ppermute | solution.py:68
  26.8 46.7 %all-gather = s32[4,1,16]{2,1,0:T(1,128)S(1)} all-gather(s32[1,1,16]{2,1,0:T(1,128)S(1)} %add_bitcast_fusion), channel_id=1, replica_groups=mesh['rep'=2,'tp'=4,'pd'=2,'st'=2] {'pd','st'}, dimensions={0}, use_global_device_ids=true | all-gather | bytes 320 | tf_op jit(solution)/shard_map/all_gather | solution.py:113
  77.0 1.5 %gather_fusion.4 = bf16[12,64,512]{2,1,0:T(8,128)(2,1)} fusion(bf16[16,64,512]{2,1,0:T(8,128)(2,1)S(1)} %copy-done, s32[1024]{0:T(1024)S(1)} %pad_clamp_fusion.3), kind=kCustom, calls=%fused_computation.4 | custom fusion | bytes 1572912 | tf_op jit(solution)/shard_map/jit(_take)/gather | solution.py:131
  78.5 4.2 %all-to-all-start = ((bf16[4,3,64,512]{3,2,1,0:T(8,128)(2,1)}), bf16[4,3,64,512]{3,2,1,0:T(8,128)(2,1)}, u32[]{:S(2)}, u32[]{:S(2)}) async-start(bf16[4,3,64,512]{3,2,1,0:T(8,128)(2,1)} %bitcast.31), calls=%async_computation | async-start | bytes 1572864 | tf_op jit(solution)/shard_map/all_to_all | solution.py:134
  82.8 3.4 %copy-done.1 = bf16[16,2048,128]{2,1,0:T(8,128)(2,1)S(1)} copy-done((bf16[16,2048,128]{2,1,0:T(8,128)(2,1)S(1)}, bf16[16,2048,128]{2,1,0:T(8,128)(2,1)}, u32[]{:S(2)}) %copy-start.1) | copy-done | bytes 8388632
  86.2 1.6 %copy-done.5 = bf16[512,2048]{1,0:T(8,128)(2,1)S(1)} copy-done((bf16[512,2048]{1,0:T(8,128)(2,1)S(1)}, bf16[512,2048]{1,0:T(8,128)(2,1)}, u32[]{:S(2)}) %copy-start.5) | copy-done | bytes 2097176
  87.8 1.7 %down_products.2 = (bf16[512,128]{1,0:T(8,128)(2,1)S(1)}, bf16[512,128]{1,0:T(8,128)(2,1)S(1)}) custom-call(s32[2,8]{1,0:T(2,128)S(1)} %gather_fusion.1, s32[2,8]{1,0:T(2,128)S(1)} %gather_fusion.2, s32[2,8]{1,0:T(2,128)S(1)} %gather_fusion.3, bf16[16,2048,128]{2,1,0:T(8,128)(2,1)S(1)} %copy-done.1, bf16[512,2048]{1,0:T(8,128)(2,1)S(1)} %copy-done.3, ...), custom_call_target="tpu_custom_call" | custom-call | flops 536870912 | bytes 12845056 | tf_op jit(solution)/shard_map/down_products/pallas_call | solution.py:51
  89.5 1.4 collective-permute-start.1
  94.4 3.2 %gather_fusion.6 = bf16[32,64,512]{2,1,0:T(8,128)(2,1)} fusion(bf16[12,64,512]{2,1,0:T(8,128)(2,1)} %bitcast.7, s32[1024]{0:T(1024)S(1)} %pad_clamp_fusion.1), kind=kCustom, calls=%fused_computation.6 | custom fusion | bytes 4194432 | tf_op jit(solution)/shard_map/jit(_take)/gather | solution.py:144
  97.6 4.4 %collective-permute-done.3.refs_1_ = bf16[512,2048]{1,0:T(8,128)(2,1)S(1)} collective-permute-done((bf16[512,2048]{1,0:T(8,128)(2,1)}, bf16[512,2048]{1,0:T(8,128)(2,1)S(1)}, u32[]{:S(2)}, u32[]{:S(2)}) %collective-permute-start.3) | collective-permute-done | bytes 2097184 | tf_op jit(solution)/shard_map/ppermute | solution.py:68
  102.0 3.4 %copy-done.2 = bf16[16,2048,128]{2,1,0:T(8,128)(2,1)S(1)} copy-done((bf16[16,2048,128]{2,1,0:T(8,128)(2,1)S(1)}, bf16[16,2048,128]{2,1,0:T(8,128)(2,1)}, u32[]{:S(2)}) %copy-start.2) | copy-done | bytes 8388632
  105.3 3.6 %down_products.3 = (bf16[512,128]{1,0:T(8,128)(2,1)S(1)}, bf16[512,128]{1,0:T(8,128)(2,1)S(1)}) custom-call(s32[2,8]{1,0:T(2,128)S(1)} %gather_fusion.7, s32[2,8]{1,0:T(2,128)S(1)} %gather_fusion.8, s32[2,8]{1,0:T(2,128)S(1)} %gather_fusion.9, bf16[16,2048,128]{2,1,0:T(8,128)(2,1)S(1)} %copy-done.2, bf16[512,2048]{1,0:T(8,128)(2,1)} %collective-permute-done.2.refs_0_, ...), custom_call_target="tpu_custom_call" | custom-call | flops 536870912 | bytes 12845056 | tf_op jit(solution)/shard_map/down_products/pallas_call | solution.py:51
  109.0 1.3 collective-permute-done.4
  111.7 4.4 %collective-permute-done.5 = bf16[512,128]{1,0:T(8,128)(2,1)} collective-permute-done((bf16[512,128]{1,0:T(8,128)(2,1)S(1)}, bf16[512,128]{1,0:T(8,128)(2,1)}, u32[]{:S(2)}, u32[]{:S(2)}) %collective-permute-start.5) | collective-permute-done | bytes 131104 | tf_op jit(solution)/shard_map/ppermute | solution.py:68
  117.3 2.9 %collective-permute-start.6 = (bf16[256,128]{1,0:T(8,128)(2,1)S(1)}, bf16[256,128]{1,0:T(8,128)(2,1)S(1)}, u32[]{:S(2)}, u32[]{:S(2)}) collective-permute-start(bf16[256,128]{1,0:T(8,128)(2,1)S(1)} %select_convert_fusion), channel_id=1, source_target_pairs={{0,8},{4,12},{8,0},{12,4},{1,9},{5,13},{9,1},{13,5},{2,10},{6,14},... | collective-permute-start | bytes 196616 | tf_op jit(solution)/shard_map/ppermute | solution.py:68
  120.2 2.6 %collective-permute-done.6 = bf16[256,128]{1,0:T(8,128)(2,1)S(1)} collective-permute-done((bf16[256,128]{1,0:T(8,128)(2,1)S(1)}, bf16[256,128]{1,0:T(8,128)(2,1)S(1)}, u32[]{:S(2)}, u32[]{:S(2)}) %collective-permute-start.6) | collective-permute-done | bytes 65568 | tf_op jit(solution)/shard_map/ppermute | solution.py:68
  123.0 1.6 %collective-permute-start.7 = (bf16[256,128]{1,0:T(8,128)(2,1)S(1)}, bf16[256,128]{1,0:T(8,128)(2,1)S(1)}, u32[]{:S(2)}, u32[]{:S(2)}) collective-permute-start(bf16[256,128]{1,0:T(8,128)(2,1)S(1)} %get-tuple-element.37), channel_id=1, source_target_pairs={{0,4},{4,0},{8,12},{12,8},{1,5},{5,1},{9,13},{13,9},{2,6},{6,2},{1... | collective-permute-start | bytes 196616 | tf_op jit(solution)/shard_map/ppermute | solution.py:199
  124.6 2.8 %collective-permute-done.7 = bf16[256,128]{1,0:T(8,128)(2,1)S(1)} collective-permute-done((bf16[256,128]{1,0:T(8,128)(2,1)S(1)}, bf16[256,128]{1,0:T(8,128)(2,1)S(1)}, u32[]{:S(2)}, u32[]{:S(2)}) %collective-permute-start.7) | collective-permute-done | bytes 65568 | tf_op jit(solution)/shard_map/ppermute | solution.py:199
  128.2 1.7 %collective-permute-start.8 = (bf16[32,8192]{1,0:T(8,128)(2,1)S(1)}, bf16[32,8192]{1,0:T(8,128)(2,1)S(1)}, u32[]{:S(2)}, u32[]{:S(2)}) collective-permute-start(bf16[32,8192]{1,0:T(8,128)(2,1)S(1)} %bitcast.33), channel_id=1, source_target_pairs={{0,2},{2,0},{1,3},{3,1},{4,6},{6,4},{5,7},{7,5},{8,10},{10,8},{9,1... | collective-permute-start | bytes 1572872 | tf_op jit(solution)/shard_map/ppermute | solution.py:68
  130.3 8.7 %collective-permute-done.8 = bf16[32,8192]{1,0:T(8,128)(2,1)S(1)} collective-permute-done((bf16[32,8192]{1,0:T(8,128)(2,1)S(1)}, bf16[32,8192]{1,0:T(8,128)(2,1)S(1)}, u32[]{:S(2)}, u32[]{:S(2)}) %collective-permute-start.8) | collective-permute-done | bytes 524320 | tf_op jit(solution)/shard_map/ppermute | solution.py:68
  (74 shorter events, 12.9 us)
Async XLA Ops:
  6.5 70.4 %copy-start = (bf16[16,64,512]{2,1,0:T(8,128)(2,1)S(1)}, bf16[16,64,512]{2,1,0:T(8,128)(2,1)}, u32[]{:S(2)}) copy-start(bf16[16,64,512]{2,1,0:T(8,128)(2,1)} %param.11) | copy-start | bytes 3145732
  6.5 91.1 %reduce-scatter.2.cloned.1.call-start = ((), (), s32[]{:S(2)}) async-start(), calls=%async_computation.2 | async-start | bytes 2621440 | tf_op jit(solution)/shard_map/reduce_scatter | solution.py:110
  6.5 4.5 %collective-permute-start = (bf16[512,2048]{1,0:T(8,128)(2,1)}, bf16[512,2048]{1,0:T(8,128)(2,1)S(1)}, u32[]{:S(2)}, u32[]{:S(2)}) collective-permute-start(bf16[512,2048]{1,0:T(8,128)(2,1)} %refs_0_.1), channel_id=1, source_target_pairs={{0,1},{1,0},{2,3},{3,2},{4,5},{5,4},{6,7},{7,6},{8,9},{9,8},{10,11... | collective-permute-start | bytes 6291464 | tf_op jit(solution)/shard_map/ppermute | solution.py:68
  11.0 1.4 copy-start.4
  22.2 1.6 %copy-start.3 = (bf16[512,2048]{1,0:T(8,128)(2,1)S(1)}, bf16[512,2048]{1,0:T(8,128)(2,1)}, u32[]{:S(2)}) copy-start(bf16[512,2048]{1,0:T(8,128)(2,1)} %refs_0_.1) | copy-start | bytes 6291460
  22.2 4.6 %copy-start.10 = (s32[1,8]{1,0:T(1,128)S(1)}, s32[1,8]{1,0:T(1,128)}, u32[]{:S(2)}) copy-start(s32[1,8]{1,0:T(1,128)} %param.14) | copy-start | bytes 100
  22.2 4.6 %copy-start.11 = (s32[1,8]{1,0:T(1,128)S(1)}, s32[1,8]{1,0:T(1,128)}, u32[]{:S(2)}) copy-start(s32[1,8]{1,0:T(1,128)} %param.13) | copy-start | bytes 100
  22.2 52.2 %copy-start.6 = (s32[64]{0:T(128)S(1)}, s32[64]{0:T(128)}, u32[]{:S(2)}) copy-start(s32[64]{0:T(128)} %param.12) | copy-start | bytes 772
  23.8 73.8 %collective-permute-start.2 = (bf16[512,2048]{1,0:T(8,128)(2,1)S(1)}, bf16[512,2048]{1,0:T(8,128)(2,1)}, u32[]{:S(2)}, u32[]{:S(2)}) collective-permute-start(bf16[512,2048]{1,0:T(8,128)(2,1)S(1)} %copy-done.3), channel_id=1, source_target_pairs={{0,2},{2,0},{1,3},{3,1},{4,6},{6,4},{5,7},{7,5},{8,10},{10,8},{9,1... | collective-permute-start | bytes 6291464 | tf_op jit(solution)/shard_map/ppermute | solution.py:68
  78.5 15.9 %all-to-all-start = ((bf16[4,3,64,512]{3,2,1,0:T(8,128)(2,1)}), bf16[4,3,64,512]{3,2,1,0:T(8,128)(2,1)}, u32[]{:S(2)}, u32[]{:S(2)}) async-start(bf16[4,3,64,512]{3,2,1,0:T(8,128)(2,1)} %bitcast.31), calls=%async_computation | async-start | bytes 1572864 | tf_op jit(solution)/shard_map/all_to_all | solution.py:134
  82.8 3.4 %copy-start.1 = (bf16[16,2048,128]{2,1,0:T(8,128)(2,1)S(1)}, bf16[16,2048,128]{2,1,0:T(8,128)(2,1)}, u32[]{:S(2)}) copy-start(bf16[16,2048,128]{2,1,0:T(8,128)(2,1)} %down.3) | copy-start | bytes 25165828
  86.2 1.6 %copy-start.5 = (bf16[512,2048]{1,0:T(8,128)(2,1)S(1)}, bf16[512,2048]{1,0:T(8,128)(2,1)}, u32[]{:S(2)}) copy-start(bf16[512,2048]{1,0:T(8,128)(2,1)} %copy-done.4) | copy-start | bytes 6291460
  89.5 3.8 %collective-permute-start.1 = (bf16[512,128]{1,0:T(8,128)(2,1)S(1)}, bf16[512,128]{1,0:T(8,128)(2,1)}, u32[]{:S(2)}, u32[]{:S(2)}) collective-permute-start(bf16[512,128]{1,0:T(8,128)(2,1)S(1)} %get-tuple-element.26), channel_id=1, source_target_pairs={{0,1},{1,0},{2,3},{3,2},{4,5},{5,4},{6,7},{7,6},{8,9},{9,8},{10,11... | collective-permute-start | bytes 393224 | tf_op jit(solution)/shard_map/ppermute | solution.py:68
  97.6 4.4 %collective-permute-start.3 = (bf16[512,2048]{1,0:T(8,128)(2,1)}, bf16[512,2048]{1,0:T(8,128)(2,1)S(1)}, u32[]{:S(2)}, u32[]{:S(2)}) collective-permute-start(bf16[512,2048]{1,0:T(8,128)(2,1)} %collective-permute-done.2.refs_0_), channel_id=1, source_target_pairs={{0,1},{1,0},{2,3},{3,2},{4,5},{5,4},{6,7},{7,6},{8,9},{9,8},{10,11... | collective-permute-start | bytes 6291464 | tf_op jit(solution)/shard_map/ppermute | solution.py:68
  102.0 3.4 %copy-start.2 = (bf16[16,2048,128]{2,1,0:T(8,128)(2,1)S(1)}, bf16[16,2048,128]{2,1,0:T(8,128)(2,1)}, u32[]{:S(2)}) copy-start(bf16[16,2048,128]{2,1,0:T(8,128)(2,1)} %down.3) | copy-start | bytes 25165828
  109.0 1.4 collective-permute-start.4
  110.4 17.1 %copy-start.7 = (bf16[32,64,512]{2,1,0:T(8,128)(2,1)S(1)}, bf16[32,64,512]{2,1,0:T(8,128)(2,1)}, u32[]{:S(2)}) copy-start(bf16[32,64,512]{2,1,0:T(8,128)(2,1)} %gather_fusion.6) | copy-start | bytes 6291460
  110.4 5.7 %collective-permute-start.5 = (bf16[512,128]{1,0:T(8,128)(2,1)S(1)}, bf16[512,128]{1,0:T(8,128)(2,1)}, u32[]{:S(2)}, u32[]{:S(2)}) collective-permute-start(bf16[512,128]{1,0:T(8,128)(2,1)S(1)} %add.140), channel_id=1, source_target_pairs={{0,2},{2,0},{1,3},{3,1},{4,6},{6,4},{5,7},{7,5},{8,10},{10,8},{9,1... | collective-permute-start | bytes 393224 | tf_op jit(solution)/shard_map/ppermute | solution.py:68
  111.7 15.8 %copy-start.8 = (bf16[512,512]{1,0:T(8,128)(2,1)S(1)}, bf16[512,512]{1,0:T(8,128)(2,1)}, u32[]{:S(2)}) copy-start(bf16[512,512]{1,0:T(8,128)(2,1)} %reduce-scatter.2.cloned.1.call-done) | copy-start | bytes 1572868
  117.3 5.5 %collective-permute-start.6 = (bf16[256,128]{1,0:T(8,128)(2,1)S(1)}, bf16[256,128]{1,0:T(8,128)(2,1)S(1)}, u32[]{:S(2)}, u32[]{:S(2)}) collective-permute-start(bf16[256,128]{1,0:T(8,128)(2,1)S(1)} %select_convert_fusion), channel_id=1, source_target_pairs={{0,8},{4,12},{8,0},{12,4},{1,9},{5,13},{9,1},{13,5},{2,10},{6,14},... | collective-permute-start | bytes 196616 | tf_op jit(solution)/shard_map/ppermute | solution.py:68
  123.0 4.3 %collective-permute-start.7 = (bf16[256,128]{1,0:T(8,128)(2,1)S(1)}, bf16[256,128]{1,0:T(8,128)(2,1)S(1)}, u32[]{:S(2)}, u32[]{:S(2)}) collective-permute-start(bf16[256,128]{1,0:T(8,128)(2,1)S(1)} %get-tuple-element.37), channel_id=1, source_target_pairs={{0,4},{4,0},{8,12},{12,8},{1,5},{5,1},{9,13},{13,9},{2,6},{6,2},{1... | collective-permute-start | bytes 196616 | tf_op jit(solution)/shard_map/ppermute | solution.py:199
  127.5 2.4 %copy-start.9 = (s32[4,32]{1,0:T(4,128)S(1)}, s32[4,32]{1,0:T(4,128)}, u32[]{:S(2)}) copy-start(s32[4,32]{1,0:T(4,128)} %param.15) | copy-start | bytes 1540
  128.2 10.8 %collective-permute-start.8 = (bf16[32,8192]{1,0:T(8,128)(2,1)S(1)}, bf16[32,8192]{1,0:T(8,128)(2,1)S(1)}, u32[]{:S(2)}, u32[]{:S(2)}) collective-permute-start(bf16[32,8192]{1,0:T(8,128)(2,1)S(1)} %bitcast.33), channel_id=1, source_target_pairs={{0,2},{2,0},{1,3},{3,1},{4,6},{6,4},{5,7},{7,5},{8,10},{10,8},{9,1... | collective-permute-start | bytes 1572872 | tf_op jit(solution)/shard_map/ppermute | solution.py:68
Sparse Core Ops, SparseCore 0:
  22.4 46.4 reduce-scatter.1

commit v3 on v2

--- a/solution.py
+++ b/solution.py
@@ -92,25 +92,35 @@
     token_rows = tokens.shape[0]
     page_count = token_rows // PAGE_TOKENS
 
+    asked = jnp.concatenate([request_adapter, prefill_span_pages], axis=1)
+    asked_by_step = [asked] + [shifted(asked, "pd", step) for step in range(1, pd_count)]
+    tokens, asked_by_step = lax.optimization_barrier((tokens, asked_by_step))
+    asked_steps = jnp.stack(asked_by_step)
+    asked_turns = jnp.stack(
+        [asked_steps] + [shifted(asked_steps, "st", turn) for turn in range(1, st_count)], axis=1
+    )
+
     travelled = {(0, 0): tokens}
+    for turn in range(1, st_count):
+        travelled[0, turn] = shifted(tokens, "st", turn)
     for step in range(1, pd_count):
         travelled[step, 0] = shifted(tokens, "pd", step)
-    for turn in range(1, st_count):
-        travelled[0, turn] = shifted(tokens, "st", turn)
-
-    tokens, near_other = lax.optimization_barrier(
-        (tokens, [travelled[0, turn] for turn in range(1, st_count)])
+
+    tokens, asked_turns, near_other = lax.optimization_barrier(
+        (tokens, asked_turns, [travelled[0, turn] for turn in range(1, st_count)])
     )
     for turn in range(1, st_count):
         travelled[0, turn] = near_other[turn - 1]
     base_part = jnp.dot(tokens, key_value_matrix, preferred_element_type=jnp.float32)
-    base_part, request_adapter, prefill_span_pages = lax.optimization_barrier(
-        (base_part.astype(jnp.bfloat16), request_adapter, prefill_span_pages)
-    )
+    base_part, asked_turns = lax.optimization_barrier((base_part.astype(jnp.bfloat16), asked_turns))
     base_sum = lax.psum_scatter(base_part, "tp", scatter_dimension=1, tiled=True)
 
-    asked = jnp.concatenate([request_adapter, prefill_span_pages], axis=1)
-    asked = lax.all_gather(asked, ("pd", "st"), axis=0, tiled=True)
+    by_pd = jnp.take(
+        asked_turns, (pd_index - jnp.arange(pd_count)) % pd_count, axis=0, mode="clip"
+    )
+    asked = jnp.take(
+        by_pd, (st_index - jnp.arange(st_count)) % st_count, axis=1, mode="clip"
+    ).reshape(groups, 2 * requests)
     store_slot = jnp.take(adapter_store_slot, asked[:, :requests])
     counts = asked[:, requests:]
     ends = jnp.cumsum(counts, axis=1)

time: 148 us -> 139 us (0.939)
  blocking collectives: 46.7 us -> 0 us
  waiting for transfers between devices: 28.5 us -> 61.5 us
  starting transfers between devices: 16.4 us -> 20.9 us
    all_gather x1 -> x0, blocking collectives: 46.7 us -> none  [on_device(): asked = lax.all_gather(asked, ('pd', 'st'), axis=0, tiled=True)]
    all_to_all x1, waiting for transfers between devices: 0.19 us -> 31.9 us  [on_device(): lax.all_to_all(up_page_list, ('pd', 'st'), split_axis=0, concat_axis=0, t...]
    ppermute x8 -> x10, starting transfers between devices: 10.7 us -> 15.4 us  [shifted(): lax.ppermute(value, axis, [(i, (i + step) % size) for i in range(size)])]
    ppermute x8 -> x10, waiting for transfers between devices: 25.5 us -> 26.6 us  [shifted(): lax.ppermute(value, axis, [(i, (i + step) % size) for i in range(size)])]
    unnamed x26 -> x22, local copies, waits for them, and re-layouts: 12.5 us -> 12.4 us
  transfers between devices with their start and end apart: 11 -> 13, of which waited for: 8 -> 10; matrix products, arithmetic and copies ran while one was open for 8% -> 9% of each run, Pallas kernels for 1% -> 1%
where the time goes in v3:
time: 139 us; the launch traced here: 138 us
  waiting for transfers between devices  61.5 us (44%)
  local copies, waits for them, and re-layouts  23.5 us (17%)
  starting transfers between devices  20.9 us (15%)
  between operations  13.7 us (10%)
  matrix products  10.9 us (8%)
  other arithmetic  3.99 us (3%)
  Pallas kernels  3.86 us (3%)
    all_to_all x1, waiting for transfers between devices, on_device(): lax.all_to_all(up_page_list, ('pd', 'st'), split_axis=0, concat_axis=0, t...  31.9 us
    ppermute x10, waiting for transfers between devices, shifted(): lax.ppermute(value, axis, [(i, (i + step) % size) for i in range(size)])  26.6 us
    ppermute x10, starting transfers between devices, shifted(): lax.ppermute(value, axis, [(i, (i + step) % size) for i in range(size)])  15.4 us
    unnamed x22, local copies, waits for them, and re-layouts  12.4 us
    dot_general x1, matrix products, on_device(): jnp.dot(tokens, key_value_matrix, preferred_element_type=jnp.float32)  9.85 us
    all_to_all x1, starting transfers between devices, on_device(): lax.all_to_all(up_page_list, ('pd', 'st'), split_axis=0, concat_axis=0, t...  4.19 us
    pallas_call x2, Pallas kernels, down_products(): pl.pallas_call(functools.partial(down_kernel, sources, requests), out_sha...  3.86 us
    gather x6, local copies, waits for them, and re-layouts, request_tables(): jnp.take(table, source_group, axis=0, mode='clip')  3.36 us
  transfers between devices with their start and end apart: 13, of which 10 were waited for; matrix products, arithmetic and copies ran while one was open for 9% of the time, Pallas kernels for 1%

profile of v3, /device:TPU:0, one launch (start us, length us, event | category | flops | bytes accessed | tf_op | source)
XLA Modules:
  0.0 138.4 jit_solution(9859633333311798257)
XLA Ops:
  7.4 2.9 %collective-permute-start = (s32[1,16]{1,0:T(1,128)S(1)}, s32[1,16]{1,0:T(1,128)S(1)}, u32[]{:S(2)}, u32[]{:S(2)}) collective-permute-start(s32[1,16]{1,0:T(1,128)S(1)} %pad_add_fusion.2), channel_id=1, source_target_pairs={{0,2},{2,0},{1,3},{3,1},{4,6},{6,4},{5,7},{7,5},{8,10},{10,8},{9,1... | collective-permute-start | bytes 200 | tf_op jit(solution)/shard_map/ppermute | solution.py:68
  10.3 1.5 %collective-permute-done = s32[1,16]{1,0:T(1,128)S(1)} collective-permute-done((s32[1,16]{1,0:T(1,128)S(1)}, s32[1,16]{1,0:T(1,128)S(1)}, u32[]{:S(2)}, u32[]{:S(2)}) %collective-permute-start) | collective-permute-done | bytes 96 | tf_op jit(solution)/shard_map/ppermute | solution.py:68
  12.3 3.3 %collective-permute-done.1 = s32[2,1,16]{2,1,0:T(1,128)S(1)} collective-permute-done((s32[2,1,16]{2,1,0:T(1,128)S(1)}, s32[2,1,16]{2,1,0:T(1,128)S(1)}, u32[]{:S(2)}, u32[]{:S(2)}) %collective-permute-start.1) | collective-permute-done | bytes 160 | tf_op jit(solution)/shard_map/ppermute | solution.py:68
  17.5 9.8 %convolution_convert_fusion = bf16[512,2048]{1,0:T(8,128)(2,1)} fusion(bf16[512,2048]{1,0:T(8,128)(2,1)} %refs_0_, bf16[2048,2048]{1,0:T(8,128)(2,1)} %param.9), kind=kOutput, calls=%fused_computation.14 | convolution fusion | flops 4296015872 | bytes 12582912 | tf_op jit(solution)/shard_map/dot_general | solution.py:114
  27.6 1.4 %copy-done.3 = bf16[512,2048]{1,0:T(8,128)(2,1)S(1)} copy-done((bf16[512,2048]{1,0:T(8,128)(2,1)S(1)}, bf16[512,2048]{1,0:T(8,128)(2,1)}, u32[]{:S(2)}) %copy-start.3) | copy-done | bytes 2097176
  28.9 2.0 %collective-permute-start.4 = (bf16[512,2048]{1,0:T(8,128)(2,1)S(1)}, bf16[512,2048]{1,0:T(8,128)(2,1)}, u32[]{:S(2)}, u32[]{:S(2)}) collective-permute-start(bf16[512,2048]{1,0:T(8,128)(2,1)S(1)} %copy-done.3), channel_id=1, source_target_pairs={{0,2},{2,0},{1,3},{3,1},{4,6},{6,4},{5,7},{7,5},{8,10},{10,8},{9,1... | collective-permute-start | bytes 6291464 | tf_op jit(solution)/shard_map/ppermute | solution.py:68
  35.7 1.5 %gather_fusion.6 = bf16[12,64,512]{2,1,0:T(8,128)(2,1)} fusion(bf16[16,64,512]{2,1,0:T(8,128)(2,1)S(1)} %copy-done, s32[1024]{0:T(1024)S(1)} %pad_clamp_fusion.3), kind=kCustom, calls=%fused_computation.6 | custom fusion | bytes 1572912 | tf_op jit(solution)/shard_map/jit(_take)/gather | solution.py:141
  37.2 4.2 %all-to-all-start = ((bf16[4,3,64,512]{3,2,1,0:T(8,128)(2,1)}), bf16[4,3,64,512]{3,2,1,0:T(8,128)(2,1)}, u32[]{:S(2)}, u32[]{:S(2)}) async-start(bf16[4,3,64,512]{3,2,1,0:T(8,128)(2,1)} %bitcast.41), calls=%async_computation | async-start | bytes 1572864 | tf_op jit(solution)/shard_map/all_to_all | solution.py:144
  41.5 3.4 %copy-done.1 = bf16[16,2048,128]{2,1,0:T(8,128)(2,1)S(1)} copy-done((bf16[16,2048,128]{2,1,0:T(8,128)(2,1)S(1)}, bf16[16,2048,128]{2,1,0:T(8,128)(2,1)}, u32[]{:S(2)}) %copy-start.1) | copy-done | bytes 8388632
  44.9 1.6 %copy-done.5 = bf16[512,2048]{1,0:T(8,128)(2,1)S(1)} copy-done((bf16[512,2048]{1,0:T(8,128)(2,1)S(1)}, bf16[512,2048]{1,0:T(8,128)(2,1)}, u32[]{:S(2)}) %copy-start.5) | copy-done | bytes 2097176
  46.5 1.4 %down_products.2 = (bf16[512,128]{1,0:T(8,128)(2,1)S(1)}, bf16[512,128]{1,0:T(8,128)(2,1)S(1)}) custom-call(s32[2,8]{1,0:T(2,128)S(1)} %gather_fusion.3, s32[2,8]{1,0:T(2,128)S(1)} %gather_fusion.4, s32[2,8]{1,0:T(2,128)S(1)} %gather_fusion.5, bf16[16,2048,128]{2,1,0:T(8,128)(2,1)S(1)} %copy-done.1, bf16[512,2048]{1,0:T(8,128)(2,1)S(1)} %copy-done.3, ...), custom_call_target="tpu_custom_call" | custom-call | flops 536870912 | bytes 12845056 | tf_op jit(solution)/shard_map/down_products/pallas_call | solution.py:51
  47.9 2.3 %collective-permute-start.3 = (bf16[512,128]{1,0:T(8,128)(2,1)S(1)}, bf16[512,128]{1,0:T(8,128)(2,1)}, u32[]{:S(2)}, u32[]{:S(2)}) collective-permute-start(bf16[512,128]{1,0:T(8,128)(2,1)S(1)} %get-tuple-element.32), channel_id=1, source_target_pairs={{0,1},{1,0},{2,3},{3,2},{4,5},{5,4},{6,7},{7,6},{8,9},{9,8},{10,11... | collective-permute-start | bytes 393224 | tf_op jit(solution)/shard_map/ppermute | solution.py:68
  53.5 31.9 %all-to-all-done = bf16[4,3,64,512]{3,2,1,0:T(8,128)(2,1)} async-done(((bf16[4,3,64,512]{3,2,1,0:T(8,128)(2,1)}), bf16[4,3,64,512]{3,2,1,0:T(8,128)(2,1)}, u32[]{:S(2)}, u32[]{:S(2)}) %all-to-all-start) | async-done | bytes 786464 | tf_op jit(solution)/shard_map/all_to_all | solution.py:144
  85.4 3.1 %gather_fusion.8 = bf16[32,64,512]{2,1,0:T(8,128)(2,1)} fusion(bf16[12,64,512]{2,1,0:T(8,128)(2,1)} %bitcast.14, s32[1024]{0:T(1024)S(1)} %pad_clamp_fusion.1), kind=kCustom, calls=%fused_computation.8 | custom fusion | bytes 4194432 | tf_op jit(solution)/shard_map/jit(_take)/gather | solution.py:154
  88.6 4.4 %collective-permute-done.5.refs_1_ = bf16[512,2048]{1,0:T(8,128)(2,1)S(1)} collective-permute-done((bf16[512,2048]{1,0:T(8,128)(2,1)}, bf16[512,2048]{1,0:T(8,128)(2,1)S(1)}, u32[]{:S(2)}, u32[]{:S(2)}) %collective-permute-start.5) | collective-permute-done | bytes 2097184 | tf_op jit(solution)/shard_map/ppermute | solution.py:68
  92.9 3.4 %copy-done.2 = bf16[16,2048,128]{2,1,0:T(8,128)(2,1)S(1)} copy-done((bf16[16,2048,128]{2,1,0:T(8,128)(2,1)S(1)}, bf16[16,2048,128]{2,1,0:T(8,128)(2,1)}, u32[]{:S(2)}) %copy-start.2) | copy-done | bytes 8388632
  96.3 2.4 %down_products.3 = (bf16[512,128]{1,0:T(8,128)(2,1)S(1)}, bf16[512,128]{1,0:T(8,128)(2,1)S(1)}) custom-call(s32[2,8]{1,0:T(2,128)S(1)} %gather_fusion.9, s32[2,8]{1,0:T(2,128)S(1)} %gather_fusion.10, s32[2,8]{1,0:T(2,128)S(1)} %gather_fusion.11, bf16[16,2048,128]{2,1,0:T(8,128)(2,1)S(1)} %copy-done.2, bf16[512,2048]{1,0:T(8,128)(2,1)} %collective-permute-done.4.refs_0_, ...), custom_call_target="tpu_custom_call" | custom-call | flops 536870912 | bytes 12845056 | tf_op jit(solution)/shard_map/down_products/pallas_call | solution.py:51
  101.2 1.8 %collective-permute-start.7 = (bf16[512,128]{1,0:T(8,128)(2,1)S(1)}, bf16[512,128]{1,0:T(8,128)(2,1)}, u32[]{:S(2)}, u32[]{:S(2)}) collective-permute-start(bf16[512,128]{1,0:T(8,128)(2,1)S(1)} %add.166), channel_id=1, source_target_pairs={{0,2},{2,0},{1,3},{3,1},{4,6},{6,4},{5,7},{7,5},{8,10},{10,8},{9,1... | collective-permute-start | bytes 393224 | tf_op jit(solution)/shard_map/ppermute | solution.py:68
  103.0 4.1 %collective-permute-done.7 = bf16[512,128]{1,0:T(8,128)(2,1)} collective-permute-done((bf16[512,128]{1,0:T(8,128)(2,1)S(1)}, bf16[512,128]{1,0:T(8,128)(2,1)}, u32[]{:S(2)}, u32[]{:S(2)}) %collective-permute-start.7) | collective-permute-done | bytes 131104 | tf_op jit(solution)/shard_map/ppermute | solution.py:68
  108.3 2.9 %collective-permute-start.8 = (bf16[256,128]{1,0:T(8,128)(2,1)S(1)}, bf16[256,128]{1,0:T(8,128)(2,1)S(1)}, u32[]{:S(2)}, u32[]{:S(2)}) collective-permute-start(bf16[256,128]{1,0:T(8,128)(2,1)S(1)} %select_convert_fusion), channel_id=1, source_target_pairs={{0,8},{4,12},{8,0},{12,4},{1,9},{5,13},{9,1},{13,5},{2,10},{6,14},... | collective-permute-start | bytes 196616 | tf_op jit(solution)/shard_map/ppermute | solution.py:68
  111.2 2.9 %collective-permute-done.8 = bf16[256,128]{1,0:T(8,128)(2,1)S(1)} collective-permute-done((bf16[256,128]{1,0:T(8,128)(2,1)S(1)}, bf16[256,128]{1,0:T(8,128)(2,1)S(1)}, u32[]{:S(2)}, u32[]{:S(2)}) %collective-permute-start.8) | collective-permute-done | bytes 65568 | tf_op jit(solution)/shard_map/ppermute | solution.py:68
  115.5 3.0 %collective-permute-done.9 = bf16[256,128]{1,0:T(8,128)(2,1)S(1)} collective-permute-done((bf16[256,128]{1,0:T(8,128)(2,1)S(1)}, bf16[256,128]{1,0:T(8,128)(2,1)S(1)}, u32[]{:S(2)}, u32[]{:S(2)}) %collective-permute-start.9) | collective-permute-done | bytes 65568 | tf_op jit(solution)/shard_map/ppermute | solution.py:209
  119.4 1.6 %collective-permute-start.10 = (bf16[32,8192]{1,0:T(8,128)(2,1)S(1)}, bf16[32,8192]{1,0:T(8,128)(2,1)S(1)}, u32[]{:S(2)}, u32[]{:S(2)}) collective-permute-start(bf16[32,8192]{1,0:T(8,128)(2,1)S(1)} %bitcast.43), channel_id=1, source_target_pairs={{0,2},{2,0},{1,3},{3,1},{4,6},{6,4},{5,7},{7,5},{8,10},{10,8},{9,1... | collective-permute-start | bytes 1572872 | tf_op jit(solution)/shard_map/ppermute | solution.py:68
  121.3 8.9 %collective-permute-done.10 = bf16[32,8192]{1,0:T(8,128)(2,1)S(1)} collective-permute-done((bf16[32,8192]{1,0:T(8,128)(2,1)S(1)}, bf16[32,8192]{1,0:T(8,128)(2,1)S(1)}, u32[]{:S(2)}, u32[]{:S(2)}) %collective-permute-start.10) | collective-permute-done | bytes 524320 | tf_op jit(solution)/shard_map/ppermute | solution.py:68
  (83 shorter events, 19.0 us)
Async XLA Ops:
  6.5 29.1 %copy-start = (bf16[16,64,512]{2,1,0:T(8,128)(2,1)S(1)}, bf16[16,64,512]{2,1,0:T(8,128)(2,1)}, u32[]{:S(2)}) copy-start(bf16[16,64,512]{2,1,0:T(8,128)(2,1)} %param.11) | copy-start | bytes 3145732
  6.5 82.0 %reduce-scatter.2.cloned.1.call-start = ((), (), s32[]{:S(2)}) async-start(), calls=%async_computation.2 | async-start | bytes 2621440 | tf_op jit(solution)/shard_map/reduce_scatter | solution.py:116
  7.4 4.5 %collective-permute-start = (s32[1,16]{1,0:T(1,128)S(1)}, s32[1,16]{1,0:T(1,128)S(1)}, u32[]{:S(2)}, u32[]{:S(2)}) collective-permute-start(s32[1,16]{1,0:T(1,128)S(1)} %pad_add_fusion.2), channel_id=1, source_target_pairs={{0,2},{2,0},{1,3},{3,1},{4,6},{6,4},{5,7},{7,5},{8,10},{10,8},{9,1... | collective-permute-start | bytes 200 | tf_op jit(solution)/shard_map/ppermute | solution.py:68
  11.8 4.4 %collective-permute-start.2 = (bf16[512,2048]{1,0:T(8,128)(2,1)}, bf16[512,2048]{1,0:T(8,128)(2,1)S(1)}, u32[]{:S(2)}, u32[]{:S(2)}) collective-permute-start(bf16[512,2048]{1,0:T(8,128)(2,1)} %refs_0_), channel_id=1, source_target_pairs={{0,1},{1,0},{2,3},{3,2},{4,5},{5,4},{6,7},{7,6},{8,9},{9,8},{10,11... | collective-permute-start | bytes 6291464 | tf_op jit(solution)/shard_map/ppermute | solution.py:68
  11.8 3.8 %collective-permute-start.1 = (s32[2,1,16]{2,1,0:T(1,128)S(1)}, s32[2,1,16]{2,1,0:T(1,128)S(1)}, u32[]{:S(2)}, u32[]{:S(2)}) collective-permute-start(s32[2,1,16]{2,1,0:T(1,128)S(1)} %pad_add_fusion.1), channel_id=1, source_target_pairs={{0,1},{1,0},{2,3},{3,2},{4,5},{5,4},{6,7},{7,6},{8,9},{9,8},{10,11... | collective-permute-start | bytes 392 | tf_op jit(solution)/shard_map/ppermute | solution.py:68
  16.2 1.3 copy-start.4
  27.4 1.6 %copy-start.3 = (bf16[512,2048]{1,0:T(8,128)(2,1)S(1)}, bf16[512,2048]{1,0:T(8,128)(2,1)}, u32[]{:S(2)}) copy-start(bf16[512,2048]{1,0:T(8,128)(2,1)} %refs_0_) | copy-start | bytes 6291460
  27.4 5.7 %copy-start.6 = (s32[64]{0:T(128)S(1)}, s32[64]{0:T(128)}, u32[]{:S(2)}) copy-start(s32[64]{0:T(128)} %param.12) | copy-start | bytes 772
  28.9 59.6 %collective-permute-start.4 = (bf16[512,2048]{1,0:T(8,128)(2,1)S(1)}, bf16[512,2048]{1,0:T(8,128)(2,1)}, u32[]{:S(2)}, u32[]{:S(2)}) collective-permute-start(bf16[512,2048]{1,0:T(8,128)(2,1)S(1)} %copy-done.3), channel_id=1, source_target_pairs={{0,2},{2,0},{1,3},{3,1},{4,6},{6,4},{5,7},{7,5},{8,10},{10,8},{9,1... | collective-permute-start | bytes 6291464 | tf_op jit(solution)/shard_map/ppermute | solution.py:68
  37.2 48.3 %all-to-all-start = ((bf16[4,3,64,512]{3,2,1,0:T(8,128)(2,1)}), bf16[4,3,64,512]{3,2,1,0:T(8,128)(2,1)}, u32[]{:S(2)}, u32[]{:S(2)}) async-start(bf16[4,3,64,512]{3,2,1,0:T(8,128)(2,1)} %bitcast.41), calls=%async_computation | async-start | bytes 1572864 | tf_op jit(solution)/shard_map/all_to_all | solution.py:144
  41.5 3.4 %copy-start.1 = (bf16[16,2048,128]{2,1,0:T(8,128)(2,1)S(1)}, bf16[16,2048,128]{2,1,0:T(8,128)(2,1)}, u32[]{:S(2)}) copy-start(bf16[16,2048,128]{2,1,0:T(8,128)(2,1)} %down.3) | copy-start | bytes 25165828
  44.9 1.6 %copy-start.5 = (bf16[512,2048]{1,0:T(8,128)(2,1)S(1)}, bf16[512,2048]{1,0:T(8,128)(2,1)}, u32[]{:S(2)}) copy-start(bf16[512,2048]{1,0:T(8,128)(2,1)} %copy-done.4) | copy-start | bytes 6291460
  47.9 4.7 %collective-permute-start.3 = (bf16[512,128]{1,0:T(8,128)(2,1)S(1)}, bf16[512,128]{1,0:T(8,128)(2,1)}, u32[]{:S(2)}, u32[]{:S(2)}) collective-permute-start(bf16[512,128]{1,0:T(8,128)(2,1)S(1)} %get-tuple-element.32), channel_id=1, source_target_pairs={{0,1},{1,0},{2,3},{3,2},{4,5},{5,4},{6,7},{7,6},{8,9},{9,8},{10,11... | collective-permute-start | bytes 393224 | tf_op jit(solution)/shard_map/ppermute | solution.py:68
  88.6 4.4 %collective-permute-start.5 = (bf16[512,2048]{1,0:T(8,128)(2,1)}, bf16[512,2048]{1,0:T(8,128)(2,1)S(1)}, u32[]{:S(2)}, u32[]{:S(2)}) collective-permute-start(bf16[512,2048]{1,0:T(8,128)(2,1)} %collective-permute-done.4.refs_0_), channel_id=1, source_target_pairs={{0,1},{1,0},{2,3},{3,2},{4,5},{5,4},{6,7},{7,6},{8,9},{9,8},{10,11... | collective-permute-start | bytes 6291464 | tf_op jit(solution)/shard_map/ppermute | solution.py:68
  92.9 3.4 %copy-start.2 = (bf16[16,2048,128]{2,1,0:T(8,128)(2,1)S(1)}, bf16[16,2048,128]{2,1,0:T(8,128)(2,1)}, u32[]{:S(2)}) copy-start(bf16[16,2048,128]{2,1,0:T(8,128)(2,1)} %down.3) | copy-start | bytes 25165828
  98.8 2.4 %collective-permute-start.6 = (bf16[512,128]{1,0:T(8,128)(2,1)S(1)}, bf16[512,128]{1,0:T(8,128)(2,1)S(1)}, u32[]{:S(2)}, u32[]{:S(2)}) collective-permute-start(bf16[512,128]{1,0:T(8,128)(2,1)S(1)} %get-tuple-element.41), channel_id=1, source_target_pairs={{0,1},{1,0},{2,3},{3,2},{4,5},{5,4},{6,7},{7,6},{8,9},{9,8},{10,11... | collective-permute-start | bytes 393224 | tf_op jit(solution)/shard_map/ppermute | solution.py:68
  101.1 17.6 %copy-start.7 = (bf16[32,64,512]{2,1,0:T(8,128)(2,1)S(1)}, bf16[32,64,512]{2,1,0:T(8,128)(2,1)}, u32[]{:S(2)}) copy-start(bf16[32,64,512]{2,1,0:T(8,128)(2,1)} %gather_fusion.8) | copy-start | bytes 6291460
  101.2 5.9 %collective-permute-start.7 = (bf16[512,128]{1,0:T(8,128)(2,1)S(1)}, bf16[512,128]{1,0:T(8,128)(2,1)}, u32[]{:S(2)}, u32[]{:S(2)}) collective-permute-start(bf16[512,128]{1,0:T(8,128)(2,1)S(1)} %add.166), channel_id=1, source_target_pairs={{0,2},{2,0},{1,3},{3,1},{4,6},{6,4},{5,7},{7,5},{8,10},{10,8},{9,1... | collective-permute-start | bytes 393224 | tf_op jit(solution)/shard_map/ppermute | solution.py:68
  103.0 15.7 %copy-start.8 = (bf16[512,512]{1,0:T(8,128)(2,1)S(1)}, bf16[512,512]{1,0:T(8,128)(2,1)}, u32[]{:S(2)}) copy-start(bf16[512,512]{1,0:T(8,128)(2,1)} %reduce-scatter.2.cloned.1.call-done) | copy-start | bytes 1572868
  108.3 5.8 %collective-permute-start.8 = (bf16[256,128]{1,0:T(8,128)(2,1)S(1)}, bf16[256,128]{1,0:T(8,128)(2,1)S(1)}, u32[]{:S(2)}, u32[]{:S(2)}) collective-permute-start(bf16[256,128]{1,0:T(8,128)(2,1)S(1)} %select_convert_fusion), channel_id=1, source_target_pairs={{0,8},{4,12},{8,0},{12,4},{1,9},{5,13},{9,1},{13,5},{2,10},{6,14},... | collective-permute-start | bytes 196616 | tf_op jit(solution)/shard_map/ppermute | solution.py:68
  114.2 4.3 %collective-permute-start.9 = (bf16[256,128]{1,0:T(8,128)(2,1)S(1)}, bf16[256,128]{1,0:T(8,128)(2,1)S(1)}, u32[]{:S(2)}, u32[]{:S(2)}) collective-permute-start(bf16[256,128]{1,0:T(8,128)(2,1)S(1)} %get-tuple-element.43), channel_id=1, source_target_pairs={{0,4},{4,0},{8,12},{12,8},{1,5},{5,1},{9,13},{13,9},{2,6},{6,2},{1... | collective-permute-start | bytes 196616 | tf_op jit(solution)/shard_map/ppermute | solution.py:209
  118.7 2.3 %copy-start.9 = (s32[4,32]{1,0:T(4,128)S(1)}, s32[4,32]{1,0:T(4,128)}, u32[]{:S(2)}) copy-start(s32[4,32]{1,0:T(4,128)} %param.15) | copy-start | bytes 1540
  119.4 10.8 %collective-permute-start.10 = (bf16[32,8192]{1,0:T(8,128)(2,1)S(1)}, bf16[32,8192]{1,0:T(8,128)(2,1)S(1)}, u32[]{:S(2)}, u32[]{:S(2)}) collective-permute-start(bf16[32,8192]{1,0:T(8,128)(2,1)S(1)} %bitcast.43), channel_id=1, source_target_pairs={{0,2},{2,0},{1,3},{3,1},{4,6},{6,4},{5,7},{7,5},{8,10},{10,8},{9,1... | collective-permute-start | bytes 1572872 | tf_op jit(solution)/shard_map/ppermute | solution.py:68
Sparse Core Ops, SparseCore 0:
  27.5 45.5 reduce-scatter.1

commit v4 on v3

--- a/solution.py
+++ b/solution.py
@@ -100,20 +100,20 @@
         [asked_steps] + [shifted(asked_steps, "st", turn) for turn in range(1, st_count)], axis=1
     )
 
-    travelled = {(0, 0): tokens}
-    for turn in range(1, st_count):
-        travelled[0, turn] = shifted(tokens, "st", turn)
-    for step in range(1, pd_count):
-        travelled[step, 0] = shifted(tokens, "pd", step)
-
-    tokens, asked_turns, near_other = lax.optimization_barrier(
-        (tokens, asked_turns, [travelled[0, turn] for turn in range(1, st_count)])
-    )
-    for turn in range(1, st_count):
-        travelled[0, turn] = near_other[turn - 1]
+    half_rows = token_rows // 2
+    far_steps = range(1, pd_count)
+    first_half = [shifted(tokens[:half_rows], "pd", step) for step in far_steps]
     base_part = jnp.dot(tokens, key_value_matrix, preferred_element_type=jnp.float32)
-    base_part, asked_turns = lax.optimization_barrier((base_part.astype(jnp.bfloat16), asked_turns))
-    base_sum = lax.psum_scatter(base_part, "tp", scatter_dimension=1, tiled=True)
+    base_part = base_part.astype(jnp.bfloat16)
+    near_rows = [tokens] + [shifted(tokens, "st", turn) for turn in range(1, st_count)]
+    near_rows, first_half, after_base, asked_turns = lax.optimization_barrier(
+        (near_rows, first_half, base_part, asked_turns)
+    )
+    base_sum = lax.psum_scatter(after_base, "tp", scatter_dimension=1, tiled=True)
+    second_half = [shifted(near_rows[0][half_rows:], "pd", step) for step in far_steps]
+    first_rows = [
+        [rows] + [shifted(rows, "st", turn) for turn in range(1, st_count)] for rows in first_half
+    ]
 
     by_pd = jnp.take(
         asked_turns, (pd_index - jnp.arange(pd_count)) % pd_count, axis=0, mode="clip"
@@ -141,9 +141,6 @@
     up_page_list = jnp.take(adapter_up_weight, asked_pages, axis=0, mode="clip").reshape(
         groups, slot_capacity, adapter_rank_value, column_range
     )
-    arrived_up = lax.all_to_all(
-        up_page_list, ("pd", "st"), split_axis=0, concat_axis=0, tiled=True
-    )
     own_holder = lax.dynamic_index_in_dim(holder, me, 0, keepdims=False)
     own_rank = lax.dynamic_index_in_dim(rank_in, me, 0, keepdims=False)
     own_ends = lax.dynamic_index_in_dim(ends, me, 0, keepdims=False)
@@ -151,13 +148,6 @@
         (own_ends[None, :] <= jnp.arange(page_count)[:, None]).astype(jnp.int32), axis=1
     )
     source_of_page = jnp.take(own_holder * slot_capacity + own_rank, request_of_page, mode="clip")
-    page_up_weight = jnp.take(
-        arrived_up.reshape(groups * slot_capacity, adapter_rank_value, column_range),
-        source_of_page,
-        axis=0,
-        mode="clip",
-    )
-
     def request_tables(step):
         source_group = jnp.stack(
             [
@@ -171,30 +161,56 @@
         ]
         return tables
 
-    def summed_products(tables, row_list):
-        products = down_products(row_list, *tables, adapter_down_weight)
-        chip_sum = products[0]
+    def summed_products(tables, row_list, bounds):
+        slots, firsts, lengths = tables
+        pieces = len(bounds) - 1
+        held_first, held_length = [], []
+        for low, high in zip(bounds[:-1], bounds[1:]):
+            first = jnp.clip(firsts, low, high)
+            held_first.append(first - low)
+            held_length.append(jnp.clip(firsts + lengths, low, high) - first)
+        products = down_products(
+            [piece for rows in row_list for piece in rows],
+            jnp.repeat(slots, pieces, axis=0),
+            jnp.stack(held_first, axis=1).reshape(-1, requests),
+            jnp.stack(held_length, axis=1).reshape(-1, requests),
+            adapter_down_weight,
+        )
+        by_turn = [
+            jnp.concatenate(products[turn * pieces : (turn + 1) * pieces], axis=0)
+            for turn in range(st_count)
+        ]
+        chip_sum = by_turn[0]
         for turn in range(1, st_count):
-            chip_sum = chip_sum + shifted(products[turn], "st", -turn)
+            chip_sum = chip_sum + shifted(by_turn[turn], "st", -turn)
         return chip_sum
 
-    near_rows = [travelled[0, turn] for turn in range(st_count)]
-    inner = summed_products(request_tables(0), near_rows).astype(jnp.float32)
-    far_tables = [request_tables(step) for step in range(1, pd_count)]
-    far_rows = [travelled[step, 0] for step in range(1, pd_count)]
-    inner, page_up_weight, base_sum, far_tables, far_rows = lax.optimization_barrier(
-        (inner, page_up_weight, base_sum, far_tables, far_rows)
-    )
-    for step in range(1, pd_count):
-        rows = far_rows[step - 1]
-        row_list = [rows] + [shifted(rows, "st", turn) for turn in range(1, st_count)]
-        returned = shifted(summed_products(far_tables[step - 1], row_list), "pd", -step)
-        inner = inner + returned
+    whole = token_rows // PAGE_TOKENS
+    inner = summed_products(request_tables(0), [[rows] for rows in near_rows], [0, whole])
+    inner = inner.astype(jnp.float32)
+    far_tables = [request_tables(step) for step in far_steps]
+    inner, up_page_list, base_sum, far_tables, first_rows, second_half = lax.optimization_barrier(
+        (inner, up_page_list, base_sum, far_tables, first_rows, second_half)
+    )
+    for step in far_steps:
+        rows = second_half[step - 1]
+        second_rows = [rows] + [shifted(rows, "st", turn) for turn in range(1, st_count)]
+        row_list = [list(halves) for halves in zip(first_rows[step - 1], second_rows)]
+        far_sum = summed_products(far_tables[step - 1], row_list, [0, whole // 2, whole])
+        inner = inner + shifted(far_sum, "pd", -step)
+    arrived_up = lax.all_to_all(
+        up_page_list, ("pd", "st"), split_axis=0, concat_axis=0, tiled=True
+    )
+    page_up_weight = jnp.take(
+        arrived_up.reshape(groups * slot_capacity, adapter_rank_value, column_range),
+        source_of_page,
+        axis=0,
+        mode="clip",
+    )
 
     tp_count = lax.axis_size("tp")
     half_tensor_parallel = tp_count // 2
     upper = lax.axis_index("tp") >= half_tensor_parallel
-    half_rows = token_rows // 2
 
     def packed(columns):
         return jnp.concatenate([columns[:half_rows], columns[half_rows:]], axis=1)

time: 139 us -> 141 us (1.014)
  waiting for transfers between devices: 61.5 us -> 68.8 us
  starting transfers between devices: 20.9 us -> 15.4 us
  Pallas kernels: 3.86 us -> 7.21 us
  local copies, waits for them, and re-layouts: 23.5 us -> 21.7 us
  other arithmetic: 3.99 us -> 2.25 us
    all_to_all x1, waiting for transfers between devices: 31.9 us -> 5.23 us  [on_device(): lax.all_to_all(up_page_list, ('pd', 'st'), split_axis=0, concat_axis=0, t...]
    ppermute x10 -> x12, waiting for transfers between devices: 26.6 us -> 47.2 us  [shifted(): lax.ppermute(value, axis, [(i, (i + step) % size) for i in range(size)])]
    reduce_scatter x1, waiting for transfers between devices: 0.01 us -> 16.3 us  [on_device(): lax.psum_scatter(after_base, 'tp', scatter_dimension=1, tiled=True)]
    unnamed x22 -> x16, local copies, waits for them, and re-layouts: 12.4 us -> 8.21 us
    ppermute x10 -> x12, starting transfers between devices: 15.4 us -> 11.8 us  [shifted(): lax.ppermute(value, axis, [(i, (i + step) % size) for i in range(size)])]
    slice x0 -> x2, local copies, waits for them, and re-layouts: none -> 3.5 us  [the longest x1 2.33 us: on_device(): first_half = [shifted(tokens[:half_rows], 'pd', step) for step in far_steps]]
    pallas_call x2, Pallas kernels: 3.86 us -> 7.21 us  [down_products(): pl.pallas_call(functools.partial(down_kernel, sources, requests), out_sha...]
    ppermute x1, waiting for transfers between devices: 2.98 us -> 0.01 us  [on_device(): mine = mine + lax.ppermute(mine.astype(jnp.bfloat16), 'tp', pairs)]
  transfers between devices with their start and end apart: 13 -> 15, of which waited for: 10 -> 10; matrix products, arithmetic and copies ran while one was open for 9% -> 17% of each run, Pallas kernels for 1% -> 2%
where the time goes in v4:
time: 141 us
  waiting for transfers between devices  68.8 us (49%)
  local copies, waits for them, and re-layouts  21.7 us (15%)
  starting transfers between devices  15.4 us (11%)
  between operations  13.7 us (10%)
  matrix products  11.7 us (8%)
  Pallas kernels  7.21 us (5%)
  other arithmetic  2.25 us (2%)
    ppermute x12, waiting for transfers between devices, shifted(): lax.ppermute(value, axis, [(i, (i + step) % size) for i in range(size)])  47.2 us
    reduce_scatter x1, waiting for transfers between devices, on_device(): lax.psum_scatter(after_base, 'tp', scatter_dimension=1, tiled=True)  16.3 us
    ppermute x12, starting transfers between devices, shifted(): lax.ppermute(value, axis, [(i, (i + step) % size) for i in range(size)])  11.8 us
    dot_general x1, matrix products, on_device(): jnp.dot(tokens, key_value_matrix, preferred_element_type=jnp.float32)  9.02 us
    unnamed x16, local copies, waits for them, and re-layouts  8.21 us
    pallas_call x2, Pallas kernels, down_products(): pl.pallas_call(functools.partial(down_kernel, sources, requests), out_sha...  7.21 us
    all_to_all x1, waiting for transfers between devices, on_device(): lax.all_to_all(up_page_list, ('pd', 'st'), split_axis=0, concat_axis=0, t...  5.23 us
    all_to_all x1, starting transfers between devices, on_device(): lax.all_to_all(up_page_list, ('pd', 'st'), split_axis=0, concat_axis=0, t...  3.5 us
  transfers between devices with their start and end apart: 15, of which 10 were waited for; matrix products, arithmetic and copies ran while one was open for 17% of the time, Pallas kernels for 2%

profile of v4, /device:TPU:0, one launch (start us, length us, event | category | flops | bytes accessed | tf_op | source)
XLA Modules:
  0.0 140.8 jit_solution(15597648706898758022)
XLA Ops:
  7.4 2.9 %collective-permute-start = (s32[1,16]{1,0:T(1,128)S(1)}, s32[1,16]{1,0:T(1,128)S(1)}, u32[]{:S(2)}, u32[]{:S(2)}) collective-permute-start(s32[1,16]{1,0:T(1,128)S(1)} %pad_add_fusion.4), channel_id=1, source_target_pairs={{0,2},{2,0},{1,3},{3,1},{4,6},{6,4},{5,7},{7,5},{8,10},{10,8},{9,1... | collective-permute-start | bytes 200 | tf_op jit(solution)/shard_map/ppermute | solution.py:68
  10.4 1.5 %collective-permute-done = s32[1,16]{1,0:T(1,128)S(1)} collective-permute-done((s32[1,16]{1,0:T(1,128)S(1)}, s32[1,16]{1,0:T(1,128)S(1)}, u32[]{:S(2)}, u32[]{:S(2)}) %collective-permute-start) | collective-permute-done | bytes 96 | tf_op jit(solution)/shard_map/ppermute | solution.py:68
  11.9 2.3 %slice.36 = bf16[256,2048]{1,0:T(8,128)(2,1)} slice(bf16[512,2048]{1,0:T(8,128)(2,1)} %refs_0_), slice={[0:256], [0:2048]} | slice | bytes 2097152 | tf_op jit(solution)/shard_map/slice | solution.py:105
  14.7 2.0 %collective-permute-start.2 = (bf16[256,2048]{1,0:T(8,128)(2,1)}, bf16[256,2048]{1,0:T(8,128)(2,1)}, u32[]{:S(2)}, u32[]{:S(2)}) collective-permute-start(bf16[256,2048]{1,0:T(8,128)(2,1)} %slice.36), channel_id=1, source_target_pairs={{0,2},{2,0},{1,3},{3,1},{4,6},{6,4},{5,7},{7,5},{8,10},{10,8},{9,1... | collective-permute-start | bytes 3145736 | tf_op jit(solution)/shard_map/ppermute | solution.py:68
  16.8 9.0 %convolution_convert_fusion = bf16[512,2048]{1,0:T(8,128)(2,1)} fusion(bf16[512,2048]{1,0:T(8,128)(2,1)S(1)} %copy-done.3, bf16[2048,2048]{1,0:T(8,128)(2,1)} %param.9), kind=kOutput, calls=%fused_computation.14 | convolution fusion | flops 4296015872 | bytes 12582912 | tf_op jit(solution)/shard_map/dot_general | solution.py:106
  25.8 14.7 %collective-permute-done.2.refs_0_ = bf16[256,2048]{1,0:T(8,128)(2,1)} collective-permute-done((bf16[256,2048]{1,0:T(8,128)(2,1)}, bf16[256,2048]{1,0:T(8,128)(2,1)}, u32[]{:S(2)}, u32[]{:S(2)}) %collective-permute-start.2) | collective-permute-done | bytes 1048608 | tf_op jit(solution)/shard_map/ppermute | solution.py:68
  44.7 1.7 %collective-permute-start.6 = (bf16[256,2048]{1,0:T(8,128)(2,1)}, bf16[256,2048]{1,0:T(8,128)(2,1)}, u32[]{:S(2)}, u32[]{:S(2)}) collective-permute-start(bf16[256,2048]{1,0:T(8,128)(2,1)} %slice.39), channel_id=1, source_target_pairs={{0,2},{2,0},{1,3},{3,1},{4,6},{6,4},{5,7},{7,5},{8,10},{10,8},{9,1... | collective-permute-start | bytes 3145736 | tf_op jit(solution)/shard_map/ppermute | solution.py:68
  47.7 3.6 %copy-done.1 = bf16[16,2048,128]{2,1,0:T(8,128)(2,1)S(1)} copy-done((bf16[16,2048,128]{2,1,0:T(8,128)(2,1)S(1)}, bf16[16,2048,128]{2,1,0:T(8,128)(2,1)}, u32[]{:S(2)}) %copy-start.1) | copy-done | bytes 8388632
  51.3 3.4 %down_products.2 = (bf16[512,128]{1,0:T(8,128)(2,1)S(1)}, bf16[512,128]{1,0:T(8,128)(2,1)S(1)}) custom-call(s32[2,8]{1,0:T(2,128)S(1)} %gather_fusion.3, s32[2,8]{1,0:T(2,128)S(1)} %get-tuple-element.73.starts, s32[2,8]{1,0:T(2,128)S(1)} %get-tuple-element.72.counts, bf16[16,2048,128]{2,1,0:T(8,128)(2,1)S(1)} %copy-done.1, bf16[512,2048]{1,0:T(8,128)(2,1)S(1)} %copy-done.3, ...), custom_call_target="tpu_custom_call" | custom-call | flops 536870912 | bytes 12845056 | tf_op jit(solution)/shard_map/down_products/pallas_call | solution.py:51
  57.4 1.5 %gather_fusion.6 = bf16[12,64,512]{2,1,0:T(8,128)(2,1)} fusion(bf16[16,64,512]{2,1,0:T(8,128)(2,1)S(1)} %copy-done, s32[1024]{0:T(1024)S(1)} %pad_clamp_fusion.3), kind=kCustom, calls=%fused_computation.6 | custom fusion | bytes 1572912 | tf_op jit(solution)/shard_map/jit(_take)/gather | solution.py:141
  58.9 10.8 %collective-permute-done.6.refs_1_ = bf16[256,2048]{1,0:T(8,128)(2,1)} collective-permute-done((bf16[256,2048]{1,0:T(8,128)(2,1)}, bf16[256,2048]{1,0:T(8,128)(2,1)}, u32[]{:S(2)}, u32[]{:S(2)}) %collective-permute-start.6) | collective-permute-done | bytes 1048608 | tf_op jit(solution)/shard_map/ppermute | solution.py:68
  69.7 16.3 %reduce-scatter.2.cloned.1.call-done = bf16[512,512]{1,0:T(8,128)(2,1)} async-done(((bf16[512,2048]{1,0:T(8,128)(2,1)}), bf16[512,512]{1,0:T(8,128)(2,1)}) %reduce-scatter.2.cloned.1.call-update) | async-done | bytes 524304 | tf_op jit(solution)/shard_map/reduce_scatter | solution.py:112
  86.1 2.8 %collective-permute-done.7.refs_3_ = bf16[256,2048]{1,0:T(8,128)(2,1)S(1)} collective-permute-done((bf16[256,2048]{1,0:T(8,128)(2,1)}, bf16[256,2048]{1,0:T(8,128)(2,1)S(1)}, u32[]{:S(2)}, u32[]{:S(2)}) %collective-permute-start.7) | collective-permute-done | bytes 1048608 | tf_op jit(solution)/shard_map/ppermute | solution.py:68
  88.9 3.4 %copy-done.2 = bf16[16,2048,128]{2,1,0:T(8,128)(2,1)S(1)} copy-done((bf16[16,2048,128]{2,1,0:T(8,128)(2,1)S(1)}, bf16[16,2048,128]{2,1,0:T(8,128)(2,1)}, u32[]{:S(2)}) %copy-start.2) | copy-done | bytes 8388632
  92.3 3.9 %down_products.3 = (bf16[256,128]{1,0:T(8,128)(2,1)S(1)}, bf16[256,128]{1,0:T(8,128)(2,1)S(1)}, bf16[256,128]{1,0:T(8,128)(2,1)S(1)}, bf16[256,128]{1,0:T(8,128)(2,1)S(1)}) custom-call(s32[4,8]{1,0:T(4,128)S(1)} %bitcast.54, s32[4,8]{1,0:T(4,128)S(1)} %bitcast.53, s32[4,8]{1,0:T(4,128)S(1)} %bitcast.52, bf16[16,2048,128]{2,1,0:T(8,128)(2,1)S(1)} %copy-done.2, ...), custom_call_target="tpu_custom_call" | custom-call | flops 536870912 | bytes 12845056 | tf_op jit(solution)/shard_map/down_products/pallas_call | solution.py:51
  96.3 1.3 collective-permute-done.8
  97.6 1.8 %collective-permute-start.9 = (bf16[512,128]{1,0:T(8,128)(2,1)S(1)}, bf16[512,128]{1,0:T(8,128)(2,1)S(1)}, u32[]{:S(2)}, u32[]{:S(2)}) collective-permute-start(bf16[512,128]{1,0:T(8,128)(2,1)S(1)} %maximum_add_fusion), channel_id=1, source_target_pairs={{0,2},{2,0},{1,3},{3,1},{4,6},{6,4},{5,7},{7,5},{8,10},{10,8},{9,1... | collective-permute-start | bytes 393224 | tf_op jit(solution)/shard_map/ppermute | solution.py:68
  99.5 3.5 %all-to-all-start = ((bf16[4,3,64,512]{3,2,1,0:T(8,128)(2,1)}), bf16[4,3,64,512]{3,2,1,0:T(8,128)(2,1)S(1)}, u32[]{:S(2)}, u32[]{:S(2)}) async-start(bf16[4,3,64,512]{3,2,1,0:T(8,128)(2,1)} %bitcast.56), calls=%async_computation.1 | async-start | bytes 1572864 | tf_op jit(solution)/shard_map/all_to_all | solution.py:201
  103.5 1.8 %collective-permute-start.10 = (bf16[256,128]{1,0:T(8,128)(2,1)S(1)}, bf16[256,128]{1,0:T(8,128)(2,1)S(1)}, u32[]{:S(2)}, u32[]{:S(2)}) collective-permute-start(bf16[256,128]{1,0:T(8,128)(2,1)S(1)} %select_convert_fusion), channel_id=1, source_target_pairs={{0,8},{4,12},{8,0},{12,4},{1,9},{5,13},{9,1},{13,5},{2,10},{6,14},... | collective-permute-start | bytes 196616 | tf_op jit(solution)/shard_map/ppermute | solution.py:68
  106.0 3.1 %collective-permute-done.10 = bf16[256,128]{1,0:T(8,128)(2,1)S(1)} collective-permute-done((bf16[256,128]{1,0:T(8,128)(2,1)S(1)}, bf16[256,128]{1,0:T(8,128)(2,1)S(1)}, u32[]{:S(2)}, u32[]{:S(2)}) %collective-permute-start.10) | collective-permute-done | bytes 65568 | tf_op jit(solution)/shard_map/ppermute | solution.py:68
  109.4 5.2 %all-to-all-done = bf16[4,3,64,512]{3,2,1,0:T(8,128)(2,1)S(1)} async-done(((bf16[4,3,64,512]{3,2,1,0:T(8,128)(2,1)}), bf16[4,3,64,512]{3,2,1,0:T(8,128)(2,1)S(1)}, u32[]{:S(2)}, u32[]{:S(2)}) %all-to-all-start) | async-done | bytes 786464 | tf_op jit(solution)/shard_map/all_to_all | solution.py:201
  114.6 2.0 %gather_fusion.11 = bf16[32,64,512]{2,1,0:T(8,128)(2,1)} fusion(bf16[12,64,512]{2,1,0:T(8,128)(2,1)S(1)} %bitcast.55, s32[1024]{0:T(1024)S(1)} %pad_clamp_fusion), kind=kCustom, calls=%fused_computation.11 | custom fusion | bytes 4194432 | tf_op jit(solution)/shard_map/jit(_take)/gather | solution.py:204
  116.8 2.0 %fusion.1 = bf16[32,16,512]{2,1,0:T(8,128)(2,1)S(1)} fusion(bf16[32,16,512]{2,1,0:T(8,128)(2,1)S(1)} %bitcast.61, bf16[32,16,64]{2,1,0:T(8,128)(2,1)S(1)} %bitcast.62, bf16[32,64,512]{2,1,0:T(8,128)(2,1)} %gather_fusion.11), kind=kOutput, calls=%fused_computation.17 | convolution fusion | flops 34603008 | bytes 3211264 | tf_op jit(solution)/shard_map/ueo,uox->uex/dot_general | solution.py:231
  119.9 12.7 %collective-permute-done.12 = bf16[32,8192]{1,0:T(8,128)(2,1)S(1)} collective-permute-done((bf16[32,8192]{1,0:T(8,128)(2,1)S(1)}, bf16[32,8192]{1,0:T(8,128)(2,1)S(1)}, u32[]{:S(2)}, u32[]{:S(2)}) %collective-permute-start.12) | collective-permute-done | bytes 524320 | tf_op jit(solution)/shard_map/ppermute | solution.py:68
  (91 shorter events, 13.7 us)
Async XLA Ops:
  6.5 50.8 %copy-start = (bf16[16,64,512]{2,1,0:T(8,128)(2,1)S(1)}, bf16[16,64,512]{2,1,0:T(8,128)(2,1)}, u32[]{:S(2)}) copy-start(bf16[16,64,512]{2,1,0:T(8,128)(2,1)} %param.11) | copy-start | bytes 3145732
  6.5 10.2 %copy-start.3 = (bf16[512,2048]{1,0:T(8,128)(2,1)S(1)}, bf16[512,2048]{1,0:T(8,128)(2,1)}, u32[]{:S(2)}) copy-start(bf16[512,2048]{1,0:T(8,128)(2,1)} %refs_0_) | copy-start | bytes 6291460
  6.5 79.5 %reduce-scatter.2.cloned.1.call-start = ((), (), s32[]{:S(2)}) async-start(), calls=%async_computation.2 | async-start | bytes 2621440 | tf_op jit(solution)/shard_map/reduce_scatter | solution.py:112
  7.4 4.5 %collective-permute-start = (s32[1,16]{1,0:T(1,128)S(1)}, s32[1,16]{1,0:T(1,128)S(1)}, u32[]{:S(2)}, u32[]{:S(2)}) collective-permute-start(s32[1,16]{1,0:T(1,128)S(1)} %pad_add_fusion.4), channel_id=1, source_target_pairs={{0,2},{2,0},{1,3},{3,1},{4,6},{6,4},{5,7},{7,5},{8,10},{10,8},{9,1... | collective-permute-start | bytes 200 | tf_op jit(solution)/shard_map/ppermute | solution.py:68
  11.9 28.6 %collective-permute-start.1 = (bf16[512,2048]{1,0:T(8,128)(2,1)}, bf16[512,2048]{1,0:T(8,128)(2,1)}, u32[]{:S(2)}, u32[]{:S(2)}) collective-permute-start(bf16[512,2048]{1,0:T(8,128)(2,1)} %refs_0_), channel_id=1, source_target_pairs={{0,1},{1,0},{2,3},{3,2},{4,5},{5,4},{6,7},{7,6},{8,9},{9,8},{10,11... | collective-permute-start | bytes 6291464 | tf_op jit(solution)/shard_map/ppermute | solution.py:68
  14.2 11.6 %collective-permute-start.3 = (s32[2,1,16]{2,1,0:T(1,128)S(1)}, s32[2,1,16]{2,1,0:T(1,128)S(1)}, u32[]{:S(2)}, u32[]{:S(2)}) collective-permute-start(s32[2,1,16]{2,1,0:T(1,128)S(1)} %pad_add_fusion.3), channel_id=1, source_target_pairs={{0,1},{1,0},{2,3},{3,2},{4,5},{5,4},{6,7},{7,6},{8,9},{9,8},{10,11... | collective-permute-start | bytes 392 | tf_op jit(solution)/shard_map/ppermute | solution.py:68
  14.7 25.7 %collective-permute-start.2 = (bf16[256,2048]{1,0:T(8,128)(2,1)}, bf16[256,2048]{1,0:T(8,128)(2,1)}, u32[]{:S(2)}, u32[]{:S(2)}) collective-permute-start(bf16[256,2048]{1,0:T(8,128)(2,1)} %slice.36), channel_id=1, source_target_pairs={{0,2},{2,0},{1,3},{3,1},{4,6},{6,4},{5,7},{7,5},{8,10},{10,8},{9,1... | collective-permute-start | bytes 3145736 | tf_op jit(solution)/shard_map/ppermute | solution.py:68
  25.8 17.0 %copy-start.4 = (s32[64]{0:T(128)S(1)}, s32[64]{0:T(128)}, u32[]{:S(2)}) copy-start(s32[64]{0:T(128)} %param.12) | copy-start | bytes 772
  44.7 24.9 %collective-permute-start.6 = (bf16[256,2048]{1,0:T(8,128)(2,1)}, bf16[256,2048]{1,0:T(8,128)(2,1)}, u32[]{:S(2)}, u32[]{:S(2)}) collective-permute-start(bf16[256,2048]{1,0:T(8,128)(2,1)} %slice.39), channel_id=1, source_target_pairs={{0,2},{2,0},{1,3},{3,1},{4,6},{6,4},{5,7},{7,5},{8,10},{10,8},{9,1... | collective-permute-start | bytes 3145736 | tf_op jit(solution)/shard_map/ppermute | solution.py:68
  46.5 23.2 %collective-permute-start.5 = (bf16[256,2048]{1,0:T(8,128)(2,1)}, bf16[256,2048]{1,0:T(8,128)(2,1)}, u32[]{:S(2)}, u32[]{:S(2)}) collective-permute-start(bf16[256,2048]{1,0:T(8,128)(2,1)} %collective-permute-done.2.refs_0_), channel_id=1, source_target_pairs={{0,1},{1,0},{2,3},{3,2},{4,5},{5,4},{6,7},{7,6},{8,9},{9,8},{10,11... | collective-permute-start | bytes 3145736 | tf_op jit(solution)/shard_map/ppermute | solution.py:68
  47.7 3.6 %copy-start.1 = (bf16[16,2048,128]{2,1,0:T(8,128)(2,1)S(1)}, bf16[16,2048,128]{2,1,0:T(8,128)(2,1)}, u32[]{:S(2)}) copy-start(bf16[16,2048,128]{2,1,0:T(8,128)(2,1)} %down.3) | copy-start | bytes 25165828
  54.6 4.3 %collective-permute-start.4 = (bf16[512,128]{1,0:T(8,128)(2,1)S(1)}, bf16[512,128]{1,0:T(8,128)(2,1)S(1)}, u32[]{:S(2)}, u32[]{:S(2)}) collective-permute-start(bf16[512,128]{1,0:T(8,128)(2,1)S(1)} %get-tuple-element.35), channel_id=1, source_target_pairs={{0,1},{1,0},{2,3},{3,2},{4,5},{5,4},{6,7},{7,6},{8,9},{9,8},{10,11... | collective-permute-start | bytes 393224 | tf_op jit(solution)/shard_map/ppermute | solution.py:68
  86.0 2.9 %collective-permute-start.7 = (bf16[256,2048]{1,0:T(8,128)(2,1)}, bf16[256,2048]{1,0:T(8,128)(2,1)S(1)}, u32[]{:S(2)}, u32[]{:S(2)}) collective-permute-start(bf16[256,2048]{1,0:T(8,128)(2,1)} %collective-permute-done.6.refs_1_), channel_id=1, source_target_pairs={{0,1},{1,0},{2,3},{3,2},{4,5},{5,4},{6,7},{7,6},{8,9},{9,8},{10,11... | collective-permute-start | bytes 3145736 | tf_op jit(solution)/shard_map/ppermute | solution.py:68
  88.9 3.4 %copy-start.2 = (bf16[16,2048,128]{2,1,0:T(8,128)(2,1)S(1)}, bf16[16,2048,128]{2,1,0:T(8,128)(2,1)}, u32[]{:S(2)}) copy-start(bf16[16,2048,128]{2,1,0:T(8,128)(2,1)} %down.3) | copy-start | bytes 25165828
  96.2 1.4 %collective-permute-start.8 = (bf16[512,128]{1,0:T(8,128)(2,1)S(1)}, bf16[512,128]{1,0:T(8,128)(2,1)S(1)}, u32[]{:S(2)}, u32[]{:S(2)}) collective-permute-start(bf16[512,128]{1,0:T(8,128)(2,1)S(1)} %pad_maximum_fusion), channel_id=1, source_target_pairs={{0,1},{1,0},{2,3},{3,2},{4,5},{5,4},{6,7},{7,6},{8,9},{9,8},{10,11... | collective-permute-start | bytes 393224 | tf_op jit(solution)/shard_map/ppermute | solution.py:68
  97.6 5.6 %collective-permute-start.9 = (bf16[512,128]{1,0:T(8,128)(2,1)S(1)}, bf16[512,128]{1,0:T(8,128)(2,1)S(1)}, u32[]{:S(2)}, u32[]{:S(2)}) collective-permute-start(bf16[512,128]{1,0:T(8,128)(2,1)S(1)} %maximum_add_fusion), channel_id=1, source_target_pairs={{0,2},{2,0},{1,3},{3,1},{4,6},{6,4},{5,7},{7,5},{8,10},{10,8},{9,1... | collective-permute-start | bytes 393224 | tf_op jit(solution)/shard_map/ppermute | solution.py:68
  99.5 15.1 %all-to-all-start = ((bf16[4,3,64,512]{3,2,1,0:T(8,128)(2,1)}), bf16[4,3,64,512]{3,2,1,0:T(8,128)(2,1)S(1)}, u32[]{:S(2)}, u32[]{:S(2)}) async-start(bf16[4,3,64,512]{3,2,1,0:T(8,128)(2,1)} %bitcast.56), calls=%async_computation.1 | async-start | bytes 1572864 | tf_op jit(solution)/shard_map/all_to_all | solution.py:201
  103.5 5.7 %collective-permute-start.10 = (bf16[256,128]{1,0:T(8,128)(2,1)S(1)}, bf16[256,128]{1,0:T(8,128)(2,1)S(1)}, u32[]{:S(2)}, u32[]{:S(2)}) collective-permute-start(bf16[256,128]{1,0:T(8,128)(2,1)S(1)} %select_convert_fusion), channel_id=1, source_target_pairs={{0,8},{4,12},{8,0},{12,4},{1,9},{5,13},{9,1},{13,5},{2,10},{6,14},... | collective-permute-start | bytes 196616 | tf_op jit(solution)/shard_map/ppermute | solution.py:68
  109.3 7.3 %collective-permute-start.11 = (bf16[256,128]{1,0:T(8,128)(2,1)S(1)}, bf16[256,128]{1,0:T(8,128)(2,1)S(1)}, u32[]{:S(2)}, u32[]{:S(2)}) collective-permute-start(bf16[256,128]{1,0:T(8,128)(2,1)S(1)} %get-tuple-element.51), channel_id=1, source_target_pairs={{0,4},{4,0},{8,12},{12,8},{1,5},{5,1},{9,13},{13,9},{2,6},{6,2},{1... | collective-permute-start | bytes 196616 | tf_op jit(solution)/shard_map/ppermute | solution.py:225
  114.6 2.2 %copy-start.5 = (bf16[512,512]{1,0:T(8,128)(2,1)S(1)}, bf16[512,512]{1,0:T(8,128)(2,1)}, u32[]{:S(2)}) copy-start(bf16[512,512]{1,0:T(8,128)(2,1)} %reduce-scatter.2.cloned.1.call-done) | copy-start | bytes 1572868
  116.8 2.7 %copy-start.6 = (s32[4,32]{1,0:T(4,128)S(1)}, s32[4,32]{1,0:T(4,128)}, u32[]{:S(2)}) copy-start(s32[4,32]{1,0:T(4,128)} %param.15) | copy-start | bytes 1540
  119.1 13.5 %collective-permute-start.12 = (bf16[32,8192]{1,0:T(8,128)(2,1)S(1)}, bf16[32,8192]{1,0:T(8,128)(2,1)S(1)}, u32[]{:S(2)}, u32[]{:S(2)}) collective-permute-start(bf16[32,8192]{1,0:T(8,128)(2,1)S(1)} %bitcast.58), channel_id=1, source_target_pairs={{0,2},{2,0},{1,3},{3,1},{4,6},{6,4},{5,7},{7,5},{8,10},{10,8},{9,1... | collective-permute-start | bytes 1572872 | tf_op jit(solution)/shard_map/ppermute | solution.py:68
Sparse Core Ops, SparseCore 0:
  40.6 45.3 reduce-scatter.1

commit v5 on v4

--- a/solution.py
+++ b/solution.py
@@ -16,9 +16,10 @@
 
 def down_kernel(sources, requests, slots, starts, counts, down, *refs):
     rows, outs = refs[:sources], refs[sources:]
-    page_count = rows[0].shape[0] // PAGE_TOKENS
+    assert min(piece.shape[0] for piece in rows) >= CHUNK_PAGES * PAGE_TOKENS
     chunk_rows = CHUNK_PAGES * PAGE_TOKENS
     for source in range(sources):
+        page_count = rows[source].shape[0] // PAGE_TOKENS
         outs[source][...] = jnp.zeros_like(outs[source])
 
         @pl.loop(0, requests)
@@ -44,19 +45,21 @@
 
 def down_products(row_list, slots, starts, counts, down):
     sources, requests = slots.shape
-    token_rows, width = row_list[0].shape
-    rank = down.shape[2]
+    total_rows = sum(rows.shape[0] for rows in row_list)
+    width, rank = down.shape[1:]
     in_vmem = pl.BlockSpec(memory_space=pltpu.VMEM)
     in_smem = pl.BlockSpec(memory_space=pltpu.SMEM)
     return pl.pallas_call(
         functools.partial(down_kernel, sources, requests),
-        out_shape=[jax.ShapeDtypeStruct((token_rows, rank), jnp.bfloat16)] * sources,
+        out_shape=[
+            jax.ShapeDtypeStruct((rows.shape[0], rank), jnp.bfloat16) for rows in row_list
+        ],
         in_specs=[in_smem] * 3 + [in_vmem] * (1 + sources),
         out_specs=[in_vmem] * sources,
         compiler_params=pltpu.CompilerParams(vmem_limit_bytes=40 * 1024 * 1024),
         cost_estimate=pl.CostEstimate(
-            flops=2 * sources * token_rows * width * rank,
-            bytes_accessed=2 * (down.size + sources * token_rows * (width + rank)),
+            flops=2 * total_rows * width * rank,
+            bytes_accessed=2 * (down.size + total_rows * (width + rank)),
             transcendentals=0,
         ),
         name="down_products",
@@ -101,18 +104,19 @@
     )
 
     half_rows = token_rows // 2
+    first_count = token_rows // 4
     far_steps = range(1, pd_count)
-    first_half = [shifted(tokens[:half_rows], "pd", step) for step in far_steps]
+    first_piece = [shifted(tokens[:first_count], "pd", step) for step in far_steps]
     base_part = jnp.dot(tokens, key_value_matrix, preferred_element_type=jnp.float32)
     base_part = base_part.astype(jnp.bfloat16)
     near_rows = [tokens] + [shifted(tokens, "st", turn) for turn in range(1, st_count)]
-    near_rows, first_half, after_base, asked_turns = lax.optimization_barrier(
-        (near_rows, first_half, base_part, asked_turns)
+    near_rows, first_piece, after_base, asked_turns, rest = lax.optimization_barrier(
+        (near_rows, first_piece, base_part, asked_turns, tokens[first_count:])
     )
     base_sum = lax.psum_scatter(after_base, "tp", scatter_dimension=1, tiled=True)
-    second_half = [shifted(near_rows[0][half_rows:], "pd", step) for step in far_steps]
+    second_piece = [shifted(rest, "pd", step) for step in far_steps]
     first_rows = [
-        [rows] + [shifted(rows, "st", turn) for turn in range(1, st_count)] for rows in first_half
+        [rows] + [shifted(rows, "st", turn) for turn in range(1, st_count)] for rows in first_piece
     ]
 
     by_pd = jnp.take(
@@ -189,15 +193,19 @@
     inner = summed_products(request_tables(0), [[rows] for rows in near_rows], [0, whole])
     inner = inner.astype(jnp.float32)
     far_tables = [request_tables(step) for step in far_steps]
-    inner, up_page_list, base_sum, far_tables, first_rows, second_half = lax.optimization_barrier(
-        (inner, up_page_list, base_sum, far_tables, first_rows, second_half)
-    )
+    inner, up_page_list, base_sum, far_tables, first_rows, second_piece = lax.optimization_barrier(
+        (inner, up_page_list, base_sum, far_tables, first_rows, second_piece)
+    )
+    far_sums = []
     for step in far_steps:
-        rows = second_half[step - 1]
+        rows = second_piece[step - 1]
         second_rows = [rows] + [shifted(rows, "st", turn) for turn in range(1, st_count)]
-        row_list = [list(halves) for halves in zip(first_rows[step - 1], second_rows)]
-        far_sum = summed_products(far_tables[step - 1], row_list, [0, whole // 2, whole])
-        inner = inner + shifted(far_sum, "pd", -step)
+        row_list = [list(pieces) for pieces in zip(first_rows[step - 1], second_rows)]
+        far_sums.append(
+            summed_products(
+                far_tables[step - 1], row_list, [0, first_count // PAGE_TOKENS, whole]
+            )
+        )
     arrived_up = lax.all_to_all(
         up_page_list, ("pd", "st"), split_axis=0, concat_axis=0, tiled=True
     )
@@ -207,6 +215,9 @@
         axis=0,
         mode="clip",
     )
+    far_sums, page_up_weight = lax.optimization_barrier((far_sums, page_up_weight))
+    for step in far_steps:
+        inner = inner + shifted(far_sums[step - 1], "pd", -step)
 
     tp_count = lax.axis_size("tp")
     half_tensor_parallel = tp_count // 2

time: 141 us -> 129 us (0.915)
  waiting for transfers between devices: 68.8 us -> 53.9 us
  other arithmetic: 2.25 us -> 5.1 us
    ppermute x12, waiting for transfers between devices: 47.2 us -> 38.6 us  [shifted(): lax.ppermute(value, axis, [(i, (i + step) % size) for i in range(size)])]
    reduce_scatter x1, waiting for transfers between devices: 16.3 us -> 8.72 us  [on_device(): lax.psum_scatter(after_base, 'tp', scatter_dimension=1, tiled=True)]
    ppermute x1, waiting for transfers between devices: 0.01 us -> 4.25 us  [on_device(): mine = mine + lax.ppermute(mine.astype(jnp.bfloat16), 'tp', pairs)]
    all_to_all x1, waiting for transfers between devices: 5.23 us -> 2.38 us  [on_device(): lax.all_to_all(up_page_list, ('pd', 'st'), split_axis=0, concat_axis=0, t...]
    dot_general x1, matrix products: 1.99 us -> 0.4 us  [on_device(): jnp.einsum('ueo,uox->uex', adapter_halfway, page_up_weight, preferred_ele...]
    add x1, other arithmetic: 0.04 us -> 1.6 us  [summed_products(): chip_sum = chip_sum + shifted(by_turn[turn], 'st', -turn)]
  transfers between devices with their start and end apart: 15 -> 15, of which waited for: 10 -> 9; matrix products, arithmetic and copies ran while one was open for 17% -> 21% of each run, Pallas kernels for 2% -> 5%
where the time goes in v5:
time: 129 us; the launch traced here: 128 us
  waiting for transfers between devices  53.9 us (42%)
  local copies, waits for them, and re-layouts  22.5 us (17%)
  starting transfers between devices  14.9 us (12%)
  between operations  13.7 us (11%)
  matrix products  11 us (9%)
  Pallas kernels  6.98 us (5%)
  other arithmetic  5.1 us (4%)
    ppermute x12, waiting for transfers between devices, shifted(): lax.ppermute(value, axis, [(i, (i + step) % size) for i in range(size)])  38.6 us
    ppermute x12, starting transfers between devices, shifted(): lax.ppermute(value, axis, [(i, (i + step) % size) for i in range(size)])  10.7 us
    dot_general x1, matrix products, on_device(): jnp.dot(tokens, key_value_matrix, preferred_element_type=jnp.float32)  9.95 us
    reduce_scatter x1, waiting for transfers between devices, on_device(): lax.psum_scatter(after_base, 'tp', scatter_dimension=1, tiled=True)  8.72 us
    unnamed x16, local copies, waits for them, and re-layouts  8.43 us
    pallas_call x2, Pallas kernels, down_products(): pl.pallas_call(functools.partial(down_kernel, sources, requests), out_sha...  6.98 us
    gather x6, local copies, waits for them, and re-layouts, request_tables(): jnp.take(table, source_group, axis=0, mode='clip')  4.49 us
    ppermute x1, waiting for transfers between devices, on_device(): mine = mine + lax.ppermute(mine.astype(jnp.bfloat16), 'tp', pairs)  4.25 us
  transfers between devices with their start and end apart: 15, of which 9 were waited for; matrix products, arithmetic and copies ran while one was open for 21% of the time, Pallas kernels for 5%

profile of v5, /device:TPU:0, one launch (start us, length us, event | category | flops | bytes accessed | tf_op | source)
XLA Modules:
  0.0 128.3 jit_solution(7536796232396683169)
XLA Ops:
  7.4 2.9 %collective-permute-start = (s32[1,16]{1,0:T(1,128)S(1)}, s32[1,16]{1,0:T(1,128)S(1)}, u32[]{:S(2)}, u32[]{:S(2)}) collective-permute-start(s32[1,16]{1,0:T(1,128)S(1)} %pad_add_fusion.4), channel_id=1, source_target_pairs={{0,2},{2,0},{1,3},{3,1},{4,6},{6,4},{5,7},{7,5},{8,10},{10,8},{9,1... | collective-permute-start | bytes 200 | tf_op jit(solution)/shard_map/ppermute | solution.py:71
  10.3 1.5 %collective-permute-done = s32[1,16]{1,0:T(1,128)S(1)} collective-permute-done((s32[1,16]{1,0:T(1,128)S(1)}, s32[1,16]{1,0:T(1,128)S(1)}, u32[]{:S(2)}, u32[]{:S(2)}) %collective-permute-start) | collective-permute-done | bytes 96 | tf_op jit(solution)/shard_map/ppermute | solution.py:71
  11.8 1.9 %slice.36 = bf16[128,2048]{1,0:T(8,128)(2,1)} slice(bf16[512,2048]{1,0:T(8,128)(2,1)} %refs_0_), slice={[0:128], [0:2048]} | slice | bytes 1048576 | tf_op jit(solution)/shard_map/slice | solution.py:109
  13.7 2.0 %collective-permute-start.2 = (bf16[128,2048]{1,0:T(8,128)(2,1)}, bf16[128,2048]{1,0:T(8,128)(2,1)}, u32[]{:S(2)}, u32[]{:S(2)}) collective-permute-start(bf16[128,2048]{1,0:T(8,128)(2,1)} %slice.36), channel_id=1, source_target_pairs={{0,2},{2,0},{1,3},{3,1},{4,6},{6,4},{5,7},{7,5},{8,10},{10,8},{9,1... | collective-permute-start | bytes 1572872 | tf_op jit(solution)/shard_map/ppermute | solution.py:71
  16.0 10.0 %convolution_convert_fusion = bf16[512,2048]{1,0:T(8,128)(2,1)} fusion(bf16[512,2048]{1,0:T(8,128)(2,1)} %refs_0_, bf16[2048,2048]{1,0:T(8,128)(2,1)} %param.9), kind=kOutput, calls=%fused_computation.14 | convolution fusion | flops 4296015872 | bytes 12582912 | tf_op jit(solution)/shard_map/dot_general | solution.py:110
  25.9 1.3 %slice.37 = bf16[384,2048]{1,0:T(8,128)(2,1)} slice(bf16[512,2048]{1,0:T(8,128)(2,1)S(1)} %copy-done.3), slice={[128:512], [0:2048]} | slice | bytes 3145728 | tf_op jit(solution)/shard_map/slice | solution.py:114
  27.2 1.4 %collective-permute-done.2.refs_0_ = bf16[128,2048]{1,0:T(8,128)(2,1)} collective-permute-done((bf16[128,2048]{1,0:T(8,128)(2,1)}, bf16[128,2048]{1,0:T(8,128)(2,1)}, u32[]{:S(2)}, u32[]{:S(2)}) %collective-permute-start.2) | collective-permute-done | bytes 524320 | tf_op jit(solution)/shard_map/ppermute | solution.py:71
  28.9 1.8 %collective-permute-start.6 = (bf16[384,2048]{1,0:T(8,128)(2,1)}, bf16[384,2048]{1,0:T(8,128)(2,1)}, u32[]{:S(2)}, u32[]{:S(2)}) collective-permute-start(bf16[384,2048]{1,0:T(8,128)(2,1)} %slice.37), channel_id=1, source_target_pairs={{0,2},{2,0},{1,3},{3,1},{4,6},{6,4},{5,7},{7,5},{8,10},{10,8},{9,1... | collective-permute-start | bytes 4718600 | tf_op jit(solution)/shard_map/ppermute | solution.py:71
  34.8 3.8 %copy-done.1 = bf16[16,2048,128]{2,1,0:T(8,128)(2,1)S(1)} copy-done((bf16[16,2048,128]{2,1,0:T(8,128)(2,1)S(1)}, bf16[16,2048,128]{2,1,0:T(8,128)(2,1)}, u32[]{:S(2)}) %copy-start.1) | copy-done | bytes 8388632
  38.5 3.4 %down_products.2 = (bf16[512,128]{1,0:T(8,128)(2,1)S(1)}, bf16[512,128]{1,0:T(8,128)(2,1)S(1)}) custom-call(s32[2,8]{1,0:T(2,128)S(1)} %gather_fusion.3, s32[2,8]{1,0:T(2,128)S(1)} %get-tuple-element.79.starts, s32[2,8]{1,0:T(2,128)S(1)} %get-tuple-element.78.counts, bf16[16,2048,128]{2,1,0:T(8,128)(2,1)S(1)} %copy-done.1, bf16[512,2048]{1,0:T(8,128)(2,1)S(1)} %copy-done.3, ...), custom_call_target="tpu_custom_call" | custom-call | flops 536870912 | bytes 12845056 | tf_op jit(solution)/shard_map/down_products/pallas_call | solution.py:52
  45.9 1.5 %gather_fusion.6 = bf16[12,64,512]{2,1,0:T(8,128)(2,1)} fusion(bf16[16,64,512]{2,1,0:T(8,128)(2,1)S(1)} %copy-done, s32[1024]{0:T(1024)S(1)} %pad_clamp_fusion.3), kind=kCustom, calls=%fused_computation.6 | custom fusion | bytes 1572912 | tf_op jit(solution)/shard_map/jit(_take)/gather | solution.py:145
  47.4 18.1 %collective-permute-done.6.refs_1_ = bf16[384,2048]{1,0:T(8,128)(2,1)} collective-permute-done((bf16[384,2048]{1,0:T(8,128)(2,1)}, bf16[384,2048]{1,0:T(8,128)(2,1)}, u32[]{:S(2)}, u32[]{:S(2)}) %collective-permute-start.6) | collective-permute-done | bytes 1572896 | tf_op jit(solution)/shard_map/ppermute | solution.py:71
  65.5 8.7 %reduce-scatter.2.cloned.1.call-done = bf16[512,512]{1,0:T(8,128)(2,1)} async-done(((bf16[512,2048]{1,0:T(8,128)(2,1)}), bf16[512,512]{1,0:T(8,128)(2,1)}) %reduce-scatter.2.cloned.1.call-update) | async-done | bytes 524304 | tf_op jit(solution)/shard_map/reduce_scatter | solution.py:116
  74.3 4.2 %all-to-all-start = ((bf16[4,3,64,512]{3,2,1,0:T(8,128)(2,1)}), bf16[4,3,64,512]{3,2,1,0:T(8,128)(2,1)}, u32[]{:S(2)}, u32[]{:S(2)}) async-start(bf16[4,3,64,512]{3,2,1,0:T(8,128)(2,1)} %bitcast.55), calls=%async_computation.1 | async-start | bytes 1572864 | tf_op jit(solution)/shard_map/all_to_all | solution.py:209
  79.3 3.4 %copy-done.2 = bf16[16,2048,128]{2,1,0:T(8,128)(2,1)S(1)} copy-done((bf16[16,2048,128]{2,1,0:T(8,128)(2,1)S(1)}, bf16[16,2048,128]{2,1,0:T(8,128)(2,1)}, u32[]{:S(2)}) %copy-start.2) | copy-done | bytes 8388632
  82.6 3.6 %down_products.3 = (bf16[128,128]{1,0:T(8,128)(2,1)S(1)}, bf16[384,128]{1,0:T(8,128)(2,1)S(1)}, bf16[128,128]{1,0:T(8,128)(2,1)S(1)}, bf16[384,128]{1,0:T(8,128)(2,1)S(1)}) custom-call(s32[4,8]{1,0:T(4,128)S(1)} %bitcast.54, s32[4,8]{1,0:T(4,128)S(1)} %bitcast.52, s32[4,8]{1,0:T(4,128)S(1)} %bitcast.53, bf16[16,2048,128]{2,1,0:T(8,128)(2,1)S(1)} %copy-done.2, ...), custom_call_target="tpu_custom_call" | custom-call | flops 536870912 | bytes 12845056 | tf_op jit(solution)/shard_map/down_products/pallas_call | solution.py:52
  87.8 2.4 %all-to-all-done = bf16[4,3,64,512]{3,2,1,0:T(8,128)(2,1)} async-done(((bf16[4,3,64,512]{3,2,1,0:T(8,128)(2,1)}), bf16[4,3,64,512]{3,2,1,0:T(8,128)(2,1)}, u32[]{:S(2)}, u32[]{:S(2)}) %all-to-all-start) | async-done | bytes 786464 | tf_op jit(solution)/shard_map/all_to_all | solution.py:209
  90.2 1.8 %gather_fusion.11 = bf16[32,64,512]{2,1,0:T(8,128)(2,1)S(1)} fusion(bf16[12,64,512]{2,1,0:T(8,128)(2,1)} %bitcast.24, s32[1024]{0:T(1024)S(1)} %pad_clamp_fusion), kind=kCustom, calls=%fused_computation.11 | custom fusion | bytes 4194432 | tf_op jit(solution)/shard_map/jit(_take)/gather | solution.py:212
  92.0 1.6 %maximum_add_fusion = bf16[512,128]{1,0:T(8,128)(2,1)} fusion(bf16[512,128]{1,0:T(8,128)(2,1)} %collective-permute-done.8, bf16[384,128]{1,0:T(8,128)(2,1)S(1)} %get-tuple-element.51, bf16[128,128]{1,0:T(8,128)(2,1)S(1)} %get-tuple-element.50), kind=kLoop, calls=%fused_computation.19 | loop fusion | flops 393216 | bytes 393216 | tf_op jit(solution)/shard_map/add | solution.py:189
  94.0 4.9 %collective-permute-done.9 = bf16[512,128]{1,0:T(8,128)(2,1)S(1)} collective-permute-done((bf16[512,128]{1,0:T(8,128)(2,1)}, bf16[512,128]{1,0:T(8,128)(2,1)S(1)}, u32[]{:S(2)}, u32[]{:S(2)}) %collective-permute-start.9) | collective-permute-done | bytes 131104 | tf_op jit(solution)/shard_map/ppermute | solution.py:71
  99.2 1.8 %collective-permute-start.10 = (bf16[256,128]{1,0:T(8,128)(2,1)S(1)}, bf16[256,128]{1,0:T(8,128)(2,1)S(1)}, u32[]{:S(2)}, u32[]{:S(2)}) collective-permute-start(bf16[256,128]{1,0:T(8,128)(2,1)S(1)} %select_convert_fusion), channel_id=1, source_target_pairs={{0,8},{4,12},{8,0},{12,4},{1,9},{5,13},{9,1},{13,5},{2,10},{6,14},... | collective-permute-start | bytes 196616 | tf_op jit(solution)/shard_map/ppermute | solution.py:71
  101.0 3.4 %collective-permute-done.10 = bf16[256,128]{1,0:T(8,128)(2,1)S(1)} collective-permute-done((bf16[256,128]{1,0:T(8,128)(2,1)S(1)}, bf16[256,128]{1,0:T(8,128)(2,1)S(1)}, u32[]{:S(2)}, u32[]{:S(2)}) %collective-permute-start.10) | collective-permute-done | bytes 65568 | tf_op jit(solution)/shard_map/ppermute | solution.py:71
  104.6 4.3 %collective-permute-done.11 = bf16[256,128]{1,0:T(8,128)(2,1)S(1)} collective-permute-done((bf16[256,128]{1,0:T(8,128)(2,1)S(1)}, bf16[256,128]{1,0:T(8,128)(2,1)S(1)}, u32[]{:S(2)}, u32[]{:S(2)}) %collective-permute-start.11) | collective-permute-done | bytes 65568 | tf_op jit(solution)/shard_map/ppermute | solution.py:236
  110.8 9.3 %collective-permute-done.12 = bf16[32,8192]{1,0:T(8,128)(2,1)S(1)} collective-permute-done((bf16[32,8192]{1,0:T(8,128)(2,1)S(1)}, bf16[32,8192]{1,0:T(8,128)(2,1)S(1)}, u32[]{:S(2)}, u32[]{:S(2)}) %collective-permute-start.12) | collective-permute-done | bytes 524320 | tf_op jit(solution)/shard_map/ppermute | solution.py:71
  (91 shorter events, 15.7 us)
Async XLA Ops:
  6.5 39.3 %copy-start = (bf16[16,64,512]{2,1,0:T(8,128)(2,1)S(1)}, bf16[16,64,512]{2,1,0:T(8,128)(2,1)}, u32[]{:S(2)}) copy-start(bf16[16,64,512]{2,1,0:T(8,128)(2,1)} %param.11) | copy-start | bytes 3145732
  6.5 67.7 %reduce-scatter.2.cloned.1.call-start = ((), (), s32[]{:S(2)}) async-start(), calls=%async_computation.2 | async-start | bytes 2621440 | tf_op jit(solution)/shard_map/reduce_scatter | solution.py:116
  7.4 4.5 %collective-permute-start = (s32[1,16]{1,0:T(1,128)S(1)}, s32[1,16]{1,0:T(1,128)S(1)}, u32[]{:S(2)}, u32[]{:S(2)}) collective-permute-start(s32[1,16]{1,0:T(1,128)S(1)} %pad_add_fusion.4), channel_id=1, source_target_pairs={{0,2},{2,0},{1,3},{3,1},{4,6},{6,4},{5,7},{7,5},{8,10},{10,8},{9,1... | collective-permute-start | bytes 200 | tf_op jit(solution)/shard_map/ppermute | solution.py:71
  11.8 16.8 %collective-permute-start.1 = (bf16[512,2048]{1,0:T(8,128)(2,1)}, bf16[512,2048]{1,0:T(8,128)(2,1)}, u32[]{:S(2)}, u32[]{:S(2)}) collective-permute-start(bf16[512,2048]{1,0:T(8,128)(2,1)} %refs_0_), channel_id=1, source_target_pairs={{0,1},{1,0},{2,3},{3,2},{4,5},{5,4},{6,7},{7,6},{8,9},{9,8},{10,11... | collective-permute-start | bytes 6291464 | tf_op jit(solution)/shard_map/ppermute | solution.py:71
  13.7 14.9 %collective-permute-start.2 = (bf16[128,2048]{1,0:T(8,128)(2,1)}, bf16[128,2048]{1,0:T(8,128)(2,1)}, u32[]{:S(2)}, u32[]{:S(2)}) collective-permute-start(bf16[128,2048]{1,0:T(8,128)(2,1)} %slice.36), channel_id=1, source_target_pairs={{0,2},{2,0},{1,3},{3,1},{4,6},{6,4},{5,7},{7,5},{8,10},{10,8},{9,1... | collective-permute-start | bytes 1572872 | tf_op jit(solution)/shard_map/ppermute | solution.py:71
  15.7 10.2 %copy-start.3 = (bf16[512,2048]{1,0:T(8,128)(2,1)S(1)}, bf16[512,2048]{1,0:T(8,128)(2,1)}, u32[]{:S(2)}) copy-start(bf16[512,2048]{1,0:T(8,128)(2,1)} %refs_0_) | copy-start | bytes 6291460
  15.7 11.5 %collective-permute-start.3 = (s32[2,1,16]{2,1,0:T(1,128)S(1)}, s32[2,1,16]{2,1,0:T(1,128)S(1)}, u32[]{:S(2)}, u32[]{:S(2)}) collective-permute-start(s32[2,1,16]{2,1,0:T(1,128)S(1)} %pad_add_fusion.3), channel_id=1, source_target_pairs={{0,1},{1,0},{2,3},{3,2},{4,5},{5,4},{6,7},{7,6},{8,9},{9,8},{10,11... | collective-permute-start | bytes 392 | tf_op jit(solution)/shard_map/ppermute | solution.py:71
  25.9 6.1 %copy-start.4 = (s32[64]{0:T(128)S(1)}, s32[64]{0:T(128)}, u32[]{:S(2)}) copy-start(s32[64]{0:T(128)} %param.12) | copy-start | bytes 772
  28.9 36.6 %collective-permute-start.6 = (bf16[384,2048]{1,0:T(8,128)(2,1)}, bf16[384,2048]{1,0:T(8,128)(2,1)}, u32[]{:S(2)}, u32[]{:S(2)}) collective-permute-start(bf16[384,2048]{1,0:T(8,128)(2,1)} %slice.37), channel_id=1, source_target_pairs={{0,2},{2,0},{1,3},{3,1},{4,6},{6,4},{5,7},{7,5},{8,10},{10,8},{9,1... | collective-permute-start | bytes 4718600 | tf_op jit(solution)/shard_map/ppermute | solution.py:71
  34.8 3.8 %copy-start.1 = (bf16[16,2048,128]{2,1,0:T(8,128)(2,1)S(1)}, bf16[16,2048,128]{2,1,0:T(8,128)(2,1)}, u32[]{:S(2)}) copy-start(bf16[16,2048,128]{2,1,0:T(8,128)(2,1)} %down.3) | copy-start | bytes 25165828
  41.9 5.5 %collective-permute-start.4 = (bf16[512,128]{1,0:T(8,128)(2,1)S(1)}, bf16[512,128]{1,0:T(8,128)(2,1)S(1)}, u32[]{:S(2)}, u32[]{:S(2)}) collective-permute-start(bf16[512,128]{1,0:T(8,128)(2,1)S(1)} %get-tuple-element.38), channel_id=1, source_target_pairs={{0,1},{1,0},{2,3},{3,2},{4,5},{5,4},{6,7},{7,6},{8,9},{9,8},{10,11... | collective-permute-start | bytes 393224 | tf_op jit(solution)/shard_map/ppermute | solution.py:71
  42.0 5.4 %collective-permute-start.5 = (bf16[128,2048]{1,0:T(8,128)(2,1)}, bf16[128,2048]{1,0:T(8,128)(2,1)S(1)}, u32[]{:S(2)}, u32[]{:S(2)}) collective-permute-start(bf16[128,2048]{1,0:T(8,128)(2,1)} %collective-permute-done.2.refs_0_), channel_id=1, source_target_pairs={{0,1},{1,0},{2,3},{3,2},{4,5},{5,4},{6,7},{7,6},{8,9},{9,8},{10,11... | collective-permute-start | bytes 1572872 | tf_op jit(solution)/shard_map/ppermute | solution.py:71
  74.2 5.0 %collective-permute-start.7 = (bf16[384,2048]{1,0:T(8,128)(2,1)}, bf16[384,2048]{1,0:T(8,128)(2,1)S(1)}, u32[]{:S(2)}, u32[]{:S(2)}) collective-permute-start(bf16[384,2048]{1,0:T(8,128)(2,1)} %collective-permute-done.6.refs_1_), channel_id=1, source_target_pairs={{0,1},{1,0},{2,3},{3,2},{4,5},{5,4},{6,7},{7,6},{8,9},{9,8},{10,11... | collective-permute-start | bytes 4718600 | tf_op jit(solution)/shard_map/ppermute | solution.py:71
  74.3 15.9 %all-to-all-start = ((bf16[4,3,64,512]{3,2,1,0:T(8,128)(2,1)}), bf16[4,3,64,512]{3,2,1,0:T(8,128)(2,1)}, u32[]{:S(2)}, u32[]{:S(2)}) async-start(bf16[4,3,64,512]{3,2,1,0:T(8,128)(2,1)} %bitcast.55), calls=%async_computation.1 | async-start | bytes 1572864 | tf_op jit(solution)/shard_map/all_to_all | solution.py:209
  79.3 3.4 %copy-start.2 = (bf16[16,2048,128]{2,1,0:T(8,128)(2,1)S(1)}, bf16[16,2048,128]{2,1,0:T(8,128)(2,1)}, u32[]{:S(2)}) copy-start(bf16[16,2048,128]{2,1,0:T(8,128)(2,1)} %down.3) | copy-start | bytes 25165828
  86.9 5.1 %collective-permute-start.8 = (bf16[512,128]{1,0:T(8,128)(2,1)}, bf16[512,128]{1,0:T(8,128)(2,1)}, u32[]{:S(2)}, u32[]{:S(2)}) collective-permute-start(bf16[512,128]{1,0:T(8,128)(2,1)} %pad_maximum_fusion), channel_id=1, source_target_pairs={{0,1},{1,0},{2,3},{3,2},{4,5},{5,4},{6,7},{7,6},{8,9},{9,8},{10,11... | collective-permute-start | bytes 393224 | tf_op jit(solution)/shard_map/ppermute | solution.py:71
  93.6 5.3 %collective-permute-start.9 = (bf16[512,128]{1,0:T(8,128)(2,1)}, bf16[512,128]{1,0:T(8,128)(2,1)S(1)}, u32[]{:S(2)}, u32[]{:S(2)}) collective-permute-start(bf16[512,128]{1,0:T(8,128)(2,1)} %maximum_add_fusion), channel_id=1, source_target_pairs={{0,2},{2,0},{1,3},{3,1},{4,6},{6,4},{5,7},{7,5},{8,10},{10,8},{9,1... | collective-permute-start | bytes 393224 | tf_op jit(solution)/shard_map/ppermute | solution.py:71
  94.0 15.0 %copy-start.5 = (bf16[512,512]{1,0:T(8,128)(2,1)S(1)}, bf16[512,512]{1,0:T(8,128)(2,1)}, u32[]{:S(2)}) copy-start(bf16[512,512]{1,0:T(8,128)(2,1)} %reduce-scatter.2.cloned.1.call-done) | copy-start | bytes 1572868
  99.2 5.2 %collective-permute-start.10 = (bf16[256,128]{1,0:T(8,128)(2,1)S(1)}, bf16[256,128]{1,0:T(8,128)(2,1)S(1)}, u32[]{:S(2)}, u32[]{:S(2)}) collective-permute-start(bf16[256,128]{1,0:T(8,128)(2,1)S(1)} %select_convert_fusion), channel_id=1, source_target_pairs={{0,8},{4,12},{8,0},{12,4},{1,9},{5,13},{9,1},{13,5},{2,10},{6,14},... | collective-permute-start | bytes 196616 | tf_op jit(solution)/shard_map/ppermute | solution.py:71
  104.6 4.3 %collective-permute-start.11 = (bf16[256,128]{1,0:T(8,128)(2,1)S(1)}, bf16[256,128]{1,0:T(8,128)(2,1)S(1)}, u32[]{:S(2)}, u32[]{:S(2)}) collective-permute-start(bf16[256,128]{1,0:T(8,128)(2,1)S(1)} %get-tuple-element.57), channel_id=1, source_target_pairs={{0,4},{4,0},{8,12},{12,8},{1,5},{5,1},{9,13},{13,9},{2,6},{6,2},{1... | collective-permute-start | bytes 196616 | tf_op jit(solution)/shard_map/ppermute | solution.py:236
  109.0 1.4 %copy-start.6 = (s32[4,32]{1,0:T(4,128)S(1)}, s32[4,32]{1,0:T(4,128)}, u32[]{:S(2)}) copy-start(s32[4,32]{1,0:T(4,128)} %param.15) | copy-start | bytes 1540
  109.8 10.3 %collective-permute-start.12 = (bf16[32,8192]{1,0:T(8,128)(2,1)S(1)}, bf16[32,8192]{1,0:T(8,128)(2,1)S(1)}, u32[]{:S(2)}, u32[]{:S(2)}) collective-permute-start(bf16[32,8192]{1,0:T(8,128)(2,1)S(1)} %bitcast.57), channel_id=1, source_target_pairs={{0,2},{2,0},{1,3},{3,1},{4,6},{6,4},{5,7},{7,5},{8,10},{10,8},{9,1... | collective-permute-start | bytes 1572872 | tf_op jit(solution)/shard_map/ppermute | solution.py:71
Sparse Core Ops, SparseCore 0:
  28.8 45.3 reduce-scatter.1

commit v6 on v5

--- a/solution.py
+++ b/solution.py
@@ -113,7 +113,13 @@
     near_rows, first_piece, after_base, asked_turns, rest = lax.optimization_barrier(
         (near_rows, first_piece, base_part, asked_turns, tokens[first_count:])
     )
-    base_sum = lax.psum_scatter(after_base, "tp", scatter_dimension=1, tiled=True)
+    early_count = token_rows - first_count
+    base_sum = lax.psum_scatter(
+        after_base[:early_count], "tp", scatter_dimension=1, tiled=True
+    )
+    late_sum = lax.psum_scatter(
+        after_base[early_count:], "tp", scatter_dimension=1, tiled=True
+    )
     second_piece = [shifted(rest, "pd", step) for step in far_steps]
     first_rows = [
         [rows] + [shifted(rows, "st", turn) for turn in range(1, st_count)] for rows in first_piece
@@ -215,7 +221,10 @@
         axis=0,
         mode="clip",
     )
-    far_sums, page_up_weight = lax.optimization_barrier((far_sums, page_up_weight))
+    far_sums, page_up_weight, late_sum = lax.optimization_barrier(
+        (far_sums, page_up_weight, late_sum)
+    )
+    base_sum = jnp.concatenate([base_sum, late_sum], axis=0)
     for step in far_steps:
         inner = inner + shifted(far_sums[step - 1], "pd", -step)
 

time: 129 us -> 126 us (0.977)
  waiting for transfers between devices: 53.9 us -> 49.4 us
  local copies, waits for them, and re-layouts: 22.5 us -> 26.7 us
  Pallas kernels: 6.98 us -> 5.04 us
  matrix products: 11 us -> 9.6 us
  starting transfers between devices: 14.9 us -> 16.3 us
    reduce_scatter x1 -> x2, waiting for transfers between devices: 8.72 us -> 3.59 us  [the longest x1 3.12 us: on_device(): lax.psum_scatter(after_base[early_count:], 'tp', scatter_dimension=1, til...]
    slice x0 -> x2, local copies, waits for them, and re-layouts: none -> 3.13 us  [the longest x1 1.88 us: on_device(): after_base[early_count:]]
    unnamed x16 -> x24, local copies, waits for them, and re-layouts: 8.43 us -> 11.3 us
    pallas_call x2, Pallas kernels: 6.98 us -> 5.04 us  [down_products(): pl.pallas_call(functools.partial(down_kernel, sources, requests), out_sha...]
    dot_general x1, matrix products: 9.95 us -> 8.51 us  [on_device(): jnp.dot(tokens, key_value_matrix, preferred_element_type=jnp.float32)]
    ppermute x12, starting transfers between devices: 10.7 us -> 12 us  [shifted(): lax.ppermute(value, axis, [(i, (i + step) % size) for i in range(size)])]
  transfers between devices with their start and end apart: 15 -> 16, of which waited for: 9 -> 10; matrix products, arithmetic and copies ran while one was open for 21% -> 21% of each run, Pallas kernels for 5% -> 4%
where the time goes in v6:
time: 126 us; the launch traced here: 125 us
  waiting for transfers between devices  49.4 us (39%)
  local copies, waits for them, and re-layouts  26.7 us (21%)
  starting transfers between devices  16.3 us (13%)
  between operations  13.8 us (11%)
  matrix products  9.6 us (8%)
  Pallas kernels  5.04 us (4%)
  other arithmetic  4.43 us (4%)
    ppermute x12, waiting for transfers between devices, shifted(): lax.ppermute(value, axis, [(i, (i + step) % size) for i in range(size)])  38.3 us
    ppermute x12, starting transfers between devices, shifted(): lax.ppermute(value, axis, [(i, (i + step) % size) for i in range(size)])  12 us
    unnamed x24, local copies, waits for them, and re-layouts  11.3 us
    dot_general x1, matrix products, on_device(): jnp.dot(tokens, key_value_matrix, preferred_element_type=jnp.float32)  8.51 us
    pallas_call x2, Pallas kernels, down_products(): pl.pallas_call(functools.partial(down_kernel, sources, requests), out_sha...  5.04 us
    all_to_all x1, starting transfers between devices, on_device(): lax.all_to_all(up_page_list, ('pd', 'st'), split_axis=0, concat_axis=0, t...  4.2 us
    ppermute x1, waiting for transfers between devices, on_device(): mine = mine + lax.ppermute(mine.astype(jnp.bfloat16), 'tp', pairs)  4.19 us
    gather x6, local copies, waits for them, and re-layouts, request_tables(): jnp.take(table, source_group, axis=0, mode='clip')  3.36 us
  transfers between devices with their start and end apart: 16, of which 10 were waited for; matrix products, arithmetic and copies ran while one was open for 21% of the time, Pallas kernels for 4%

profile of v6, /device:TPU:0, one launch (start us, length us, event | category | flops | bytes accessed | tf_op | source)
XLA Modules:
  0.0 125.3 jit_solution(5460343062740472062)
XLA Ops:
  7.4 2.9 %collective-permute-start = (s32[1,16]{1,0:T(1,128)S(1)}, s32[1,16]{1,0:T(1,128)S(1)}, u32[]{:S(2)}, u32[]{:S(2)}) collective-permute-start(s32[1,16]{1,0:T(1,128)S(1)} %pad_add_fusion.4), channel_id=1, source_target_pairs={{0,2},{2,0},{1,3},{3,1},{4,6},{6,4},{5,7},{7,5},{8,10},{10,8},{9,1... | collective-permute-start | bytes 200 | tf_op jit(solution)/shard_map/ppermute | solution.py:71
  10.3 1.5 %collective-permute-done = s32[1,16]{1,0:T(1,128)S(1)} collective-permute-done((s32[1,16]{1,0:T(1,128)S(1)}, s32[1,16]{1,0:T(1,128)S(1)}, u32[]{:S(2)}, u32[]{:S(2)}) %collective-permute-start) | collective-permute-done | bytes 96 | tf_op jit(solution)/shard_map/ppermute | solution.py:71
  13.5 2.0 %collective-permute-start.2 = (bf16[128,2048]{1,0:T(8,128)(2,1)S(1)}, bf16[128,2048]{1,0:T(8,128)(2,1)}, u32[]{:S(2)}, u32[]{:S(2)}) collective-permute-start(bf16[128,2048]{1,0:T(8,128)(2,1)S(1)} %slice.42), channel_id=1, source_target_pairs={{0,2},{2,0},{1,3},{3,1},{4,6},{6,4},{5,7},{7,5},{8,10},{10,8},{9,1... | collective-permute-start | bytes 1572872 | tf_op jit(solution)/shard_map/ppermute | solution.py:71
  15.5 8.5 %convolution_convert_fusion = bf16[512,2048]{1,0:T(8,128)(2,1)S(1)} fusion(bf16[512,2048]{1,0:T(8,128)(2,1)} %refs_0_, bf16[2048,2048]{1,0:T(8,128)(2,1)} %param.9), kind=kOutput, calls=%fused_computation.14 | convolution fusion | flops 4296015872 | bytes 12582912 | tf_op jit(solution)/shard_map/dot_general | solution.py:110
  25.5 2.3 %collective-permute-done.2.refs_0_ = bf16[128,2048]{1,0:T(8,128)(2,1)} collective-permute-done((bf16[128,2048]{1,0:T(8,128)(2,1)S(1)}, bf16[128,2048]{1,0:T(8,128)(2,1)}, u32[]{:S(2)}, u32[]{:S(2)}) %collective-permute-start.2) | collective-permute-done | bytes 524320 | tf_op jit(solution)/shard_map/ppermute | solution.py:71
  30.6 1.8 %collective-permute-start.6 = (bf16[384,2048]{1,0:T(8,128)(2,1)}, bf16[384,2048]{1,0:T(8,128)(2,1)}, u32[]{:S(2)}, u32[]{:S(2)}) collective-permute-start(bf16[384,2048]{1,0:T(8,128)(2,1)} %slice.43), channel_id=1, source_target_pairs={{0,2},{2,0},{1,3},{3,1},{4,6},{6,4},{5,7},{7,5},{8,10},{10,8},{9,1... | collective-permute-start | bytes 4718600 | tf_op jit(solution)/shard_map/ppermute | solution.py:71
  36.5 3.7 %copy-done.1 = bf16[16,2048,128]{2,1,0:T(8,128)(2,1)S(1)} copy-done((bf16[16,2048,128]{2,1,0:T(8,128)(2,1)S(1)}, bf16[16,2048,128]{2,1,0:T(8,128)(2,1)}, u32[]{:S(2)}) %copy-start.1) | copy-done | bytes 8388632
  40.2 1.6 %copy-done.5 = bf16[512,2048]{1,0:T(8,128)(2,1)S(1)} copy-done((bf16[512,2048]{1,0:T(8,128)(2,1)S(1)}, bf16[512,2048]{1,0:T(8,128)(2,1)}, u32[]{:S(2)}) %copy-start.5) | copy-done | bytes 2097176
  41.8 1.7 %down_products.2 = (bf16[512,128]{1,0:T(8,128)(2,1)S(1)}, bf16[512,128]{1,0:T(8,128)(2,1)S(1)}) custom-call(s32[2,8]{1,0:T(2,128)S(1)} %gather_fusion.3, s32[2,8]{1,0:T(2,128)S(1)} %get-tuple-element.81.starts, s32[2,8]{1,0:T(2,128)S(1)} %get-tuple-element.80.counts, bf16[16,2048,128]{2,1,0:T(8,128)(2,1)S(1)} %copy-done.1, bf16[512,2048]{1,0:T(8,128)(2,1)S(1)} %copy-done.3, ...), custom_call_target="tpu_custom_call" | custom-call | flops 536870912 | bytes 12845056 | tf_op jit(solution)/shard_map/down_products/pallas_call | solution.py:52
  47.9 19.0 %collective-permute-done.6.refs_1_ = bf16[384,2048]{1,0:T(8,128)(2,1)} collective-permute-done((bf16[384,2048]{1,0:T(8,128)(2,1)}, bf16[384,2048]{1,0:T(8,128)(2,1)}, u32[]{:S(2)}, u32[]{:S(2)}) %collective-permute-start.6) | collective-permute-done | bytes 1572896 | tf_op jit(solution)/shard_map/ppermute | solution.py:71
  67.3 1.9 %slice.47 = bf16[128,2048]{1,0:T(8,128)(2,1)} slice(bf16[512,2048]{1,0:T(8,128)(2,1)} %copy-done.7), slice={[384:512], [0:2048]} | slice | bytes 1048576 | tf_op jit(solution)/shard_map/slice | solution.py:121
  69.4 4.2 %all-to-all-start = ((bf16[4,3,64,512]{3,2,1,0:T(8,128)(2,1)}), bf16[4,3,64,512]{3,2,1,0:T(8,128)(2,1)}, u32[]{:S(2)}, u32[]{:S(2)}) async-start(bf16[4,3,64,512]{3,2,1,0:T(8,128)(2,1)} %bitcast.55), calls=%async_computation.1 | async-start | bytes 1572864 | tf_op jit(solution)/shard_map/all_to_all | solution.py:215
  73.7 3.5 %copy-done.2 = bf16[16,2048,128]{2,1,0:T(8,128)(2,1)S(1)} copy-done((bf16[16,2048,128]{2,1,0:T(8,128)(2,1)S(1)}, bf16[16,2048,128]{2,1,0:T(8,128)(2,1)}, u32[]{:S(2)}) %copy-start.2) | copy-done | bytes 8388632
  77.1 3.3 %down_products.3 = (bf16[128,128]{1,0:T(8,128)(2,1)S(1)}, bf16[384,128]{1,0:T(8,128)(2,1)S(1)}, bf16[128,128]{1,0:T(8,128)(2,1)S(1)}, bf16[384,128]{1,0:T(8,128)(2,1)S(1)}) custom-call(s32[4,8]{1,0:T(4,128)S(1)} %bitcast.54, s32[4,8]{1,0:T(4,128)S(1)} %bitcast.53, s32[4,8]{1,0:T(4,128)S(1)} %bitcast.52, bf16[16,2048,128]{2,1,0:T(8,128)(2,1)S(1)} %copy-done.2, ...), custom_call_target="tpu_custom_call" | custom-call | flops 536870912 | bytes 12845056 | tf_op jit(solution)/shard_map/down_products/pallas_call | solution.py:52
  82.0 3.3 %all-to-all-done = bf16[4,3,64,512]{3,2,1,0:T(8,128)(2,1)} async-done(((bf16[4,3,64,512]{3,2,1,0:T(8,128)(2,1)}), bf16[4,3,64,512]{3,2,1,0:T(8,128)(2,1)}, u32[]{:S(2)}, u32[]{:S(2)}) %all-to-all-start) | async-done | bytes 786464 | tf_op jit(solution)/shard_map/all_to_all | solution.py:215
  85.3 1.8 %gather_fusion.11 = bf16[32,64,512]{2,1,0:T(8,128)(2,1)S(1)} fusion(bf16[12,64,512]{2,1,0:T(8,128)(2,1)} %bitcast.23, s32[1024]{0:T(1024)S(1)} %pad_clamp_fusion), kind=kCustom, calls=%fused_computation.11 | custom fusion | bytes 4194432 | tf_op jit(solution)/shard_map/jit(_take)/gather | solution.py:218
  87.1 1.6 %maximum_add_fusion = bf16[512,128]{1,0:T(8,128)(2,1)} fusion(bf16[512,128]{1,0:T(8,128)(2,1)} %collective-permute-done.8, bf16[384,128]{1,0:T(8,128)(2,1)S(1)} %get-tuple-element.51, bf16[128,128]{1,0:T(8,128)(2,1)S(1)} %get-tuple-element.50), kind=kLoop, calls=%fused_computation.20 | loop fusion | flops 393216 | bytes 393216 | tf_op jit(solution)/shard_map/add | solution.py:195
  88.7 3.1 %reduce-scatter.5.cloned.1.call-done = bf16[128,512]{1,0:T(8,128)(2,1)} async-done(((bf16[128,2048]{1,0:T(8,128)(2,1)}), bf16[128,512]{1,0:T(8,128)(2,1)}) %reduce-scatter.5.cloned.1.call-update) | async-done | bytes 131088 | tf_op jit(solution)/shard_map/reduce_scatter | solution.py:120
  91.8 1.5 %collective-permute-start.9 = (bf16[512,128]{1,0:T(8,128)(2,1)}, bf16[512,128]{1,0:T(8,128)(2,1)S(1)}, u32[]{:S(2)}, u32[]{:S(2)}) collective-permute-start(bf16[512,128]{1,0:T(8,128)(2,1)} %maximum_add_fusion), channel_id=1, source_target_pairs={{0,2},{2,0},{1,3},{3,1},{4,6},{6,4},{5,7},{7,5},{8,10},{10,8},{9,1... | collective-permute-start | bytes 393224 | tf_op jit(solution)/shard_map/ppermute | solution.py:71
  93.4 3.6 %collective-permute-done.9 = bf16[512,128]{1,0:T(8,128)(2,1)S(1)} collective-permute-done((bf16[512,128]{1,0:T(8,128)(2,1)}, bf16[512,128]{1,0:T(8,128)(2,1)S(1)}, u32[]{:S(2)}, u32[]{:S(2)}) %collective-permute-start.9) | collective-permute-done | bytes 131104 | tf_op jit(solution)/shard_map/ppermute | solution.py:71
  98.1 4.5 %collective-permute-done.10 = bf16[256,128]{1,0:T(8,128)(2,1)S(1)} collective-permute-done((bf16[256,128]{1,0:T(8,128)(2,1)S(1)}, bf16[256,128]{1,0:T(8,128)(2,1)S(1)}, u32[]{:S(2)}, u32[]{:S(2)}) %collective-permute-start.10) | collective-permute-done | bytes 65568 | tf_op jit(solution)/shard_map/ppermute | solution.py:71
  102.9 4.2 %collective-permute-done.11 = bf16[256,128]{1,0:T(8,128)(2,1)S(1)} collective-permute-done((bf16[256,128]{1,0:T(8,128)(2,1)S(1)}, bf16[256,128]{1,0:T(8,128)(2,1)S(1)}, u32[]{:S(2)}, u32[]{:S(2)}) %collective-permute-start.11) | collective-permute-done | bytes 65568 | tf_op jit(solution)/shard_map/ppermute | solution.py:245
  107.9 1.6 %collective-permute-start.12 = (bf16[32,8192]{1,0:T(8,128)(2,1)S(1)}, bf16[32,8192]{1,0:T(8,128)(2,1)S(1)}, u32[]{:S(2)}, u32[]{:S(2)}) collective-permute-start(bf16[32,8192]{1,0:T(8,128)(2,1)S(1)} %bitcast.58), channel_id=1, source_target_pairs={{0,2},{2,0},{1,3},{3,1},{4,6},{6,4},{5,7},{7,5},{8,10},{10,8},{9,1... | collective-permute-start | bytes 1572872 | tf_op jit(solution)/shard_map/ppermute | solution.py:71
  109.8 7.3 %collective-permute-done.12 = bf16[32,8192]{1,0:T(8,128)(2,1)S(1)} collective-permute-done((bf16[32,8192]{1,0:T(8,128)(2,1)S(1)}, bf16[32,8192]{1,0:T(8,128)(2,1)S(1)}, u32[]{:S(2)}, u32[]{:S(2)}) %collective-permute-start.12) | collective-permute-done | bytes 524320 | tf_op jit(solution)/shard_map/ppermute | solution.py:71
  (105 shorter events, 21.0 us)
Async XLA Ops:
  6.5 39.8 %copy-start = (bf16[16,64,512]{2,1,0:T(8,128)(2,1)S(1)}, bf16[16,64,512]{2,1,0:T(8,128)(2,1)}, u32[]{:S(2)}) copy-start(bf16[16,64,512]{2,1,0:T(8,128)(2,1)} %param.11) | copy-start | bytes 3145732
  6.5 60.8 %reduce-scatter.3.cloned.1.call-start = ((), (), s32[]{:S(2)}) async-start(), calls=%async_computation.3 | async-start | bytes 1966080 | tf_op jit(solution)/shard_map/reduce_scatter | solution.py:117
  7.4 4.5 %collective-permute-start = (s32[1,16]{1,0:T(1,128)S(1)}, s32[1,16]{1,0:T(1,128)S(1)}, u32[]{:S(2)}, u32[]{:S(2)}) collective-permute-start(s32[1,16]{1,0:T(1,128)S(1)} %pad_add_fusion.4), channel_id=1, source_target_pairs={{0,2},{2,0},{1,3},{3,1},{4,6},{6,4},{5,7},{7,5},{8,10},{10,8},{9,1... | collective-permute-start | bytes 200 | tf_op jit(solution)/shard_map/ppermute | solution.py:71
  11.8 16.0 %collective-permute-start.1 = (bf16[512,2048]{1,0:T(8,128)(2,1)}, bf16[512,2048]{1,0:T(8,128)(2,1)S(1)}, u32[]{:S(2)}, u32[]{:S(2)}) collective-permute-start(bf16[512,2048]{1,0:T(8,128)(2,1)} %refs_0_), channel_id=1, source_target_pairs={{0,1},{1,0},{2,3},{3,2},{4,5},{5,4},{6,7},{7,6},{8,9},{9,8},{10,11... | collective-permute-start | bytes 6291464 | tf_op jit(solution)/shard_map/ppermute | solution.py:71
  12.9 11.1 %copy-start.3 = (bf16[512,2048]{1,0:T(8,128)(2,1)S(1)}, bf16[512,2048]{1,0:T(8,128)(2,1)}, u32[]{:S(2)}) copy-start(bf16[512,2048]{1,0:T(8,128)(2,1)} %refs_0_) | copy-start | bytes 6291460
  12.9 12.5 %collective-permute-start.3 = (s32[2,1,16]{2,1,0:T(1,128)S(1)}, s32[2,1,16]{2,1,0:T(1,128)S(1)}, u32[]{:S(2)}, u32[]{:S(2)}) collective-permute-start(s32[2,1,16]{2,1,0:T(1,128)S(1)} %pad_add_fusion.3), channel_id=1, source_target_pairs={{0,1},{1,0},{2,3},{3,2},{4,5},{5,4},{6,7},{7,6},{8,9},{9,8},{10,11... | collective-permute-start | bytes 392 | tf_op jit(solution)/shard_map/ppermute | solution.py:71
  13.5 14.3 %collective-permute-start.2 = (bf16[128,2048]{1,0:T(8,128)(2,1)S(1)}, bf16[128,2048]{1,0:T(8,128)(2,1)}, u32[]{:S(2)}, u32[]{:S(2)}) collective-permute-start(bf16[128,2048]{1,0:T(8,128)(2,1)S(1)} %slice.42), channel_id=1, source_target_pairs={{0,2},{2,0},{1,3},{3,1},{4,6},{6,4},{5,7},{7,5},{8,10},{10,8},{9,1... | collective-permute-start | bytes 1572872 | tf_op jit(solution)/shard_map/ppermute | solution.py:71
  24.1 3.8 %copy-start.7 = (bf16[512,2048]{1,0:T(8,128)(2,1)}, bf16[512,2048]{1,0:T(8,128)(2,1)S(1)}, u32[]{:S(2)}) copy-start(bf16[512,2048]{1,0:T(8,128)(2,1)S(1)} %convolution_convert_fusion) | copy-start | bytes 6291460
  25.5 9.1 %copy-start.6 = (s32[64]{0:T(128)S(1)}, s32[64]{0:T(128)}, u32[]{:S(2)}) copy-start(s32[64]{0:T(128)} %param.12) | copy-start | bytes 772
  30.4 61.4 %reduce-scatter.5.cloned.1.call-start = ((), (), s32[]{:S(2)}) async-start(), calls=%async_computation.4 | async-start | bytes 655360 | tf_op jit(solution)/shard_map/reduce_scatter | solution.py:120
  30.6 36.2 %collective-permute-start.6 = (bf16[384,2048]{1,0:T(8,128)(2,1)}, bf16[384,2048]{1,0:T(8,128)(2,1)}, u32[]{:S(2)}, u32[]{:S(2)}) collective-permute-start(bf16[384,2048]{1,0:T(8,128)(2,1)} %slice.43), channel_id=1, source_target_pairs={{0,2},{2,0},{1,3},{3,1},{4,6},{6,4},{5,7},{7,5},{8,10},{10,8},{9,1... | collective-permute-start | bytes 4718600 | tf_op jit(solution)/shard_map/ppermute | solution.py:71
  36.5 3.7 %copy-start.1 = (bf16[16,2048,128]{2,1,0:T(8,128)(2,1)S(1)}, bf16[16,2048,128]{2,1,0:T(8,128)(2,1)}, u32[]{:S(2)}) copy-start(bf16[16,2048,128]{2,1,0:T(8,128)(2,1)} %down.3) | copy-start | bytes 25165828
  43.5 4.3 %collective-permute-start.4 = (bf16[512,128]{1,0:T(8,128)(2,1)S(1)}, bf16[512,128]{1,0:T(8,128)(2,1)S(1)}, u32[]{:S(2)}, u32[]{:S(2)}) collective-permute-start(bf16[512,128]{1,0:T(8,128)(2,1)S(1)} %get-tuple-element.39), channel_id=1, source_target_pairs={{0,1},{1,0},{2,3},{3,2},{4,5},{5,4},{6,7},{7,6},{8,9},{9,8},{10,11... | collective-permute-start | bytes 393224 | tf_op jit(solution)/shard_map/ppermute | solution.py:71
  43.6 4.3 %collective-permute-start.5 = (bf16[128,2048]{1,0:T(8,128)(2,1)}, bf16[128,2048]{1,0:T(8,128)(2,1)S(1)}, u32[]{:S(2)}, u32[]{:S(2)}) collective-permute-start(bf16[128,2048]{1,0:T(8,128)(2,1)} %collective-permute-done.2.refs_0_), channel_id=1, source_target_pairs={{0,1},{1,0},{2,3},{3,2},{4,5},{5,4},{6,7},{7,6},{8,9},{9,8},{10,11... | collective-permute-start | bytes 1572872 | tf_op jit(solution)/shard_map/ppermute | solution.py:71
  67.3 6.3 %collective-permute-start.7 = (bf16[384,2048]{1,0:T(8,128)(2,1)}, bf16[384,2048]{1,0:T(8,128)(2,1)S(1)}, u32[]{:S(2)}, u32[]{:S(2)}) collective-permute-start(bf16[384,2048]{1,0:T(8,128)(2,1)} %collective-permute-done.6.refs_1_), channel_id=1, source_target_pairs={{0,1},{1,0},{2,3},{3,2},{4,5},{5,4},{6,7},{7,6},{8,9},{9,8},{10,11... | collective-permute-start | bytes 4718600 | tf_op jit(solution)/shard_map/ppermute | solution.py:71
  69.4 15.9 %all-to-all-start = ((bf16[4,3,64,512]{3,2,1,0:T(8,128)(2,1)}), bf16[4,3,64,512]{3,2,1,0:T(8,128)(2,1)}, u32[]{:S(2)}, u32[]{:S(2)}) async-start(bf16[4,3,64,512]{3,2,1,0:T(8,128)(2,1)} %bitcast.55), calls=%async_computation.1 | async-start | bytes 1572864 | tf_op jit(solution)/shard_map/all_to_all | solution.py:215
  73.7 3.5 %copy-start.2 = (bf16[16,2048,128]{2,1,0:T(8,128)(2,1)S(1)}, bf16[16,2048,128]{2,1,0:T(8,128)(2,1)}, u32[]{:S(2)}) copy-start(bf16[16,2048,128]{2,1,0:T(8,128)(2,1)} %down.3) | copy-start | bytes 25165828
  81.1 6.0 %collective-permute-start.8 = (bf16[512,128]{1,0:T(8,128)(2,1)}, bf16[512,128]{1,0:T(8,128)(2,1)}, u32[]{:S(2)}, u32[]{:S(2)}) collective-permute-start(bf16[512,128]{1,0:T(8,128)(2,1)} %pad_maximum_fusion.1), channel_id=1, source_target_pairs={{0,1},{1,0},{2,3},{3,2},{4,5},{5,4},{6,7},{7,6},{8,9},{9,8},{10,11... | collective-permute-start | bytes 393224 | tf_op jit(solution)/shard_map/ppermute | solution.py:71
  91.8 5.2 %collective-permute-start.9 = (bf16[512,128]{1,0:T(8,128)(2,1)}, bf16[512,128]{1,0:T(8,128)(2,1)S(1)}, u32[]{:S(2)}, u32[]{:S(2)}) collective-permute-start(bf16[512,128]{1,0:T(8,128)(2,1)} %maximum_add_fusion), channel_id=1, source_target_pairs={{0,2},{2,0},{1,3},{3,1},{4,6},{6,4},{5,7},{7,5},{8,10},{10,8},{9,1... | collective-permute-start | bytes 393224 | tf_op jit(solution)/shard_map/ppermute | solution.py:71
  93.4 9.4 %copy-start.8 = (bf16[384,512]{1,0:T(8,128)(2,1)S(1)}, bf16[384,512]{1,0:T(8,128)(2,1)}, u32[]{:S(2)}) copy-start(bf16[384,512]{1,0:T(8,128)(2,1)} %reduce-scatter.3.cloned.1.call-done) | copy-start | bytes 1179652
  93.4 9.4 %copy-start.9 = (bf16[128,512]{1,0:T(8,128)(2,1)S(1)}, bf16[128,512]{1,0:T(8,128)(2,1)}, u32[]{:S(2)}) copy-start(bf16[128,512]{1,0:T(8,128)(2,1)} %reduce-scatter.5.cloned.1.call-done) | copy-start | bytes 393220
  97.3 5.3 %collective-permute-start.10 = (bf16[256,128]{1,0:T(8,128)(2,1)S(1)}, bf16[256,128]{1,0:T(8,128)(2,1)S(1)}, u32[]{:S(2)}, u32[]{:S(2)}) collective-permute-start(bf16[256,128]{1,0:T(8,128)(2,1)S(1)} %select_convert_fusion), channel_id=1, source_target_pairs={{0,8},{4,12},{8,0},{12,4},{1,9},{5,13},{9,1},{13,5},{2,10},{6,14},... | collective-permute-start | bytes 196616 | tf_op jit(solution)/shard_map/ppermute | solution.py:71
  102.7 4.3 %collective-permute-start.11 = (bf16[256,128]{1,0:T(8,128)(2,1)S(1)}, bf16[256,128]{1,0:T(8,128)(2,1)S(1)}, u32[]{:S(2)}, u32[]{:S(2)}) collective-permute-start(bf16[256,128]{1,0:T(8,128)(2,1)S(1)} %get-tuple-element.59), channel_id=1, source_target_pairs={{0,4},{4,0},{8,12},{12,8},{1,5},{5,1},{9,13},{13,9},{2,6},{6,2},{1... | collective-permute-start | bytes 196616 | tf_op jit(solution)/shard_map/ppermute | solution.py:245
  107.9 9.2 %collective-permute-start.12 = (bf16[32,8192]{1,0:T(8,128)(2,1)S(1)}, bf16[32,8192]{1,0:T(8,128)(2,1)S(1)}, u32[]{:S(2)}, u32[]{:S(2)}) collective-permute-start(bf16[32,8192]{1,0:T(8,128)(2,1)S(1)} %bitcast.58), channel_id=1, source_target_pairs={{0,2},{2,0},{1,3},{3,1},{4,6},{6,4},{5,7},{7,5},{8,10},{10,8},{9,1... | collective-permute-start | bytes 1572872 | tf_op jit(solution)/shard_map/ppermute | solution.py:71
  (3 other events, 5.2 us)
Sparse Core Ops, SparseCore 0:
  30.5 36.7 reduce-scatter.2
  69.6 22.1 reduce-scatter.4
